TPU v7x, 32 devices: a whole 2x2x4 slice. The times are simulated.
32 devices in a mesh: tile: 8 (over z, y), acq: 4 (over x, core).
Axes of the slice: x: 2, y: 2, z: 4, core: 2. Of those that a mesh axis runs over, the one named last changes fastest.
Arguments:
- strips: float32 [192, 512, 1024], P('acq', 'tile'), may hold values from -6 to 6
- strip_quality: float32 [192], P('acq'), may hold values from 0.3 to 3
- valid_ranges: int32 [192, 4], P('acq'), may hold values from 0 to 1024, as said below
Outputs:
- mean_elev: float32 [512, 1024], P('tile', 'acq')
- covariance: float32 [10, 512, 1024], P(None, 'tile', 'acq')
Inputs may be any that keep to these rules, and one draw needn't show every extreme that they name: `valid_ranges`: row and column ranges of each strip are non-empty, start in the lower half of the grid and hold at least half of its rows or columns; some strip starts at row and column 0 and ends at the last row and column.
All inputs are finite; a program needn't handle non-finite values.
Results may differ from a plain program's by a relative error of at most 0.0003.
Values sent between devices are 32-bit elements; how exact they have to be, the bound alone decides.
No kernel may reach another device: no remote copies, remote signals or barrier semaphores. Data moves between devices by JAX's collectives and lax.ppermute only.
A program may use at most 192 MiB of HBM per device.

v0:
```python
import jax
import jax.numpy as jnp
from jax import lax
from jax.sharding import PartitionSpec as P


def padded_2(block, sides, width):
    for axis, dim in sides:
        count = lax.axis_size(axis)
        forward = [(i, i + 1) for i in range(count - 1)]
        backward = [(target, source) for source, target in forward]
        low = lax.ppermute(
            lax.slice_in_dim(block, block.shape[dim] - width, None, axis=dim), axis, forward
        )
        high = lax.ppermute(lax.slice_in_dim(block, 0, width, axis=dim), axis, backward)
        block = jnp.concatenate([low, block, high], axis=dim)
    return block


def stencils(padded, lat_cosine):
    row_count = padded.shape[-2] - 4
    col_count = padded.shape[-1]

    def rows_at(offset):
        return padded[..., offset : offset + row_count, :]

    elevation = rows_at(2)
    slope_y = (rows_at(0) - 8.0 * rows_at(1) + 8.0 * rows_at(3) - rows_at(4)) / 12.0
    second_y = (
        -rows_at(0) + 16.0 * rows_at(1) - 30.0 * elevation + 16.0 * rows_at(3) - rows_at(4)
    ) / 12.0
    widths = [(0, 0)] * (elevation.ndim - 1) + [(2, 2)]
    widened = jnp.pad(elevation, widths)

    def cols_at(offset):
        return widened[..., offset : offset + col_count]

    slope_x = (cols_at(0) - 8.0 * cols_at(1) + 8.0 * cols_at(3) - cols_at(4)) / (12.0 * lat_cosine)
    second_x = (
        -cols_at(0) + 16.0 * cols_at(1) - 30.0 * elevation + 16.0 * cols_at(3) - cols_at(4)
    ) / (12.0 * lat_cosine * lat_cosine)
    return (elevation, slope_x, slope_y, second_x + second_y)


def moment_terms(moment_grids, merge_weight):
    moment_addend_list = [merge_weight]
    for first_derivative in range(4):
        moment_addend_list.append(merge_weight * moment_grids[first_derivative])
    for first_derivative in range(4):
        for second_derivative in range(first_derivative, 4):
            moment_addend_list.append(
                merge_weight * moment_grids[first_derivative] * moment_grids[second_derivative]
            )
    return moment_addend_list


def finalize(moments):
    denominator = jnp.maximum(moments[0], 1.0)
    weighted_means = [moments[1 + first_derivative] / denominator for first_derivative in range(4)]
    entries = []
    position = 5
    for first_derivative in range(4):
        for second_derivative in range(first_derivative, 4):
            entries.append(
                moments[position] / denominator
                - weighted_means[first_derivative] * weighted_means[second_derivative]
            )
            position += 1
    return (weighted_means[0], jnp.stack(entries))


def local(strips, strip_quality, valid_ranges):
    row_block = strips.shape[1]
    col_count = strips.shape[2]
    total_rows = row_block * lax.axis_size("tile")
    row_index = lax.axis_index("tile") * row_block + jnp.arange(row_block, dtype=jnp.int32)
    latitude_degrees = -1.0 + 2.0 * (row_index.astype(jnp.float32) + 0.5) / total_rows
    lat_cosine = jnp.cos(latitude_degrees)[:, None]
    col_index = jnp.arange(col_count, dtype=jnp.int32)
    padded = padded_2(strips, (("tile", 1),), 2)
    moment_grids = stencils(padded, lat_cosine)
    row_inside = (row_index[None, :] >= valid_ranges[:, 0:1]) & (
        row_index[None, :] < valid_ranges[:, 1:2]
    )
    col_inside = (col_index[None, :] >= valid_ranges[:, 2:3]) & (
        col_index[None, :] < valid_ranges[:, 3:4]
    )
    inside = (row_inside[:, :, None] & col_inside[:, None, :]).astype(jnp.float32)
    merge_weight = (
        inside
        * strip_quality[:, None, None]
        / (1.0 + moment_grids[1] * moment_grids[1] + moment_grids[2] * moment_grids[2])
    )
    moments = jnp.stack(
        [jnp.sum(addend, axis=0) for addend in moment_terms(moment_grids, merge_weight)]
    )
    summed = lax.psum(moments, "acq")
    col_share = col_count // lax.axis_size("acq")
    col_start = lax.axis_index("acq") * col_share
    owned = lax.dynamic_slice_in_dim(summed, col_start, col_share, 2)
    return finalize(owned)


def solution(mesh):
    return jax.shard_map(
        local,
        mesh=mesh,
        in_specs=(P("acq", "tile", None), P("acq"), P("acq", None)),
        out_specs=(P("tile", "acq"), P(None, "tile", "acq")),
        check_vma=False,
    )
```

profile of v0, /device:TPU:12, one launch (start us, length us, event | category | flops | bytes accessed | tf_op | source)
XLA Modules:
  0.0 282.6 jit_solution(14743257655545742816)
XLA Ops:
  7.2 0.0 all-reduce.3.cloned.1.call-start
  7.2 2.3 fusion.24
  9.5 0.1 copy.10
  9.6 2.4 collective-permute-start.1
  12.0 0.1 copy.9
  12.2 4.3 %collective-permute-start = (f32[48,2,1024]{2,0,1:T(8,128)S(1)}, f32[48,2,1024]{2,0,1:T(8,128)S(1)}, u32[]{:S(2)}, u32[]{:S(2)}) collective-permute-start(f32[48,2,1024]{2,0,1:T(8,128)S(1)} %copy.9), channel_id=1, source_target_pairs={{0,4},{4,8},{8,12},{12,16},{16,20},{20,24},{24,28},{1,5},{5,9},{9,... | collective-permute-start | bytes 1179656 | tf_op jit(solution)/shard_map/ppermute | solution.py:12
  16.5 0.1 broadcast_multiply_fusion
  16.6 0.8 slice_bitcast_fusion.3
  17.4 0.1 fusion.1
  17.5 0.1 compare_and_fusion
  17.6 0.0 copy-start.2
  17.6 11.9 %constant_dynamic-update-slice_fusion = f32[48,66,1024]{2,1,0:T(8,128)} fusion(f32[48,64,1024]{2,1,0:T(8,128)} %param.3), kind=kLoop, calls=%fused_computation.78 | loop fusion | bytes 25165824
  29.5 2.2 collective-permute-done
  31.7 0.3 copy.6
  32.0 0.0 collective-permute-done.1
  32.0 1.1 copy_dynamic-update-slice_fusion
  33.1 0.0 copy-done.2
  33.1 59.2 %fusion.23 = (f32[48,64,1024]{2,1,0:T(8,128)}, f32[48,64,1024]{2,1,0:T(8,128)}, f32[48,64,1024]{2,1,0:T(8,128)}, f32[48,64,1024]{2,1,0:T(8,128)}) fusion(f32[48,64,1024]{2,1,0:T(8,128)} %param.3, f32[48]{0:T(128)S(1)} %copy-done.2, pred[48,1024]{1,0:T(8,128)(4,1)S(1)} %fusion.1, pred[48,64]{1,0:T(8,128)(4,1)S(1)} %compare_and_fusion, ...), kind=kLoop, calls=%fused_computation.89 | loop fusion | flops 69206016 | bytes 88526272 | tf_op jit(solution)/shard_map/mul | solution.py:48
  92.4 78.0 %multiply_reduce_fusion = (f32[64,1024]{1,0:T(8,128)S(1)}, f32[64,1024]{1,0:T(8,128)S(1)}, f32[64,1024]{1,0:T(8,128)S(1)}, f32[64,1024]{1,0:T(8,128)S(1)}, f32[6...) fusion(f32[48,64,1024]{2,1,0:T(8,128)} %get-tuple-element.24, ...), kind=kLoop, calls=%fused_computation.8 | loop fusion | flops 150011904 | bytes 92406016 | tf_op jit(solution)/shard_map/reduce_sum | solution.py:95
  170.3 1.7 bitcast_dynamic-update-slice_fusion.14
  172.0 1.7 bitcast_dynamic-update-slice_fusion.13
  173.7 1.7 bitcast_dynamic-update-slice_fusion.12
  175.3 0.7 bitcast_dynamic-update-slice_fusion.11
  176.1 0.7 bitcast_dynamic-update-slice_fusion.10
  176.8 0.7 bitcast_dynamic-update-slice_fusion.9
  177.5 0.7 bitcast_dynamic-update-slice_fusion.8
  178.3 0.7 bitcast_dynamic-update-slice_fusion.7
  179.0 0.7 bitcast_dynamic-update-slice_fusion.6
  179.7 0.7 bitcast_dynamic-update-slice_fusion.5
  180.5 0.7 bitcast_dynamic-update-slice_fusion.4
  181.2 0.7 bitcast_dynamic-update-slice_fusion.3
  181.9 0.7 bitcast_dynamic-update-slice_fusion.2
  182.7 0.7 bitcast_dynamic-update-slice_fusion.1
  183.4 0.7 bitcast_dynamic-update-slice_fusion
  184.1 0.0 all-reduce.3.cloned.1.call-update
  184.1 81.5 %all-reduce.3.cloned.1.call-done = f32[15,64,1024]{2,1,0:T(8,128)} async-done(((f32[15,64,1024]{2,1,0:T(8,128)}), f32[15,64,1024]{2,1,0:T(8,128)}) %all-reduce.3.cloned.1.call-update) | async-done | bytes 3932176 | tf_op jit(solution)/shard_map/psum | solution.py:97
  265.6 0.9 fusion.21
  266.5 0.0 copy-start
  266.5 1.0 fusion.19
  267.5 0.9 fusion.17
  268.4 0.9 fusion.15
  269.4 0.9 fusion.13
  270.3 0.9 fusion.11
  271.2 0.9 fusion.9
  272.2 0.9 fusion.7
  273.1 0.9 fusion.5
  274.0 0.9 fusion.3
  274.9 0.0 copy-start.1
  274.9 0.0 copy-done
  274.9 0.8 copy-done.1
  (1 shorter events, 0.0 us)
Async XLA Ops:
  7.2 258.4 %all-reduce.3.cloned.1.call-start = ((), (), s32[]{:S(2)}) async-start(), calls=%async_computation | async-start | bytes 7864320 | tf_op jit(solution)/shard_map/psum | solution.py:97
  9.6 22.4 %collective-permute-start.1 = (f32[48,2,1024]{2,0,1:T(8,128)S(1)}, f32[48,2,1024]{2,0,1:T(8,128)S(1)}, u32[]{:S(2)}, u32[]{:S(2)}) collective-permute-start(f32[48,2,1024]{2,0,1:T(8,128)S(1)} %copy.10), channel_id=1, source_target_pairs={{4,0},{8,4},{12,8},{16,12},{20,16},{24,20},{28,24},{5,1},{9,5},{13... | collective-permute-start | bytes 1179656 | tf_op jit(solution)/shard_map/ppermute | solution.py:15
  12.2 19.5 %collective-permute-start = (f32[48,2,1024]{2,0,1:T(8,128)S(1)}, f32[48,2,1024]{2,0,1:T(8,128)S(1)}, u32[]{:S(2)}, u32[]{:S(2)}) collective-permute-start(f32[48,2,1024]{2,0,1:T(8,128)S(1)} %copy.9), channel_id=1, source_target_pairs={{0,4},{4,8},{8,12},{12,16},{16,20},{20,24},{24,28},{1,5},{5,9},{9,... | collective-permute-start | bytes 1179656 | tf_op jit(solution)/shard_map/ppermute | solution.py:12
  17.6 15.5 %copy-start.2 = (f32[48]{0:T(128)S(1)}, f32[48]{0:T(128)}, u32[]{:S(2)}) copy-start(f32[48]{0:T(128)} %param.4) | copy-start | bytes 580
  266.5 8.4 %copy-start = (f32[1,64,256]{2,1,0:T(8,128)}, f32[1,64,256]{2,1,0:T(8,128)S(1)}, u32[]{:S(2)}) copy-start(f32[1,64,256]{2,1,0:T(8,128)S(1)} %get-tuple-element.22) | copy-start | bytes 196612
  274.9 0.8 copy-start.1
Sparse Core Ops, SparseCore 0:
  184.2 81.3 all-reduce.2
where the time goes:
time: 285 us; the launch traced here: 283 us
  other arithmetic  147 us (52%)
  waiting for transfers between devices  83.6 us (29%)
  local copies, waits for them, and re-layouts  31.2 us (11%)
  between operations  14.2 us (5%)
  starting transfers between devices  6.78 us (2%)
    psum x1, waiting for transfers between devices, local(): summed = lax.psum(moments, 'acq')  81.5 us
    reduce_sum x1, other arithmetic, local(): jnp.sum(addend, axis=0)  78 us
    mul x1, other arithmetic, moment_terms(): moment_addend_list.append(merge_weight * moment_grids[first_derivative])  59.2 us
    unnamed x23, local copies, waits for them, and re-layouts  26 us
    unnamed x9, other arithmetic  8.37 us
  transfers between devices with their start and end apart: 3, of which 2 were waited for; matrix products, arithmetic and copies ran while one was open for 5% of the time, Pallas kernels for 0%

commit v1 on v0

v1 whole, which is shorter than its diff:
```python
import functools
import jax
import jax.numpy as jnp
from jax import lax
from jax.experimental import pallas as pl
from jax.experimental.pallas import tpu as pltpu
from jax.sharding import PartitionSpec as P

MOMENTS = 15
FEATURES = 4
SUB = 8
LANES = 128
EDGE_ROWS = 4
VMEM_BYTES = 56 * 1024 * 1024
F32 = jnp.float32


def stencil_terms(z, rows, cols, inverse_square, mask):
    row_m2, row_m1, row_p1, row_p2 = rows
    col_m2, col_m1, col_p1, col_p2 = cols
    slope_y = 8.0 * (row_p1 - row_m1) - (row_p2 - row_m2)
    slope_x = 8.0 * (col_p1 - col_m1) - (col_p2 - col_m2)
    center = 30.0 * z
    second_y = 16.0 * (row_p1 + row_m1) - (row_p2 + row_m2) - center
    second_x = 16.0 * (col_p1 + col_m1) - (col_p2 + col_m2) - center
    curvature = second_x * inverse_square + second_y
    steepness = (144.0 + slope_y * slope_y) + slope_x * slope_x * inverse_square
    weight = mask / steepness
    features = (z, slope_x, slope_y, curvature)
    weighted = [weight * feature for feature in features]
    terms = [weight] + weighted
    for first in range(FEATURES):
        for second in range(first, FEATURES):
            terms.append(weighted[first] * features[second])
    return terms


def shifted_columns(z, left, right, lane):
    return (
        pltpu.roll(jnp.where(lane >= LANES - 2, left, z), 2, 1),
        pltpu.roll(jnp.where(lane == LANES - 1, left, z), 1, 1),
        pltpu.roll(jnp.where(lane == 0, right, z), LANES - 1, 1),
        pltpu.roll(jnp.where(lane < 2, right, z), LANES - 2, 1),
    )


def zero_terms():
    return tuple(jnp.zeros((SUB, LANES), F32) for _ in range(MOMENTS))


def halo_kernel(strips_ref, top_ref, bottom_ref, inner_ref, first_ref, last_ref, sems):
    strip_count, row_block, col_count = strips_ref.shape
    copies = []
    for tile in range(col_count // LANES):
        lanes = pl.ds(tile * LANES, LANES)
        for which, (start, target) in enumerate(((0, first_ref), (row_block - SUB, last_ref))):
            copies.append(
                pltpu.make_async_copy(
                    strips_ref.at[:, pl.ds(start, SUB), lanes], target.at[tile], sems.at[which, tile]
                )
            )
    for copy in copies:
        copy.start()
    first_rows = first_ref.reshape(col_count // LANES, strip_count * SUB, LANES)
    last_rows = last_ref.reshape(col_count // LANES, strip_count * SUB, LANES)
    for tile in range(col_count // LANES):
        copies[2 * tile].wait()
        copies[2 * tile + 1].wait()
        lanes = slice(tile * LANES, (tile + 1) * LANES)
        for group in range(strip_count // SUB):
            strips = slice(group * SUB, (group + 1) * SUB)
            for row in range(2):
                at = group * SUB * SUB
                top_ref[row, strips, lanes] = first_rows[tile, pl.ds(at + row, SUB, stride=SUB), :]
                bottom_ref[row, strips, lanes] = last_rows[tile, pl.ds(at + 6 + row, SUB, stride=SUB), :]
                inner_ref[row, strips, lanes] = first_rows[tile, pl.ds(at + 2 + row, SUB, stride=SUB), :]
                inner_ref[2 + row, strips, lanes] = last_rows[tile, pl.ds(at + 4 + row, SUB, stride=SUB), :]


def halo_rows(strips):
    strip_count, row_block, col_count = strips.shape
    tiles = col_count // LANES
    pair = jax.ShapeDtypeStruct((2, strip_count, col_count), F32)
    inner = jax.ShapeDtypeStruct((4, strip_count, col_count), F32)
    vmem = pl.BlockSpec(memory_space=pltpu.VMEM)
    return pl.pallas_call(
        halo_kernel,
        out_shape=(pair, pair, inner),
        in_specs=[pl.BlockSpec(memory_space=pl.ANY)],
        out_specs=(vmem, vmem, vmem),
        scratch_shapes=[
            pltpu.VMEM((tiles, strip_count, SUB, LANES), F32),
            pltpu.VMEM((tiles, strip_count, SUB, LANES), F32),
            pltpu.SemaphoreType.DMA((2, tiles)),
        ],
        compiler_params=pltpu.CompilerParams(vmem_limit_bytes=VMEM_BYTES),
        cost_estimate=pl.CostEstimate(flops=0, bytes_accessed=6 << 20, transcendentals=0),
        name="halo_rows",
    )(strips)


def moment_kernel(
    quality_ref, ranges_ref, cosine_ref, strips_ref, mine_ref, other_ref,
    elevation, row_mask, col_mask, sems, *, remote, first_row, row_count, unroll,
):
    strip_count, row_block, col_count = strips_ref.shape
    tiles = col_count // LANES
    half = tiles // 2
    quarter = half // 2
    position = lax.axis_index("acq")
    side = position // 2
    core = position % 2
    base = (1 - side if remote else side) * half
    row_start = lax.axis_index("tile") * row_block + first_row
    low = max(first_row - SUB, 0)
    high = min(first_row + row_count + SUB, row_block)
    offset = SUB - (first_row - low)

    def fetch(index, tile):
        return pltpu.make_async_copy(
            strips_ref.at[:, pl.ds(low, high - low), pl.ds(pl.multiple_of(tile * LANES, LANES), LANES)],
            elevation.at[:, index, pl.ds(offset, high - low), :],
            sems.at[index],
        )

    for index in range(1, half + 1):
        fetch(index, base + index - 1).start()
    has_left = base > 0
    has_right = base + half < tiles

    @pl.when(has_left)
    def _():
        fetch(0, base - 1).start()

    @pl.when(has_right)
    def _():
        fetch(half + 1, base + half).start()

    zero = jnp.zeros((SUB, LANES), F32)

    def blank(index):
        def body(strip, carry):
            for row in range(row_count // SUB + 2):
                elevation[strip, index, row * SUB:(row + 1) * SUB, :] = zero
            return carry

        lax.fori_loop(0, strip_count, body, 0)

    @pl.when(jnp.logical_not(has_left))
    def _():
        blank(0)

    @pl.when(jnp.logical_not(has_right))
    def _():
        blank(half + 1)

    def prepare(strip, carry):
        quality = quality_ref[strip]
        row_low, row_high = ranges_ref[strip, 0], ranges_ref[strip, 1]
        col_low, col_high = ranges_ref[strip, 2], ranges_ref[strip, 3]
        for tile in range(row_count // SUB):
            row = lax.broadcasted_iota(jnp.int32, (SUB, LANES), 0) + (row_start + tile * SUB)
            row_mask[strip, tile * SUB:(tile + 1) * SUB, :] = jnp.where(
                (row >= row_low) & (row < row_high), quality, 0.0
            )
        for tile in range(half):
            col = lax.broadcasted_iota(jnp.int32, (SUB, LANES), 1) + (base + tile) * LANES
            col_mask[strip, tile] = jnp.where((col >= col_low) & (col < col_high), 1.0, 0.0)
        if low == first_row:
            for tile in range(half + 2):
                elevation[strip, tile, 0:SUB, :] = zero
        if high == first_row + row_count:
            for tile in range(half + 2):
                elevation[strip, tile, SUB + row_count:2 * SUB + row_count, :] = zero
        return carry

    lax.fori_loop(0, strip_count, prepare, 0)

    @pl.when(has_left)
    def _():
        fetch(0, base - 1).wait()

    @pl.when(has_right)
    def _():
        fetch(half + 1, base + half).wait()

    for index in range(1, half + 1):
        fetch(index, base + index - 1).wait()

    lane = lax.broadcasted_iota(jnp.int32, (SUB, LANES), 1)
    for out_ref, owner in ((mine_ref, core), (other_ref, 1 - core)):

        def column_tile(tile, carry, out_ref=out_ref, owner=owner):
            at = owner * quarter + tile
            for row in range(row_count // SUB):
                rows = slice(row * SUB, (row + 1) * SUB)
                cosine = cosine_ref[first_row + row * SUB:first_row + (row + 1) * SUB, :]
                inverse_square = 1.0 / (cosine * cosine)

                def add_strip(strip, sums):
                    def load(shift):
                        start = SUB * (row + 1) + shift
                        return elevation[strip, at + 1, start:start + SUB, :]

                    z = load(0)
                    center = slice(SUB * (row + 1), SUB * (row + 2))
                    cols = shifted_columns(
                        z, elevation[strip, at, center, :], elevation[strip, at + 2, center, :], lane
                    )
                    mask = row_mask[strip, rows, :] * col_mask[strip, at]
                    shifts = (load(-2), load(-1), load(1), load(2))
                    terms = stencil_terms(z, shifts, cols, inverse_square, mask)
                    return tuple(total + term for total, term in zip(sums, terms))

                sums = lax.fori_loop(0, strip_count, add_strip, zero_terms(), unroll=unroll)
                lanes = pl.ds(pl.multiple_of(tile * LANES, LANES), LANES)
                for moment in range(MOMENTS):
                    out_ref[moment, rows, lanes] = sums[moment]
            return carry

        lax.fori_loop(0, quarter, column_tile, 0)


def moments_of(quality, ranges, cosine, strips, remote, first_row, row_count):
    strip_count, row_block, col_count = strips.shape
    half = col_count // LANES // 2
    out = jax.ShapeDtypeStruct((MOMENTS, row_count, col_count // 4), F32)
    vmem = pl.BlockSpec(memory_space=pltpu.VMEM)
    smem = pl.BlockSpec(memory_space=pltpu.SMEM)
    cells = strip_count * row_count * col_count // 2
    return pl.pallas_call(
        functools.partial(
            moment_kernel, remote=remote, first_row=first_row, row_count=row_count, unroll=16
        ),
        out_shape=(out, out),
        in_specs=[smem, smem, vmem, pl.BlockSpec(memory_space=pl.ANY)],
        out_specs=(vmem, vmem),
        scratch_shapes=[
            pltpu.VMEM((strip_count, half + 2, row_count + 2 * SUB, LANES), F32),
            pltpu.VMEM((strip_count, row_count, LANES), F32),
            pltpu.VMEM((strip_count, half, SUB, LANES), F32),
            pltpu.SemaphoreType.DMA((half + 2,)),
        ],
        compiler_params=pltpu.CompilerParams(vmem_limit_bytes=VMEM_BYTES),
        cost_estimate=pl.CostEstimate(flops=64 * cells, bytes_accessed=4 * cells, transcendentals=cells),
        name="moments_remote" if remote else "moments_own",
    )(quality, ranges, cosine, strips)


def edge_kernel(
    quality_ref, ranges_ref, cosine_ref, above_ref, top_ref, inner_ref, bottom_ref, below_ref,
    mine_ref, other_ref,
):
    pair, strip_count, col_count = top_ref.shape
    row_block = cosine_ref.shape[0]
    tiles = col_count // LANES
    quarter = tiles // 4
    position = lax.axis_index("acq")
    side = position // 2
    core = position % 2
    row_start = lax.axis_index("tile") * row_block
    lane = lax.broadcasted_iota(jnp.int32, (SUB, LANES), 1)
    sources = [(above_ref, 0), (above_ref, 1), (top_ref, 0), (top_ref, 1), (inner_ref, 0), (inner_ref, 1)]
    sources += [(inner_ref, 2), (inner_ref, 3), (bottom_ref, 0), (bottom_ref, 1), (below_ref, 0), (below_ref, 1)]
    edges = ((0, 2), (1, 3), (row_block - 2, 8), (row_block - 1, 9))
    for out_ref, owner in ((mine_ref, core), (other_ref, 1 - core)):
        for part, owner_side in enumerate((1 - side, side)):
            out_ref[part, MOMENTS * EDGE_ROWS:, :] = jnp.zeros(
                (out_ref.shape[1] - MOMENTS * EDGE_ROWS, quarter * LANES), F32
            )

            def column_tile(tile, carry, out_ref=out_ref, part=part, first=(owner_side * 2 + owner) * quarter):
                at = first + tile
                left_keep = jnp.where(at > 0, 1.0, 0.0)
                right_keep = jnp.where(at < tiles - 1, 1.0, 0.0)
                here = pl.ds(pl.multiple_of(at * LANES, LANES), LANES)
                before = pl.ds(pl.multiple_of(jnp.maximum(at - 1, 0) * LANES, LANES), LANES)
                after = pl.ds(pl.multiple_of(jnp.minimum(at + 1, tiles - 1) * LANES, LANES), LANES)
                col = lane + at * LANES
                out_lanes = pl.ds(pl.multiple_of(tile * LANES, LANES), LANES)
                for edge, (row, source) in enumerate(edges):
                    cosine = cosine_ref[row:row + 1, :]
                    inverse_square = 1.0 / (cosine * cosine)
                    sums = zero_terms()
                    for group in range(strip_count // SUB):
                        strips = slice(group * SUB, (group + 1) * SUB)

                        def load(shift, where):
                            ref, index = sources[source + shift]
                            return ref[index, strips, where]

                        z = load(0, here)
                        cols = shifted_columns(
                            z, load(0, before) * left_keep, load(0, after) * right_keep, lane
                        )
                        limits = [ranges_ref[kind, strips, :] for kind in range(4)]
                        inside = (limits[0] <= row_start + row) & (limits[1] > row_start + row)
                        inside = inside & (col >= limits[2]) & (col < limits[3])
                        mask = jnp.where(inside, quality_ref[strips, :], 0.0)
                        shifts = tuple(load(shift, here) for shift in (-2, -1, 1, 2))
                        terms = stencil_terms(z, shifts, cols, inverse_square, mask)
                        sums = [total + term for total, term in zip(sums, terms)]
                    for moment in range(MOMENTS):
                        spot = moment * EDGE_ROWS + edge
                        out_ref[part, spot:spot + 1, out_lanes] = jnp.sum(sums[moment], axis=0, keepdims=True)
                return carry

            lax.fori_loop(0, quarter, column_tile, 0)


def edge_moments(quality, ranges, cosine, above, top, inner, bottom, below):
    pair, strip_count, col_count = top.shape
    out = jax.ShapeDtypeStruct((2, -(-MOMENTS * EDGE_ROWS // SUB) * SUB, col_count // 4), F32)
    vmem = pl.BlockSpec(memory_space=pltpu.VMEM)
    cells = 4 * strip_count * col_count
    return pl.pallas_call(
        edge_kernel,
        out_shape=(out, out),
        in_specs=[vmem] * 8,
        out_specs=(vmem, vmem),
        compiler_params=pltpu.CompilerParams(vmem_limit_bytes=VMEM_BYTES),
        cost_estimate=pl.CostEstimate(flops=64 * cells, bytes_accessed=12 * cells, transcendentals=cells),
        name="moments_edge",
    )(quality, ranges, cosine, above, top, inner, bottom, below)


def finish_kernel(pieces, cosine_ref, mine_ref, core_ref, edge_mine_ref, edge_core_ref, edge_far_ref, *refs):
    far_refs = refs[:len(pieces)]
    mean_ref, covariance_ref = refs[len(pieces):]
    row_block, width = mean_ref.shape
    sub = lax.broadcasted_iota(jnp.int32, (SUB, LANES), 0)
    for first_row, far_ref in zip(pieces, far_refs):
        for tile_row in range(first_row, first_row + far_ref.shape[1], SUB):
            rows = slice(tile_row, tile_row + SUB)
            far_rows = slice(tile_row - first_row, tile_row - first_row + SUB)
            cosine = cosine_ref[rows, :]
            scales = (1.0, 1.0 / (12.0 * cosine), 1.0 / 12.0, 1.0 / 12.0)
            spots = {0: ((0, 0), (1, 1)), row_block - SUB: ((SUB - 2, 2), (SUB - 1, 3))}.get(tile_row, ())
            for tile in range(width // LANES):
                lanes = slice(tile * LANES, (tile + 1) * LANES)

                def total(moment):
                    value = (mine_ref[moment, rows, lanes] + core_ref[moment, rows, lanes]) + far_ref[moment, far_rows, lanes]
                    for at, edge in spots:
                        spot = moment * EDGE_ROWS + edge
                        spot = slice(spot, spot + 1)
                        line = (edge_mine_ref[1, spot, lanes] + edge_core_ref[1, spot, lanes]) + edge_far_ref[spot, lanes]
                        value = jnp.where(sub == at, line, value)
                    return value

                inverse = 144.0 / jnp.maximum(144.0 * total(0), 1.0)
                means = [total(1 + first) * inverse * scales[first] for first in range(FEATURES)]
                mean_ref[rows, lanes] = means[0]
                entry = 0
                for first in range(FEATURES):
                    for second in range(first, FEATURES):
                        scale = scales[first] * scales[second]
                        covariance_ref[entry, rows, lanes] = (
                            total(5 + entry) * inverse * scale - means[first] * means[second]
                        )
                        entry += 1


def finish(pieces, cosine, mine, core, edge_mine, edge_core, edge_far, far):
    moments, row_block, width = mine.shape
    vmem = pl.BlockSpec(memory_space=pltpu.VMEM)
    entries = FEATURES * (FEATURES + 1) // 2
    return pl.pallas_call(
        functools.partial(finish_kernel, pieces),
        out_shape=(
            jax.ShapeDtypeStruct((row_block, width), F32),
            jax.ShapeDtypeStruct((entries, row_block, width), F32),
        ),
        in_specs=[vmem] * (6 + len(far)),
        out_specs=(vmem, vmem),
        compiler_params=pltpu.CompilerParams(vmem_limit_bytes=VMEM_BYTES),
        name="finish",
    )(cosine, mine, core, edge_mine, edge_core, edge_far, *far)


def exchange(value, distance):
    count = lax.axis_size("acq")
    return lax.ppermute(value, "acq", [(source, source ^ distance) for source in range(count)])


def local(strips, strip_quality, valid_ranges):
    strip_count, row_block, col_count = strips.shape
    tile_count = lax.axis_size("tile")
    row_index = lax.axis_index("tile") * row_block + jnp.arange(row_block, dtype=jnp.int32)
    latitude = -1.0 + 2.0 * (row_index.astype(F32) + 0.5) / (row_block * tile_count)
    cosine = jnp.broadcast_to(jnp.cos(latitude)[:, None], (row_block, LANES))
    quality_lanes = jnp.broadcast_to(strip_quality[:, None], (strip_count, LANES))
    range_lanes = jnp.broadcast_to(valid_ranges.T[:, :, None], (4, strip_count, LANES))

    top, bottom, inner = halo_rows(strips)
    forward = [(i, i + 1) for i in range(tile_count - 1)]
    backward = [(target, source) for source, target in forward]
    above = lax.ppermute(bottom, "tile", forward)
    below = lax.ppermute(top, "tile", backward)

    piece_rows = row_block // 2
    pieces = tuple(range(0, row_block, piece_rows))
    far = []
    for first_row in pieces:
        mine, other = moments_of(strip_quality, valid_ranges, cosine, strips, True, first_row, piece_rows)
        far.append(exchange(mine + exchange(other, 1), 2))
    mine, other = moments_of(strip_quality, valid_ranges, cosine, strips, False, 0, row_block)
    core = exchange(other, 1)
    edge_mine, edge_other = edge_moments(quality_lanes, range_lanes, cosine, above, top, inner, bottom, below)
    edge_core = exchange(edge_other, 1)
    edge_far = exchange(edge_mine[0] + edge_core[0], 2)
    return finish(pieces, cosine, mine, core, edge_mine, edge_core, edge_far, far)


def solution(mesh):
    return jax.shard_map(
        local,
        mesh=mesh,
        in_specs=(P("acq", "tile", None), P("acq"), P("acq", None)),
        out_specs=(P("tile", "acq"), P(None, "tile", "acq")),
        check_vma=False,
    )
```

time: 285 us -> 101 us (0.35)
  other arithmetic: 147 us -> 1.08 us
  waiting for transfers between devices: 83.6 us -> 18 us
  Pallas kernels: 0 us -> 64.2 us
  local copies, waits for them, and re-layouts: 31.2 us -> 4.87 us
  between operations: 14.2 us -> 0.82 us
  starting transfers between devices: 6.78 us -> 10.4 us
    psum x1 -> x0, waiting for transfers between devices: 81.5 us -> none  [local(): summed = lax.psum(moments, 'acq')]
    reduce_sum x1 -> x0, other arithmetic: 78 us -> none  [local(): jnp.sum(addend, axis=0)]
    pallas_call x0 -> x6, Pallas kernels: none -> 64.2 us  [the longest x3 52.9 us: moments_of(): pl.pallas_call(functools.partial(moment_kernel, remote=remote, first_row=...]
    mul x2 -> x0, other arithmetic: 59.3 us -> none  [the longest x1 59.2 us: moment_terms(): moment_addend_list.append(merge_weight * moment_grids[first_derivative])]
    unnamed x23, local copies, waits for them, and re-layouts: 26 us -> 2.66 us
    ppermute x2 -> x9, waiting for transfers between devices: 2.16 us -> 18 us  [the longest x1 13.7 us: local(): above = lax.ppermute(bottom, 'tile', forward)]
    unnamed x9 -> x0, other arithmetic: 8.37 us -> none
    ppermute x2 -> x9, starting transfers between devices: 6.74 us -> 10.4 us  [the longest x7 4.56 us: exchange(): lax.ppermute(value, 'acq', [(source, source ^ distance) for source in ran...]
  transfers between devices with their start and end apart: 3 -> 9, of which waited for: 2 -> 3; matrix products, arithmetic and copies ran while one was open for 5% -> 3% of each run, Pallas kernels for 0% -> 47%
where the time goes in v1:
time: 101 us; the launch traced here: 99.4 us
  Pallas kernels  64.2 us (64%)
  waiting for transfers between devices  18 us (18%)
  starting transfers between devices  10.4 us (10%)
  local copies, waits for them, and re-layouts  4.87 us (5%)
  other arithmetic  1.08 us (1%)
    pallas_call x3, Pallas kernels, moments_of(): pl.pallas_call(functools.partial(moment_kernel, remote=remote, first_row=...  52.9 us
    ppermute x1, waiting for transfers between devices, local(): above = lax.ppermute(bottom, 'tile', forward)  13.7 us
    pallas_call x1, Pallas kernels, edge_moments(): pl.pallas_call(edge_kernel, out_shape=(out, out), in_specs=[vmem] * 8, ou...  4.94 us
    ppermute x7, starting transfers between devices, exchange(): lax.ppermute(value, 'acq', [(source, source ^ distance) for source in ran...  4.56 us
    ppermute x7, waiting for transfers between devices, exchange(): lax.ppermute(value, 'acq', [(source, source ^ distance) for source in ran...  4.34 us
    ppermute x1, starting transfers between devices, local(): above = lax.ppermute(bottom, 'tile', forward)  3.44 us
    pallas_call x1, Pallas kernels, halo_rows(): pl.pallas_call(halo_kernel, out_shape=(pair, pair, inner), in_specs=[pl.B...  3.28 us
    pallas_call x1, Pallas kernels, finish(): pl.pallas_call(functools.partial(finish_kernel, pieces), out_shape=(jax.S...  3.03 us
  transfers between devices with their start and end apart: 9, of which 3 were waited for; matrix products, arithmetic and copies ran while one was open for 3% of the time, Pallas kernels for 47%

profile of v1, /device:TPU:12, one launch (start us, length us, event | category | flops | bytes accessed | tf_op | source)
XLA Modules:
  0.0 99.4 jit_solution(580719244247481552)
XLA Ops:
  0.7 1.4 %copy.5.ranges_ref = s32[48,4]{1,0:T(8,128)} copy(s32[48,4]{0,1:T(4,128)} %param.5) | data formatting | bytes 1536 | tf_op args[2]
  2.1 0.7 broadcast_in_dim.6.cosine_ref
  2.7 14.1 %moments_remote.3 = (f32[15,32,256]{2,1,0:T(8,128)}, f32[15,32,256]{2,1,0:T(8,128)}) custom-call(f32[48]{0:T(128)} %quality_ref.5, s32[48,4]{1,0:T(8,128)} %copy.5.ranges_ref, f32[64,128]{1,0:T(8,128)} %broadcast_in_dim.6.cosine_ref, f32[48,64,1024]{2,1,0:T(8,128)} %strips_ref.7), custom_call_target="tpu_custom_call" | custom-call | flops 50331648 | bytes 3145728 | tf_op jit(solution)/shard_map/moments_remote/pallas_call | solution.py:231
  16.8 0.1 collective-permute-start.7
  16.9 14.1 %moments_remote.2 = (f32[15,32,256]{2,1,0:T(8,128)}, f32[15,32,256]{2,1,0:T(8,128)}) custom-call(f32[48]{0:T(128)} %quality_ref.5, s32[48,4]{1,0:T(8,128)} %copy.5.ranges_ref, f32[64,128]{1,0:T(8,128)} %broadcast_in_dim.6.cosine_ref, f32[48,64,1024]{2,1,0:T(8,128)} %strips_ref.7), custom_call_target="tpu_custom_call" | custom-call | flops 50331648 | bytes 3145728 | tf_op jit(solution)/shard_map/moments_remote/pallas_call | solution.py:231
  31.0 0.0 copy-start.4
  31.0 0.0 copy-start.3
  31.0 0.0 copy-start.9
  31.0 0.0 copy-start.10
  31.0 0.6 collective-permute-start.5
  31.6 24.8 %moments_own.1 = (f32[15,64,256]{2,1,0:T(8,128)}, f32[15,64,256]{2,1,0:T(8,128)}) custom-call(f32[48]{0:T(128)} %quality_ref.5, s32[48,4]{1,0:T(8,128)} %copy.5.ranges_ref, f32[64,128]{1,0:T(8,128)} %broadcast_in_dim.6.cosine_ref, f32[48,64,1024]{2,1,0:T(8,128)} %strips_ref.7), custom_call_target="tpu_custom_call" | custom-call | flops 100663296 | bytes 6291456 | tf_op jit(solution)/shard_map/moments_own/pallas_call | solution.py:231
  56.4 0.2 collective-permute-start
  56.6 3.3 %halo_rows.1 = (f32[2,48,1024]{2,1,0:T(8,128)}, f32[2,48,1024]{2,1,0:T(8,128)}, f32[4,48,1024]{2,1,0:T(8,128)}) custom-call(f32[48,64,1024]{2,1,0:T(8,128)} %strips_ref.7), custom_call_target="tpu_custom_call" | custom-call | bytes 6291456 | tf_op jit(solution)/shard_map/halo_rows/pallas_call | solution.py:86
  59.9 3.4 %collective-permute-start.1 = (f32[2,48,1024]{2,1,0:T(8,128)}, f32[2,48,1024]{2,1,0:T(8,128)S(1)}, u32[]{:S(2)}, u32[]{:S(2)}) collective-permute-start(f32[2,48,1024]{2,1,0:T(8,128)} %get-tuple-element.15.bottom_ref), channel_id=1, source_target_pairs={{0,4},{4,8},{8,12},{12,16},{16,20},{20,24},{24,28},{1,5},{5,9},{9,... | collective-permute-start | bytes 1179656 | tf_op jit(solution)/shard_map/ppermute | solution.py:398
  63.4 2.4 %collective-permute-start.2 = (f32[2,48,1024]{2,1,0:T(8,128)}, f32[2,48,1024]{2,1,0:T(8,128)S(1)}, u32[]{:S(2)}, u32[]{:S(2)}) collective-permute-start(f32[2,48,1024]{2,1,0:T(8,128)} %get-tuple-element.16.top_ref), channel_id=1, source_target_pairs={{4,0},{8,4},{12,8},{16,12},{20,16},{24,20},{28,24},{5,1},{9,5},{13... | collective-permute-start | bytes 1179656 | tf_op jit(solution)/shard_map/ppermute | solution.py:399
  65.8 0.0 collective-permute-done.7
  65.8 0.0 copy-done.4
  65.8 0.1 add.51
  65.9 1.6 %collective-permute-start.8 = (f32[15,32,256]{2,1,0:T(8,128)S(1)}, f32[15,32,256]{2,1,0:T(8,128)S(1)}, u32[]{:S(2)}, u32[]{:S(2)}) collective-permute-start(f32[15,32,256]{2,1,0:T(8,128)S(1)} %add.51), channel_id=1, source_target_pairs={{0,2},{1,3},{2,0},{3,1},{4,6},{5,7},{6,4},{7,5},{8,10},{9,11},{10,... | collective-permute-start | bytes 1474568 | tf_op jit(solution)/shard_map/ppermute | solution.py:383
  67.4 0.0 collective-permute-done.5
  67.4 0.0 copy-done.3
  67.4 0.1 add.50
  67.5 0.6 collective-permute-start.6
  68.1 13.7 %collective-permute-done.1.above_ref = f32[2,48,1024]{2,1,0:T(8,128)S(1)} collective-permute-done((f32[2,48,1024]{2,1,0:T(8,128)}, f32[2,48,1024]{2,1,0:T(8,128)S(1)}, u32[]{:S(2)}, u32[]{:S(2)}) %collective-permute-start.1) | collective-permute-done | bytes 393248 | tf_op jit(solution)/shard_map/ppermute | solution.py:398
  81.8 0.0 copy-start.5
  81.8 0.0 collective-permute-done.2.below_ref
  81.8 0.0 copy-done.9
  81.8 0.0 copy-start.6
  81.8 0.8 broadcast_in_dim.7.quality_ref
  82.6 0.0 copy-done.10
  82.6 0.7 broadcast_in_dim.8.ranges_ref
  83.4 0.0 copy-done.5
  83.4 0.0 copy-done.6
  83.4 4.9 %moments_edge.1 = (f32[2,64,256]{2,1,0:T(8,128)}, f32[2,64,256]{2,1,0:T(8,128)}) custom-call(f32[48,128]{1,0:T(8,128)} %broadcast_in_dim.7.quality_ref, s32[4,48,128]{2,1,0:T(8,128)} %broadcast_in_dim.8.ranges_ref, f32[64,128]{1,0:T(8,128)} %broadcast_in_dim.6.cosine_ref, f32[2,48,1024]{2,1,0:T(8,128)} %copy-done.5, ...), custom_call_target="tpu_custom_call" | custom-call | flops 12582912 | bytes 2359296 | tf_op jit(solution)/shard_map/moments_edge/pallas_call | solution.py:316
  88.3 0.0 collective-permute-start.3
  88.3 1.6 %collective-permute-done.3.edge_core_ref = f32[2,64,256]{2,1,0:T(8,128)S(1)} collective-permute-done((f32[2,64,256]{2,1,0:T(8,128)}, f32[2,64,256]{2,1,0:T(8,128)S(1)}, u32[]{:S(2)}, u32[]{:S(2)}) %collective-permute-start.3) | collective-permute-done | bytes 131104 | tf_op jit(solution)/shard_map/ppermute | solution.py:383
  89.9 0.0 copy-start.7
  89.9 0.9 fusion
  90.8 1.6 %collective-permute-start.4 = (f32[64,256]{1,0:T(8,128)S(1)}, f32[64,256]{1,0:T(8,128)S(1)}, u32[]{:S(2)}, u32[]{:S(2)}) collective-permute-start(f32[64,256]{1,0:T(8,128)S(1)} %fusion), channel_id=1, source_target_pairs={{0,2},{1,3},{2,0},{3,1},{4,6},{5,7},{6,4},{7,5},{8,10},{9,11},{10,... | collective-permute-start | bytes 196616 | tf_op jit(solution)/shard_map/ppermute | solution.py:383
  92.3 2.8 %collective-permute-done.4.edge_far_ref = f32[64,256]{1,0:T(8,128)S(1)} collective-permute-done((f32[64,256]{1,0:T(8,128)S(1)}, f32[64,256]{1,0:T(8,128)S(1)}, u32[]{:S(2)}, u32[]{:S(2)}) %collective-permute-start.4) | collective-permute-done | bytes 65568 | tf_op jit(solution)/shard_map/ppermute | solution.py:383
  95.1 0.0 copy-start.8
  95.1 0.0 collective-permute-done.8.refs_1_
  95.1 0.0 copy-start.1
  95.1 0.0 collective-permute-done.6.refs_0_
  95.1 0.0 copy-start.2
  95.1 0.0 collective-permute-done.core_ref
  95.1 0.0 copy-start
  95.2 0.0 copy-done.7
  95.2 0.6 copy-done.8
  95.7 0.2 copy-done.1
  95.9 0.2 copy-done.2
  96.1 0.3 copy-done
  96.4 3.0 %finish.1 = (f32[64,256]{1,0:T(8,128)}, f32[10,64,256]{2,1,0:T(8,128)}) custom-call(f32[64,128]{1,0:T(8,128)} %broadcast_in_dim.6.cosine_ref, f32[15,64,256]{2,1,0:T(8,128)} %get-tuple-element.13.mine_ref, f32[15,64,256]{2,1,0:T(8,128)} %copy-done, f32[2,64,256]{2,1,0:T(8,128)} %get-tuple-element.18.edge_mine_ref, f32[2,64,256]{2,1,0:T(8,128)} %copy-done.7, ...), custom_call_target="tpu_custom_call" | custom-call | tf_op jit(solution)/shard_map/finish/pallas_call | solution.py:368
  (1 shorter events, 0.0 us)
Async XLA Ops:
  16.8 49.0 %collective-permute-start.7 = (f32[15,32,256]{2,1,0:T(8,128)}, f32[15,32,256]{2,1,0:T(8,128)S(1)}, u32[]{:S(2)}, u32[]{:S(2)}) collective-permute-start(f32[15,32,256]{2,1,0:T(8,128)} %get-tuple-element.23), channel_id=1, source_target_pairs={{0,1},{1,0},{2,3},{3,2},{4,5},{5,4},{6,7},{7,6},{8,9},{9,8},{10,11... | collective-permute-start | bytes 1474568 | tf_op jit(solution)/shard_map/ppermute | solution.py:383
  31.0 34.8 %copy-start.4 = (f32[15,32,256]{2,1,0:T(8,128)S(1)}, f32[15,32,256]{2,1,0:T(8,128)}, u32[]{:S(2)}) copy-start(f32[15,32,256]{2,1,0:T(8,128)} %get-tuple-element.22) | copy-start | bytes 1474564
  31.0 36.5 %copy-start.3 = (f32[15,32,256]{2,1,0:T(8,128)S(1)}, f32[15,32,256]{2,1,0:T(8,128)}, u32[]{:S(2)}) copy-start(f32[15,32,256]{2,1,0:T(8,128)} %get-tuple-element.20) | copy-start | bytes 1474564
  31.0 50.8 %copy-start.9 = (f32[48]{0:T(128)S(1)}, f32[48]{0:T(128)}, u32[]{:S(2)}) copy-start(f32[48]{0:T(128)} %quality_ref.5) | copy-start | bytes 580
  31.0 51.6 %copy-start.10 = (s32[48,4]{0,1:T(4,128)S(1)}, s32[48,4]{0,1:T(4,128)}, u32[]{:S(2)}) copy-start(s32[48,4]{0,1:T(4,128)} %param.5) | copy-start | bytes 2308
  31.0 36.4 %collective-permute-start.5 = (f32[15,32,256]{2,1,0:T(8,128)}, f32[15,32,256]{2,1,0:T(8,128)S(1)}, u32[]{:S(2)}, u32[]{:S(2)}) collective-permute-start(f32[15,32,256]{2,1,0:T(8,128)} %get-tuple-element.21), channel_id=1, source_target_pairs={{0,1},{1,0},{2,3},{3,2},{4,5},{5,4},{6,7},{7,6},{8,9},{9,8},{10,11... | collective-permute-start | bytes 1474568 | tf_op jit(solution)/shard_map/ppermute | solution.py:383
  56.4 38.7 %collective-permute-start = (f32[15,64,256]{2,1,0:T(8,128)}, f32[15,64,256]{2,1,0:T(8,128)S(1)}, u32[]{:S(2)}, u32[]{:S(2)}) collective-permute-start(f32[15,64,256]{2,1,0:T(8,128)} %get-tuple-element.14), channel_id=1, source_target_pairs={{0,1},{1,0},{2,3},{3,2},{4,5},{5,4},{6,7},{7,6},{8,9},{9,8},{10,11... | collective-permute-start | bytes 2949128 | tf_op jit(solution)/shard_map/ppermute | solution.py:383
  59.9 21.9 %collective-permute-start.1 = (f32[2,48,1024]{2,1,0:T(8,128)}, f32[2,48,1024]{2,1,0:T(8,128)S(1)}, u32[]{:S(2)}, u32[]{:S(2)}) collective-permute-start(f32[2,48,1024]{2,1,0:T(8,128)} %get-tuple-element.15.bottom_ref), channel_id=1, source_target_pairs={{0,4},{4,8},{8,12},{12,16},{16,20},{20,24},{24,28},{1,5},{5,9},{9,... | collective-permute-start | bytes 1179656 | tf_op jit(solution)/shard_map/ppermute | solution.py:398
  63.4 18.5 %collective-permute-start.2 = (f32[2,48,1024]{2,1,0:T(8,128)}, f32[2,48,1024]{2,1,0:T(8,128)S(1)}, u32[]{:S(2)}, u32[]{:S(2)}) collective-permute-start(f32[2,48,1024]{2,1,0:T(8,128)} %get-tuple-element.16.top_ref), channel_id=1, source_target_pairs={{4,0},{8,4},{12,8},{16,12},{20,16},{24,20},{28,24},{5,1},{9,5},{13... | collective-permute-start | bytes 1179656 | tf_op jit(solution)/shard_map/ppermute | solution.py:399
  65.9 29.2 %collective-permute-start.8 = (f32[15,32,256]{2,1,0:T(8,128)S(1)}, f32[15,32,256]{2,1,0:T(8,128)S(1)}, u32[]{:S(2)}, u32[]{:S(2)}) collective-permute-start(f32[15,32,256]{2,1,0:T(8,128)S(1)} %add.51), channel_id=1, source_target_pairs={{0,2},{1,3},{2,0},{3,1},{4,6},{5,7},{6,4},{7,5},{8,10},{9,11},{10,... | collective-permute-start | bytes 1474568 | tf_op jit(solution)/shard_map/ppermute | solution.py:383
  67.5 27.6 %collective-permute-start.6 = (f32[15,32,256]{2,1,0:T(8,128)S(1)}, f32[15,32,256]{2,1,0:T(8,128)S(1)}, u32[]{:S(2)}, u32[]{:S(2)}) collective-permute-start(f32[15,32,256]{2,1,0:T(8,128)S(1)} %add.50), channel_id=1, source_target_pairs={{0,2},{1,3},{2,0},{3,1},{4,6},{5,7},{6,4},{7,5},{8,10},{9,11},{10,... | collective-permute-start | bytes 1474568 | tf_op jit(solution)/shard_map/ppermute | solution.py:383
  81.8 1.6 %copy-start.5 = (f32[2,48,1024]{2,1,0:T(8,128)}, f32[2,48,1024]{2,1,0:T(8,128)S(1)}, u32[]{:S(2)}) copy-start(f32[2,48,1024]{2,1,0:T(8,128)S(1)} %collective-permute-done.1.above_ref) | copy-start | bytes 1179652
  81.8 1.5 %copy-start.6 = (f32[2,48,1024]{2,1,0:T(8,128)}, f32[2,48,1024]{2,1,0:T(8,128)S(1)}, u32[]{:S(2)}) copy-start(f32[2,48,1024]{2,1,0:T(8,128)S(1)} %collective-permute-done.2.below_ref) | copy-start | bytes 1179652
  88.3 1.6 %collective-permute-start.3 = (f32[2,64,256]{2,1,0:T(8,128)}, f32[2,64,256]{2,1,0:T(8,128)S(1)}, u32[]{:S(2)}, u32[]{:S(2)}) collective-permute-start(f32[2,64,256]{2,1,0:T(8,128)} %get-tuple-element.19), channel_id=1, source_target_pairs={{0,1},{1,0},{2,3},{3,2},{4,5},{5,4},{6,7},{7,6},{8,9},{9,8},{10,11... | collective-permute-start | bytes 393224 | tf_op jit(solution)/shard_map/ppermute | solution.py:383
  89.9 5.3 %copy-start.7 = (f32[2,64,256]{2,1,0:T(8,128)}, f32[2,64,256]{2,1,0:T(8,128)S(1)}, u32[]{:S(2)}) copy-start(f32[2,64,256]{2,1,0:T(8,128)S(1)} %collective-permute-done.3.edge_core_ref) | copy-start | bytes 393220
  90.8 4.3 %collective-permute-start.4 = (f32[64,256]{1,0:T(8,128)S(1)}, f32[64,256]{1,0:T(8,128)S(1)}, u32[]{:S(2)}, u32[]{:S(2)}) collective-permute-start(f32[64,256]{1,0:T(8,128)S(1)} %fusion), channel_id=1, source_target_pairs={{0,2},{1,3},{2,0},{3,1},{4,6},{5,7},{6,4},{7,5},{8,10},{9,11},{10,... | collective-permute-start | bytes 196616 | tf_op jit(solution)/shard_map/ppermute | solution.py:383
  95.1 0.6 copy-start.8
  95.1 0.8 copy-start.1
  95.1 1.0 copy-start.2
  95.1 1.3 %copy-start = (f32[15,64,256]{2,1,0:T(8,128)}, f32[15,64,256]{2,1,0:T(8,128)S(1)}, u32[]{:S(2)}) copy-start(f32[15,64,256]{2,1,0:T(8,128)S(1)} %collective-permute-done.core_ref) | copy-start | bytes 2949124

commit v2 on v1

v2 whole, which is shorter than its diff:
```python
import functools
import jax
import jax.numpy as jnp
from jax import lax
from jax.experimental import pallas as pl
from jax.experimental.pallas import tpu as pltpu
from jax.sharding import PartitionSpec as P

MOMENTS = 15
FEATURES = 4
SUB = 8
LANES = 128
EDGE_ROWS = 4
VMEM_BYTES = 56 * 1024 * 1024
F32 = jnp.float32
LOAD_PARTS = 4
SMALL_COST = pl.CostEstimate(flops=1, bytes_accessed=1, transcendentals=0)


def moment_terms(z, slope_x, second_x, rows, inverse_square, mask):
    row_m2, row_m1, row_p1, row_p2 = rows
    slope_y = 8.0 * (row_p1 - row_m1) - (row_p2 - row_m2)
    second_y = 16.0 * (row_p1 + row_m1) - (row_p2 + row_m2) - 30.0 * z
    curvature = second_x * inverse_square + second_y
    steepness = (144.0 + slope_y * slope_y) + slope_x * slope_x * inverse_square
    weight = mask / steepness
    features = (z, slope_x, slope_y, curvature)
    weighted = [weight * feature for feature in features]
    terms = [weight] + weighted
    for first in range(FEATURES):
        for second in range(first, FEATURES):
            terms.append(weighted[first] * features[second])
    return terms


def stencil_terms(z, rows, cols, inverse_square, mask):
    col_m2, col_m1, col_p1, col_p2 = cols
    slope_x = 8.0 * (col_p1 - col_m1) - (col_p2 - col_m2)
    second_x = 16.0 * (col_p1 + col_m1) - (col_p2 + col_m2) - 30.0 * z
    return moment_terms(z, slope_x, second_x, rows, inverse_square, mask)


def shifted_columns(z, left, right, lane):
    return (
        pltpu.roll(jnp.where(lane >= LANES - 2, left, z), 2, 1),
        pltpu.roll(jnp.where(lane == LANES - 1, left, z), 1, 1),
        pltpu.roll(jnp.where(lane == 0, right, z), LANES - 1, 1),
        pltpu.roll(jnp.where(lane < 2, right, z), LANES - 2, 1),
    )


def zero_terms():
    return tuple(jnp.zeros((SUB, LANES), F32) for _ in range(MOMENTS))


def halo_kernel(
    quality_ref, ranges_ref, strips_ref, top_ref, bottom_ref, inner_ref, cosine_ref, limits_ref,
    first_ref, last_ref, sems,
):
    strip_count, row_block, col_count = strips_ref.shape
    copies = []
    for tile in range(col_count // LANES):
        lanes = pl.ds(tile * LANES, LANES)
        for which, (start, target) in enumerate(((0, first_ref), (row_block - SUB, last_ref))):
            copies.append(
                pltpu.make_async_copy(
                    strips_ref.at[:, pl.ds(start, SUB), lanes], target.at[tile], sems.at[which, tile]
                )
            )
    for copy in copies:
        copy.start()
    total_rows = row_block * lax.axis_size("tile")
    row_start = lax.axis_index("tile") * row_block
    for tile in range(row_block // SUB):
        row = lax.broadcasted_iota(jnp.int32, (SUB, LANES), 0) + (row_start + tile * SUB)
        latitude = -1.0 + 2.0 * (row.astype(F32) + 0.5) / total_rows
        cosine_ref[tile * SUB:(tile + 1) * SUB, :] = jnp.cos(latitude)

    def spread(strip, carry):
        here = pl.ds(strip, 1)
        for kind in range(4):
            value = ranges_ref[kind, strip].astype(F32)
            limits_ref[kind, here, :] = jnp.full((1, LANES), value, F32)
        limits_ref[4, here, :] = jnp.full((1, LANES), quality_ref[strip], F32)
        return carry

    lax.fori_loop(0, strip_count, spread, 0)
    first_rows = first_ref.reshape(col_count // LANES, strip_count * SUB, LANES)
    last_rows = last_ref.reshape(col_count // LANES, strip_count * SUB, LANES)
    for tile in range(col_count // LANES):
        copies[2 * tile].wait()
        copies[2 * tile + 1].wait()
        lanes = slice(tile * LANES, (tile + 1) * LANES)
        for group in range(strip_count // SUB):
            strips = slice(group * SUB, (group + 1) * SUB)
            for row in range(2):
                at = group * SUB * SUB
                top_ref[row, strips, lanes] = first_rows[tile, pl.ds(at + row, SUB, stride=SUB), :]
                bottom_ref[row, strips, lanes] = last_rows[tile, pl.ds(at + 6 + row, SUB, stride=SUB), :]
                inner_ref[row, strips, lanes] = first_rows[tile, pl.ds(at + 2 + row, SUB, stride=SUB), :]
                inner_ref[2 + row, strips, lanes] = last_rows[tile, pl.ds(at + 4 + row, SUB, stride=SUB), :]


def halo_rows(quality, ranges, strips):
    strip_count, row_block, col_count = strips.shape
    tiles = col_count // LANES
    pair = jax.ShapeDtypeStruct((2, strip_count, col_count), F32)
    inner = jax.ShapeDtypeStruct((4, strip_count, col_count), F32)
    cosine = jax.ShapeDtypeStruct((row_block, LANES), F32)
    limits = jax.ShapeDtypeStruct((5, strip_count, LANES), F32)
    vmem = pl.BlockSpec(memory_space=pltpu.VMEM)
    smem = pl.BlockSpec(memory_space=pltpu.SMEM)
    return pl.pallas_call(
        halo_kernel,
        out_shape=(pair, pair, inner, cosine, limits),
        in_specs=[smem, smem, pl.BlockSpec(memory_space=pl.ANY)],
        out_specs=(vmem,) * 5,
        scratch_shapes=[
            pltpu.VMEM((tiles, strip_count, SUB, LANES), F32),
            pltpu.VMEM((tiles, strip_count, SUB, LANES), F32),
            pltpu.SemaphoreType.DMA((2, tiles)),
        ],
        compiler_params=pltpu.CompilerParams(vmem_limit_bytes=VMEM_BYTES),
        cost_estimate=SMALL_COST,
        name="halo_rows",
    )(quality, ranges, strips)


def column_weights():
    source = lax.broadcasted_iota(jnp.int32, (4 * LANES, 2 * LANES), 0)
    target = lax.broadcasted_iota(jnp.int32, (4 * LANES, 2 * LANES), 1)
    lane = source % LANES
    lane = jnp.where(source < 2 * LANES, lane, jnp.where(lane < LANES // 2, lane + LANES, lane - LANES))
    distance = lane - target % LANES
    near, far = jnp.abs(distance) == 1, jnp.abs(distance) == 2
    sign = jnp.where(distance > 0, 1.0, -1.0)
    slope = jnp.where(near, 8.0 * sign, jnp.where(far, -sign, 0.0))
    second = jnp.where(near, 16.0, jnp.where(far, -1.0, jnp.where(distance == 0, -30.0, 0.0)))
    return jnp.where(target < LANES, slope, second).astype(jnp.bfloat16)


def moment_kernel(
    quality_ref, ranges_ref, cosine_ref, strips_ref, first_order_ref, second_order_ref, mine_ref,
    *refs, remote, first_row, row_count, pieces,
):
    other_refs, token_ref = refs[:pieces], refs[pieces]
    elevation, high_part, low_part, row_mask, col_mask, weights, first_slot, second_slot, sems = refs[pieces + 1:]
    del first_order_ref, second_order_ref
    token_ref[...] = jnp.zeros((SUB, LANES), F32)
    strip_count, row_block, col_count = strips_ref.shape
    tiles = col_count // LANES
    half = tiles // 2
    quarter = half // 2
    position = lax.axis_index("acq")
    side = position // 2
    core = position % 2
    base = (1 - side if remote else side) * half
    row_start = lax.axis_index("tile") * row_block + first_row
    low = max(first_row - SUB, 0)
    high = min(first_row + row_count + SUB, row_block)
    offset = SUB - (first_row - low)

    part = strip_count // LOAD_PARTS

    def fetch(index, which):
        lanes = pl.ds(pl.multiple_of((base + index - 1) * LANES, LANES), LANES)
        strips = pl.ds(which * part, part)
        return pltpu.make_async_copy(
            strips_ref.at[strips, pl.ds(low, high - low), lanes],
            elevation.at[strips, index, pl.ds(offset, high - low), :],
            sems.at[index, which],
        )

    def present(index):
        return (base + index >= 1) & (base + index <= tiles)

    def start(index, which):
        @pl.when(present(index))
        def _():
            fetch(index, which).start()

    zero = jnp.zeros((SUB, LANES), F32)

    def blank(index):
        @pl.when(jnp.logical_not(present(index)))
        def _():
            def body(strip, carry):
                for row in range(1, row_count // SUB + 1):
                    elevation[strip, index, row * SUB:(row + 1) * SUB, :] = zero
                return carry

            lax.fori_loop(0, strip_count, body, 0)

    def arrive(index, which):
        @pl.when(present(index))
        def _():
            fetch(index, which).wait()

        def split(step, carry):
            strip = which * part + step
            value = elevation[strip, index, SUB:SUB + row_count, :]
            upper = value.astype(jnp.bfloat16)
            high_part[strip, index] = upper
            low_part[strip, index] = (value - upper.astype(F32)).astype(jnp.bfloat16)
            return carry

        lax.fori_loop(0, part, split, 0, unroll=4)

    initial = (1 - core) * quarter
    later = core * quarter
    final = later + 2 * core
    for which in range(LOAD_PARTS):
        for step in range(3):
            start(initial + step, which)
    blank(0)
    blank(half + 1)

    weights[...] = column_weights()

    def prepare(strip, carry):
        quality = quality_ref[strip]
        row_low, row_high = ranges_ref[0, strip], ranges_ref[1, strip]
        col_low, col_high = ranges_ref[2, strip], ranges_ref[3, strip]
        for tile in range(row_count // SUB):
            row = lax.broadcasted_iota(jnp.int32, (SUB, LANES), 0) + (row_start + tile * SUB)
            row_mask[strip, tile * SUB:(tile + 1) * SUB, :] = jnp.where(
                (row >= row_low) & (row < row_high), quality, 0.0
            )
        for tile in range(half):
            col = lax.broadcasted_iota(jnp.int32, (SUB, LANES), 1) + (base + tile) * LANES
            col_mask[strip, tile] = jnp.where((col >= col_low) & (col < col_high), 1.0, 0.0)
        if low == first_row:
            for tile in range(half + 2):
                elevation[strip, tile, 0:SUB, :] = zero
        if high == first_row + row_count:
            for tile in range(half + 2):
                elevation[strip, tile, SUB + row_count:2 * SUB + row_count, :] = zero
        return carry

    lax.fori_loop(0, strip_count, prepare, 0)

    tile_rows = row_count // SUB
    share = strip_count // tile_rows
    slots = (first_slot, second_slot)

    def columns_into(slot, at, first, count):
        strips = pl.ds(first, count)
        lane = lax.broadcasted_iota(jnp.int32, (count * row_count, LANES), 1)

        def load(ref, tile):
            return ref[strips, tile].reshape(count * row_count, LANES)

        edges = [
            jnp.where(lane < LANES // 2, load(ref, at + 1), load(ref, at - 1))
            for ref in (high_part, low_part)
        ]
        left = jnp.concatenate([load(high_part, at), load(low_part, at)] + edges, axis=1)
        product = jnp.dot(left, weights[...], preferred_element_type=F32)
        slots[slot][strips] = product.reshape(count, row_count, 2 * LANES)

    def column_tile(slot, at, following, store, lanes):
        def row_tile(tile, carry):
            row = pl.multiple_of(tile * SUB, SUB)
            cosine = cosine_ref[pl.ds(first_row + row, SUB), :]
            inverse_square = 1.0 / (cosine * cosine)

            if following is not None:
                columns_into(1 - slot, following, tile * share, share)
            unroll = strip_count if following is not None else 16

            def add_strips(chunk, sums):
                for index in range(unroll):
                    strip = chunk * unroll + index

                    def load(shift):
                        return elevation[strip, at, pl.ds(SUB + row + shift, SUB), :]

                    slope_x = slots[slot][strip, pl.ds(row, SUB), :LANES]
                    second_x = slots[slot][strip, pl.ds(row, SUB), LANES:]
                    mask = row_mask[strip, pl.ds(row, SUB), :] * col_mask[strip, at - 1]
                    shifts = (load(-2), load(-1), load(1), load(2))
                    terms = moment_terms(load(0), slope_x, second_x, shifts, inverse_square, mask)
                    sums = [total + term for total, term in zip(sums, terms)]
                return tuple(sums)

            if following is not None:
                sums = add_strips(0, zero_terms())
            else:
                sums = lax.fori_loop(0, strip_count // unroll, add_strips, zero_terms())
            for moment in range(MOMENTS):
                store(moment, pl.ds(row, SUB), lanes, sums[moment])
            return carry

        lax.fori_loop(0, tile_rows, row_tile, 0)

    for which in range(LOAD_PARTS):
        start(initial + 3, which)
    for which in range(LOAD_PARTS):
        for step in range(2):
            start(final + step, which)

    def first_columns(which, carry):
        for step in range(3):
            arrive(initial + step, which)
        columns_into(0, initial + 1, which * part, part)
        return carry

    lax.fori_loop(0, LOAD_PARTS, first_columns, 0)

    def arrive_whole(index):
        def body(which, carry):
            arrive(index, which)
            return carry

        lax.fori_loop(0, LOAD_PARTS, body, 0)

    def store_other(moment, rows, lanes, value):
        share = MOMENTS // pieces
        other_refs[moment // share][moment % share, rows, lanes] = value

    def store_mine(moment, rows, lanes, value):
        mine_ref[moment, rows, lanes] = value

    arrive_whole(initial + 3)
    column_tile(0, initial + 1, initial + 2, store_other, slice(0, LANES))
    arrive_whole(final)
    arrive_whole(final + 1)
    column_tile(1, initial + 2, later + 1, store_other, slice(LANES, 2 * LANES))
    column_tile(0, later + 1, later + 2, store_mine, slice(0, LANES))
    column_tile(1, later + 2, None, store_mine, slice(LANES, 2 * LANES))


def moments_of(quality, ranges, cosine, strips, order, remote, first_row, row_count, pieces):
    strip_count, row_block, col_count = strips.shape
    half = col_count // LANES // 2
    out = jax.ShapeDtypeStruct((MOMENTS, row_count, col_count // 4), F32)
    piece = jax.ShapeDtypeStruct((MOMENTS // pieces, row_count, col_count // 4), F32)
    token = jax.ShapeDtypeStruct((SUB, LANES), F32)
    vmem = pl.BlockSpec(memory_space=pltpu.VMEM)
    smem = pl.BlockSpec(memory_space=pltpu.SMEM)
    anywhere = pl.BlockSpec(memory_space=pl.ANY)
    parts = pltpu.VMEM((strip_count, half + 2, row_count, LANES), jnp.bfloat16)
    slot = pltpu.VMEM((strip_count, row_count, 2 * LANES), F32)
    return pl.pallas_call(
        functools.partial(moment_kernel, remote=remote, first_row=first_row, row_count=row_count, pieces=pieces),
        out_shape=(out,) + (piece,) * pieces + (token,),
        in_specs=[smem, smem, vmem, anywhere, anywhere, anywhere],
        out_specs=(vmem,) * (pieces + 2),
        scratch_shapes=[
            pltpu.VMEM((strip_count, half + 2, row_count + 2 * SUB, LANES), F32),
            parts,
            parts,
            pltpu.VMEM((strip_count, row_count, LANES), F32),
            pltpu.VMEM((strip_count, half, SUB, LANES), F32),
            pltpu.VMEM((4 * LANES, 2 * LANES), jnp.bfloat16),
            slot,
            slot,
            pltpu.SemaphoreType.DMA((half + 2, LOAD_PARTS)),
        ],
        compiler_params=pltpu.CompilerParams(vmem_limit_bytes=VMEM_BYTES),
        cost_estimate=SMALL_COST,
        name="moments_remote" if remote else "moments_own",
    )(quality, ranges, cosine, strips, *order)


def edge_kernel(
    limits_ref, cosine_ref, above_ref, top_ref, inner_ref, bottom_ref, below_ref,
    order_ref, mine_ref, other_ref, token_ref,
):
    del order_ref
    token_ref[...] = jnp.zeros((SUB, LANES), F32)
    pair, strip_count, col_count = top_ref.shape
    row_block = cosine_ref.shape[0]
    tiles = col_count // LANES
    quarter = tiles // 4
    position = lax.axis_index("acq")
    side = position // 2
    core = position % 2
    row_start = lax.axis_index("tile") * row_block
    lane = lax.broadcasted_iota(jnp.int32, (SUB, LANES), 1)
    sources = [(above_ref, 0), (above_ref, 1), (top_ref, 0), (top_ref, 1), (inner_ref, 0), (inner_ref, 1)]
    sources += [(inner_ref, 2), (inner_ref, 3), (bottom_ref, 0), (bottom_ref, 1), (below_ref, 0), (below_ref, 1)]
    edges = ((0, 2), (1, 3), (row_block - 2, 8), (row_block - 1, 9))
    for out_ref, owner in ((mine_ref, core), (other_ref, 1 - core)):
        for part, owner_side in enumerate((1 - side, side)):
            out_ref[part, MOMENTS * EDGE_ROWS:, :] = jnp.zeros(
                (out_ref.shape[1] - MOMENTS * EDGE_ROWS, quarter * LANES), F32
            )

            def column_tile(tile, carry, out_ref=out_ref, part=part, first=(owner_side * 2 + owner) * quarter):
                at = first + tile
                left_keep = jnp.where(at > 0, 1.0, 0.0)
                right_keep = jnp.where(at < tiles - 1, 1.0, 0.0)
                here = pl.ds(pl.multiple_of(at * LANES, LANES), LANES)
                before = pl.ds(pl.multiple_of(jnp.maximum(at - 1, 0) * LANES, LANES), LANES)
                after = pl.ds(pl.multiple_of(jnp.minimum(at + 1, tiles - 1) * LANES, LANES), LANES)
                col = (lane + at * LANES).astype(F32)
                out_lanes = pl.ds(pl.multiple_of(tile * LANES, LANES), LANES)
                for edge, (row, source) in enumerate(edges):
                    cosine = cosine_ref[row:row + 1, :]
                    inverse_square = 1.0 / (cosine * cosine)
                    sums = zero_terms()
                    for group in range(strip_count // SUB):
                        strips = slice(group * SUB, (group + 1) * SUB)

                        def load(shift, where):
                            ref, index = sources[source + shift]
                            return ref[index, strips, where]

                        z = load(0, here)
                        cols = shifted_columns(
                            z, load(0, before) * left_keep, load(0, after) * right_keep, lane
                        )
                        limits = [limits_ref[kind, strips, :] for kind in range(4)]
                        at_row = (row_start + row).astype(F32)
                        inside = (limits[0] <= at_row) & (limits[1] > at_row)
                        inside = inside & (col >= limits[2]) & (col < limits[3])
                        mask = jnp.where(inside, limits_ref[4, strips, :], 0.0)
                        shifts = tuple(load(shift, here) for shift in (-2, -1, 1, 2))
                        terms = stencil_terms(z, shifts, cols, inverse_square, mask)
                        sums = [total + term for total, term in zip(sums, terms)]
                    for moment in range(MOMENTS):
                        spot = moment * EDGE_ROWS + edge
                        out_ref[part, spot:spot + 1, out_lanes] = jnp.sum(sums[moment], axis=0, keepdims=True)
                return carry

            lax.fori_loop(0, quarter, column_tile, 0)


def edge_moments(limits, cosine, above, top, inner, bottom, below, order):
    pair, strip_count, col_count = top.shape
    out = jax.ShapeDtypeStruct((2, -(-MOMENTS * EDGE_ROWS // SUB) * SUB, col_count // 4), F32)
    vmem = pl.BlockSpec(memory_space=pltpu.VMEM)
    return pl.pallas_call(
        edge_kernel,
        out_shape=(out, out, jax.ShapeDtypeStruct((SUB, LANES), F32)),
        in_specs=[vmem] * 7 + [pl.BlockSpec(memory_space=pl.ANY)],
        out_specs=(vmem, vmem, vmem),
        compiler_params=pltpu.CompilerParams(vmem_limit_bytes=VMEM_BYTES),
        cost_estimate=SMALL_COST,
        name="moments_edge",
    )(limits, cosine, above, top, inner, bottom, below, order)


def finish_kernel(pieces, cosine_ref, mine_ref, edge_mine_ref, edge_core_ref, edge_far_ref, *refs):
    far_refs, core_refs = refs[:len(pieces)], refs[len(pieces):-2]
    mean_ref, covariance_ref = refs[-2:]
    row_block, width = mean_ref.shape
    share = MOMENTS // len(core_refs)
    sub = lax.broadcasted_iota(jnp.int32, (SUB, LANES), 0)
    for first_row, far_ref in zip(pieces, far_refs):
        for tile_row in range(first_row, first_row + far_ref.shape[1], SUB):
            rows = slice(tile_row, tile_row + SUB)
            far_rows = slice(tile_row - first_row, tile_row - first_row + SUB)
            cosine = cosine_ref[rows, :]
            scales = (1.0, 1.0 / (12.0 * cosine), 1.0 / 12.0, 1.0 / 12.0)
            spots = {0: ((0, 0), (1, 1)), row_block - SUB: ((SUB - 2, 2), (SUB - 1, 3))}.get(tile_row, ())
            for tile in range(width // LANES):
                lanes = slice(tile * LANES, (tile + 1) * LANES)

                def total(moment):
                    near = core_refs[moment // share][moment % share, rows, lanes]
                    value = (mine_ref[moment, rows, lanes] + near) + far_ref[moment, far_rows, lanes]
                    for at, edge in spots:
                        spot = moment * EDGE_ROWS + edge
                        spot = slice(spot, spot + 1)
                        line = (edge_mine_ref[1, spot, lanes] + edge_core_ref[1, spot, lanes]) + edge_far_ref[spot, lanes]
                        value = jnp.where(sub == at, line, value)
                    return value

                inverse = 144.0 / jnp.maximum(144.0 * total(0), 1.0)
                means = [total(1 + first) * inverse * scales[first] for first in range(FEATURES)]
                mean_ref[rows, lanes] = means[0]
                entry = 0
                for first in range(FEATURES):
                    for second in range(first, FEATURES):
                        scale = scales[first] * scales[second]
                        covariance_ref[entry, rows, lanes] = (
                            total(5 + entry) * inverse * scale - means[first] * means[second]
                        )
                        entry += 1


def finish(pieces, cosine, mine, edge_mine, edge_core, edge_far, far, core):
    moments, row_block, width = mine.shape
    vmem = pl.BlockSpec(memory_space=pltpu.VMEM)
    entries = FEATURES * (FEATURES + 1) // 2
    return pl.pallas_call(
        functools.partial(finish_kernel, pieces),
        out_shape=(
            jax.ShapeDtypeStruct((row_block, width), F32),
            jax.ShapeDtypeStruct((entries, row_block, width), F32),
        ),
        in_specs=[vmem] * (5 + len(far) + len(core)),
        out_specs=(vmem, vmem),
        compiler_params=pltpu.CompilerParams(vmem_limit_bytes=VMEM_BYTES),
        cost_estimate=SMALL_COST,
        name="finish",
    )(cosine, mine, edge_mine, edge_core, edge_far, *far, *core)


def exchange(value, distance):
    count = lax.axis_size("acq")
    return lax.ppermute(value, "acq", [(source, source ^ distance) for source in range(count)])


def local(strips, strip_quality, valid_ranges):
    strip_count, row_block, col_count = strips.shape
    tile_count = lax.axis_size("tile")
    ranges = valid_ranges.T
    piece_rows = row_block // 2
    pieces = tuple(range(0, row_block, piece_rows))

    top, bottom, inner, cosine, limits = halo_rows(strip_quality, ranges, strips)
    forward = [(i, i + 1) for i in range(tile_count - 1)]
    backward = [(target, source) for source, target in forward]
    above = lax.ppermute(bottom, "tile", forward)
    below = lax.ppermute(top, "tile", backward)

    def compute(order, remote, first_row, row_count, count):
        return moments_of(strip_quality, ranges, cosine, strips, order, remote, first_row, row_count, count)

    mine, other, token = compute((top, top), True, pieces[0], piece_rows, 1)
    far = [exchange(mine + exchange(other, 1), 2)]
    edge_mine, edge_other, token = edge_moments(limits, cosine, above, top, inner, bottom, below, token)
    edge_core = exchange(edge_other, 1)
    edge_far = exchange(edge_mine[0] + edge_core[0], 2)
    mine, other, token = compute((token, token), True, pieces[1], piece_rows, 1)
    far.append(exchange(mine + exchange(other, 1), 2))
    mine, *other, token = compute((token, token), False, 0, row_block, 3)
    core = [exchange(piece, 1) for piece in other]
    return finish(pieces, cosine, mine, edge_mine, edge_core, edge_far, far, core)


def solution(mesh):
    return jax.shard_map(
        local,
        mesh=mesh,
        in_specs=(P("acq", "tile", None), P("acq"), P("acq", None)),
        out_specs=(P("tile", "acq"), P(None, "tile", "acq")),
        check_vma=False,
    )
```

time: 101 us -> 79.3 us (0.79)
  waiting for transfers between devices: 18 us -> 5.24 us
  Pallas kernels: 64.2 us -> 57.8 us
  local copies, waits for them, and re-layouts: 4.87 us -> 1.92 us
    ppermute x1, waiting for transfers between devices: 13.7 us -> 3.05 us  [local(): above = lax.ppermute(bottom, 'tile', forward)]
    pallas_call x3, Pallas kernels: 52.9 us -> 45.8 us  [moments_of(): pl.pallas_call(functools.partial(moment_kernel, remote=remote, first_row=...]
    broadcast_in_dim x3 -> x0, local copies, waits for them, and re-layouts: 2.21 us -> none  [the longest x1 0.8 us: local(): jnp.broadcast_to(strip_quality[:, None], (strip_count, LANES))]
    ppermute x7 -> x9, waiting for transfers between devices: 4.34 us -> 2.19 us  [exchange(): lax.ppermute(value, 'acq', [(source, source ^ distance) for source in ran...]
    unnamed x23 -> x24, local copies, waits for them, and re-layouts: 2.66 us -> 1.92 us
    ppermute x7 -> x9, starting transfers between devices: 4.56 us -> 5 us  [exchange(): lax.ppermute(value, 'acq', [(source, source ^ distance) for source in ran...]
  transfers between devices with their start and end apart: 9 -> 11, of which waited for: 3 -> 4; matrix products, arithmetic and copies ran while one was open for 3% -> 2% of each run, Pallas kernels for 47% -> 65%
where the time goes in v2:
time: 79.3 us; the launch traced here: 77.8 us
  Pallas kernels  57.8 us (73%)
  starting transfers between devices  10.8 us (14%)
  waiting for transfers between devices  5.24 us (7%)
  local copies, waits for them, and re-layouts  1.92 us (2%)
  other arithmetic  1.18 us (1%)
    pallas_call x3, Pallas kernels, moments_of(): pl.pallas_call(functools.partial(moment_kernel, remote=remote, first_row=...  45.8 us
    ppermute x9, starting transfers between devices, exchange(): lax.ppermute(value, 'acq', [(source, source ^ distance) for source in ran...  5 us
    pallas_call x1, Pallas kernels, edge_moments(): pl.pallas_call(edge_kernel, out_shape=(out, out, jax.ShapeDtypeStruct((SU...  4.92 us
    pallas_call x1, Pallas kernels, halo_rows(): pl.pallas_call(halo_kernel, out_shape=(pair, pair, inner, cosine, limits)...  4.05 us
    ppermute x1, starting transfers between devices, local(): above = lax.ppermute(bottom, 'tile', forward)  3.43 us
    ppermute x1, waiting for transfers between devices, local(): above = lax.ppermute(bottom, 'tile', forward)  3.05 us
    pallas_call x1, Pallas kernels, finish(): pl.pallas_call(functools.partial(finish_kernel, pieces), out_shape=(jax.S...  3.02 us
    ppermute x1, starting transfers between devices, local(): below = lax.ppermute(top, 'tile', backward)  2.41 us
  transfers between devices with their start and end apart: 11, of which 4 were waited for; matrix products, arithmetic and copies ran while one was open for 2% of the time, Pallas kernels for 65%

profile of v2, /device:TPU:12, one launch (start us, length us, event | category | flops | bytes accessed | tf_op | source)
XLA Modules:
  0.0 77.8 jit_solution(12393049382342472743)
XLA Ops:
  0.6 4.1 %halo_rows.1 = (f32[2,48,1024]{2,1,0:T(8,128)}, f32[2,48,1024]{2,1,0:T(8,128)}, f32[4,48,1024]{2,1,0:T(8,128)}, f32[64,128]{1,0:T(8,128)}, f32[5,48,128]{2,1,0:T(8,128)}) custom-call(f32[48]{0:T(128)} %quality_ref.7, s32[4,48]{1,0:T(4,128)} %bitcast.3, f32[48,64,1024]{2,1,0:T(8,128)} %strips_ref.7), custom_call_target="tpu_custom_call" | custom-call | flops 1 | bytes 1 | tf_op jit(solution)/shard_map/halo_rows/pallas_call | solution.py:113
  4.7 3.4 %collective-permute-start = (f32[2,48,1024]{2,1,0:T(8,128)}, f32[2,48,1024]{2,1,0:T(8,128)S(1)}, u32[]{:S(2)}, u32[]{:S(2)}) collective-permute-start(f32[2,48,1024]{2,1,0:T(8,128)} %get-tuple-element.22.bottom_ref), channel_id=1, source_target_pairs={{0,4},{4,8},{8,12},{12,16},{16,20},{20,24},{24,28},{1,5},{5,9},{9,... | collective-permute-start | bytes 1179656 | tf_op jit(solution)/shard_map/ppermute | solution.py:517
  8.1 2.4 %collective-permute-start.1 = (f32[2,48,1024]{2,1,0:T(8,128)}, f32[2,48,1024]{2,1,0:T(8,128)S(1)}, u32[]{:S(2)}, u32[]{:S(2)}) collective-permute-start(f32[2,48,1024]{2,1,0:T(8,128)} %get-tuple-element.23.first_order_ref.second_order_ref.top_ref), channel_id=1, source_target_pairs={{4,0},{8,4},{12,8},{16,12},{20,16},{24,20},{28,24},{5,1},{9,5},{13... | collective-permute-start | bytes 1179656 | tf_op jit(solution)/shard_map/ppermute | solution.py:518
  10.5 12.4 %moments_remote.2 = (f32[15,32,256]{2,1,0:T(8,128)}, f32[15,32,256]{2,1,0:T(8,128)}, f32[8,128]{1,0:T(8,128)}) custom-call(f32[48]{0:T(128)} %quality_ref.7, s32[4,48]{1,0:T(4,128)} %bitcast.4, f32[64,128]{1,0:T(8,128)} %get-tuple-element.20.cosine_ref, f32[48,64,1024]{2,1,0:T(8,128)} %strips_ref.7, ...), custom_call_target="tpu_custom_call" | custom-call | flops 1 | bytes 1 | tf_op jit(solution)/shard_map/moments_remote/pallas_call | solution.py:344
  22.9 0.0 copy-start.2
  22.9 0.1 collective-permute-start.4
  23.0 3.0 %collective-permute-done.above_ref = f32[2,48,1024]{2,1,0:T(8,128)S(1)} collective-permute-done((f32[2,48,1024]{2,1,0:T(8,128)}, f32[2,48,1024]{2,1,0:T(8,128)S(1)}, u32[]{:S(2)}, u32[]{:S(2)}) %collective-permute-start) | collective-permute-done | bytes 393248 | tf_op jit(solution)/shard_map/ppermute | solution.py:517
  26.1 0.0 copy-start.3
  26.1 0.0 collective-permute-done.1.below_ref
  26.1 0.0 copy-start.4
  26.1 0.8 copy-done.3
  26.8 0.1 copy-done.4
  27.0 4.9 %moments_edge.1 = (f32[2,64,256]{2,1,0:T(8,128)}, f32[2,64,256]{2,1,0:T(8,128)}, f32[8,128]{1,0:T(8,128)}) custom-call(f32[5,48,128]{2,1,0:T(8,128)} %get-tuple-element.21.limits_ref, f32[64,128]{1,0:T(8,128)} %get-tuple-element.20.cosine_ref, f32[2,48,1024]{2,1,0:T(8,128)} %copy-done.3, ...), custom_call_target="tpu_custom_call" | custom-call | flops 1 | bytes 1 | tf_op jit(solution)/shard_map/moments_edge/pallas_call | solution.py:434
  31.9 0.0 copy-start.11
  31.9 0.0 copy-start.8
  31.9 12.5 %moments_remote.3 = (f32[15,32,256]{2,1,0:T(8,128)}, f32[15,32,256]{2,1,0:T(8,128)}, f32[8,128]{1,0:T(8,128)}) custom-call(f32[48]{0:T(128)} %quality_ref.7, s32[4,48]{1,0:T(4,128)} %bitcast.5, f32[64,128]{1,0:T(8,128)} %get-tuple-element.20.cosine_ref, f32[48,64,1024]{2,1,0:T(8,128)} %strips_ref.7, ...), custom_call_target="tpu_custom_call" | custom-call | flops 1 | bytes 1 | tf_op jit(solution)/shard_map/moments_remote/pallas_call | solution.py:344
  44.4 0.1 collective-permute-start.6
  44.5 0.0 copy-done.11
  44.5 0.5 collective-permute-start.2
  45.0 0.0 collective-permute-done.4
  45.0 0.0 copy-done.2
  45.0 0.1 add.14
  45.0 1.6 %collective-permute-start.5 = (f32[15,32,256]{2,1,0:T(8,128)S(1)}, f32[15,32,256]{2,1,0:T(8,128)S(1)}, u32[]{:S(2)}, u32[]{:S(2)}) collective-permute-start(f32[15,32,256]{2,1,0:T(8,128)S(1)} %add.14), channel_id=1, source_target_pairs={{0,2},{1,3},{2,0},{3,1},{4,6},{5,7},{6,4},{7,5},{8,10},{9,11},{10,... | collective-permute-start | bytes 1474568 | tf_op jit(solution)/shard_map/ppermute | solution.py:504
  46.6 0.0 collective-permute-done.6
  46.6 1.1 %add.15 = f32[15,32,256]{2,1,0:T(8,128)S(1)} add(f32[15,32,256]{2,1,0:T(8,128)} %get-tuple-element.33, f32[15,32,256]{2,1,0:T(8,128)S(1)} %collective-permute-done.6) | non-fusion elementwise | flops 122880 | bytes 1474560 | tf_op jit(solution)/shard_map/add | solution.py:529
  47.7 1.5 %collective-permute-start.7 = (f32[15,32,256]{2,1,0:T(8,128)S(1)}, f32[15,32,256]{2,1,0:T(8,128)S(1)}, u32[]{:S(2)}, u32[]{:S(2)}) collective-permute-start(f32[15,32,256]{2,1,0:T(8,128)S(1)} %add.15), channel_id=1, source_target_pairs={{0,2},{1,3},{2,0},{3,1},{4,6},{5,7},{6,4},{7,5},{8,10},{9,11},{10,... | collective-permute-start | bytes 1474568 | tf_op jit(solution)/shard_map/ppermute | solution.py:504
  49.2 0.0 collective-permute-done.2.edge_core_ref
  49.2 0.0 copy-start.9
  49.2 0.0 copy-done.8
  49.2 0.7 collective-permute-start.3
  49.9 20.9 %moments_own.1 = (f32[15,64,256]{2,1,0:T(8,128)}, f32[5,64,256]{2,1,0:T(8,128)}, f32[5,64,256]{2,1,0:T(8,128)}, f32[5,64,256]{2,1,0:T(8,128)}, f32[8,128]{1,0:T(8,128)}) custom-call(f32[48]{0:T(128)} %quality_ref.7, s32[4,48]{1,0:T(4,128)} %bitcast.6, f32[64,128]{1,0:T(8,128)} %get-tuple-element.20.cosine_ref, f32[48,64,1024]{2,1,0:T(8,128)} %strips_ref.7, ...), custom_call_target="tpu_custom_call" | custom-call | flops 1 | bytes 1 | tf_op jit(solution)/shard_map/moments_own/pallas_call | solution.py:344
  70.8 0.1 collective-permute-start.8
  70.9 0.5 collective-permute-start.9
  71.4 0.0 collective-permute-done.3.edge_far_ref
  71.4 0.0 copy-start.10
  71.4 0.1 collective-permute-start.10
  71.5 1.2 %collective-permute-done.8.refs_2_ = f32[5,64,256]{2,1,0:T(8,128)S(1)} collective-permute-done((f32[5,64,256]{2,1,0:T(8,128)}, f32[5,64,256]{2,1,0:T(8,128)S(1)}, u32[]{:S(2)}, u32[]{:S(2)}) %collective-permute-start.8) | collective-permute-done | bytes 327712 | tf_op jit(solution)/shard_map/ppermute | solution.py:504
  72.7 0.0 copy-start.5
  72.7 0.5 collective-permute-done.9.refs_3_
  73.2 0.0 copy-start.6
  73.2 0.5 collective-permute-done.10.refs_4_
  73.7 0.0 copy-start.7
  73.7 0.0 collective-permute-done.5.refs_0_
  73.7 0.0 copy-start
  73.7 0.0 collective-permute-done.7.refs_1_
  73.7 0.0 copy-start.1
  73.7 0.0 copy-done.9
  73.7 0.0 copy-done.10
  73.7 0.0 copy-done.5
  73.7 0.2 copy-done.6
  74.0 0.5 copy-done.7
  74.4 0.2 copy-done
  74.6 0.2 copy-done.1
  74.7 3.0 %finish.1 = (f32[64,256]{1,0:T(8,128)}, f32[10,64,256]{2,1,0:T(8,128)}) custom-call(f32[64,128]{1,0:T(8,128)} %get-tuple-element.20.cosine_ref, f32[15,64,256]{2,1,0:T(8,128)} %get-tuple-element.28.mine_ref, f32[2,64,256]{2,1,0:T(8,128)} %get-tuple-element.29.edge_mine_ref, f32[2,64,256]{2,1,0:T(8,128)} %copy-done.9, f32[64,256]{1,0:T(8,128)} %copy-done.10, ...), custom_call_target="tpu_custom_call" | custom-call | flops 1 | bytes 1 | tf_op jit(solution)/shard_map/finish/pallas_call | solution.py:488
  (1 shorter events, 0.0 us)
Async XLA Ops:
  4.7 21.4 %collective-permute-start = (f32[2,48,1024]{2,1,0:T(8,128)}, f32[2,48,1024]{2,1,0:T(8,128)S(1)}, u32[]{:S(2)}, u32[]{:S(2)}) collective-permute-start(f32[2,48,1024]{2,1,0:T(8,128)} %get-tuple-element.22.bottom_ref), channel_id=1, source_target_pairs={{0,4},{4,8},{8,12},{12,16},{16,20},{20,24},{24,28},{1,5},{5,9},{9,... | collective-permute-start | bytes 1179656 | tf_op jit(solution)/shard_map/ppermute | solution.py:517
  8.1 18.0 %collective-permute-start.1 = (f32[2,48,1024]{2,1,0:T(8,128)}, f32[2,48,1024]{2,1,0:T(8,128)S(1)}, u32[]{:S(2)}, u32[]{:S(2)}) collective-permute-start(f32[2,48,1024]{2,1,0:T(8,128)} %get-tuple-element.23.first_order_ref.second_order_ref.top_ref), channel_id=1, source_target_pairs={{4,0},{8,4},{12,8},{16,12},{20,16},{24,20},{28,24},{5,1},{9,5},{13... | collective-permute-start | bytes 1179656 | tf_op jit(solution)/shard_map/ppermute | solution.py:518
  22.9 22.0 %copy-start.2 = (f32[15,32,256]{2,1,0:T(8,128)S(1)}, f32[15,32,256]{2,1,0:T(8,128)}, u32[]{:S(2)}) copy-start(f32[15,32,256]{2,1,0:T(8,128)} %get-tuple-element.31) | copy-start | bytes 1474564
  22.9 22.0 %collective-permute-start.4 = (f32[15,32,256]{2,1,0:T(8,128)}, f32[15,32,256]{2,1,0:T(8,128)S(1)}, u32[]{:S(2)}, u32[]{:S(2)}) collective-permute-start(f32[15,32,256]{2,1,0:T(8,128)} %get-tuple-element.32), channel_id=1, source_target_pairs={{0,1},{1,0},{2,3},{3,2},{4,5},{5,4},{6,7},{7,6},{8,9},{9,8},{10,11... | collective-permute-start | bytes 1474568 | tf_op jit(solution)/shard_map/ppermute | solution.py:504
  26.1 0.8 copy-start.3
  26.1 0.9 %copy-start.4 = (f32[2,48,1024]{2,1,0:T(8,128)}, f32[2,48,1024]{2,1,0:T(8,128)S(1)}, u32[]{:S(2)}) copy-start(f32[2,48,1024]{2,1,0:T(8,128)S(1)} %collective-permute-done.1.below_ref) | copy-start | bytes 1179652
  31.9 12.6 %copy-start.11 = (f32[2,64,256]{2,1,0:T(8,128)S(1)}, f32[2,64,256]{2,1,0:T(8,128)}, u32[]{:S(2)}) copy-start(f32[2,64,256]{2,1,0:T(8,128)} %get-tuple-element.30) | copy-start | bytes 393220
  31.9 17.3 %copy-start.8 = (f32[2,64,256]{2,1,0:T(8,128)S(1)}, f32[2,64,256]{2,1,0:T(8,128)}, u32[]{:S(2)}) copy-start(f32[2,64,256]{2,1,0:T(8,128)} %get-tuple-element.29.edge_mine_ref) | copy-start | bytes 393220
  44.4 2.2 %collective-permute-start.6 = (f32[15,32,256]{2,1,0:T(8,128)}, f32[15,32,256]{2,1,0:T(8,128)S(1)}, u32[]{:S(2)}, u32[]{:S(2)}) collective-permute-start(f32[15,32,256]{2,1,0:T(8,128)} %get-tuple-element.34), channel_id=1, source_target_pairs={{0,1},{1,0},{2,3},{3,2},{4,5},{5,4},{6,7},{7,6},{8,9},{9,8},{10,11... | collective-permute-start | bytes 1474568 | tf_op jit(solution)/shard_map/ppermute | solution.py:504
  44.5 4.7 %collective-permute-start.2 = (f32[2,64,256]{2,1,0:T(8,128)S(1)}, f32[2,64,256]{2,1,0:T(8,128)S(1)}, u32[]{:S(2)}, u32[]{:S(2)}) collective-permute-start(f32[2,64,256]{2,1,0:T(8,128)S(1)} %copy-done.11), channel_id=1, source_target_pairs={{0,1},{1,0},{2,3},{3,2},{4,5},{5,4},{6,7},{7,6},{8,9},{9,8},{10,11... | collective-permute-start | bytes 393224 | tf_op jit(solution)/shard_map/ppermute | solution.py:504
  45.0 28.6 %collective-permute-start.5 = (f32[15,32,256]{2,1,0:T(8,128)S(1)}, f32[15,32,256]{2,1,0:T(8,128)S(1)}, u32[]{:S(2)}, u32[]{:S(2)}) collective-permute-start(f32[15,32,256]{2,1,0:T(8,128)S(1)} %add.14), channel_id=1, source_target_pairs={{0,2},{1,3},{2,0},{3,1},{4,6},{5,7},{6,4},{7,5},{8,10},{9,11},{10,... | collective-permute-start | bytes 1474568 | tf_op jit(solution)/shard_map/ppermute | solution.py:504
  47.7 26.0 %collective-permute-start.7 = (f32[15,32,256]{2,1,0:T(8,128)S(1)}, f32[15,32,256]{2,1,0:T(8,128)S(1)}, u32[]{:S(2)}, u32[]{:S(2)}) collective-permute-start(f32[15,32,256]{2,1,0:T(8,128)S(1)} %add.15), channel_id=1, source_target_pairs={{0,2},{1,3},{2,0},{3,1},{4,6},{5,7},{6,4},{7,5},{8,10},{9,11},{10,... | collective-permute-start | bytes 1474568 | tf_op jit(solution)/shard_map/ppermute | solution.py:504
  49.2 24.5 %copy-start.9 = (f32[2,64,256]{2,1,0:T(8,128)}, f32[2,64,256]{2,1,0:T(8,128)S(1)}, u32[]{:S(2)}) copy-start(f32[2,64,256]{2,1,0:T(8,128)S(1)} %collective-permute-done.2.edge_core_ref) | copy-start | bytes 393220
  49.2 22.2 %collective-permute-start.3 = (f32[64,256]{1,0:T(8,128)S(1)}, f32[64,256]{1,0:T(8,128)S(1)}, u32[]{:S(2)}, u32[]{:S(2)}) collective-permute-start(f32[64,256]{1,0:T(8,128)S(1)} %fusion), channel_id=1, source_target_pairs={{0,2},{1,3},{2,0},{3,1},{4,6},{5,7},{6,4},{7,5},{8,10},{9,11},{10,... | collective-permute-start | bytes 196616 | tf_op jit(solution)/shard_map/ppermute | solution.py:504
  70.8 1.9 %collective-permute-start.8 = (f32[5,64,256]{2,1,0:T(8,128)}, f32[5,64,256]{2,1,0:T(8,128)S(1)}, u32[]{:S(2)}, u32[]{:S(2)}) collective-permute-start(f32[5,64,256]{2,1,0:T(8,128)} %get-tuple-element.35), channel_id=1, source_target_pairs={{0,1},{1,0},{2,3},{3,2},{4,5},{5,4},{6,7},{7,6},{8,9},{9,8},{10,11... | collective-permute-start | bytes 983048 | tf_op jit(solution)/shard_map/ppermute | solution.py:504
  70.9 2.3 %collective-permute-start.9 = (f32[5,64,256]{2,1,0:T(8,128)}, f32[5,64,256]{2,1,0:T(8,128)S(1)}, u32[]{:S(2)}, u32[]{:S(2)}) collective-permute-start(f32[5,64,256]{2,1,0:T(8,128)} %get-tuple-element.36), channel_id=1, source_target_pairs={{0,1},{1,0},{2,3},{3,2},{4,5},{5,4},{6,7},{7,6},{8,9},{9,8},{10,11... | collective-permute-start | bytes 983048 | tf_op jit(solution)/shard_map/ppermute | solution.py:504
  71.4 2.3 %copy-start.10 = (f32[64,256]{1,0:T(8,128)}, f32[64,256]{1,0:T(8,128)S(1)}, u32[]{:S(2)}) copy-start(f32[64,256]{1,0:T(8,128)S(1)} %collective-permute-done.3.edge_far_ref) | copy-start | bytes 196612
  71.4 2.3 %collective-permute-start.10 = (f32[5,64,256]{2,1,0:T(8,128)}, f32[5,64,256]{2,1,0:T(8,128)S(1)}, u32[]{:S(2)}, u32[]{:S(2)}) collective-permute-start(f32[5,64,256]{2,1,0:T(8,128)} %get-tuple-element.37), channel_id=1, source_target_pairs={{0,1},{1,0},{2,3},{3,2},{4,5},{5,4},{6,7},{7,6},{8,9},{9,8},{10,11... | collective-permute-start | bytes 983048 | tf_op jit(solution)/shard_map/ppermute | solution.py:504
  72.7 1.0 %copy-start.5 = (f32[5,64,256]{2,1,0:T(8,128)}, f32[5,64,256]{2,1,0:T(8,128)S(1)}, u32[]{:S(2)}) copy-start(f32[5,64,256]{2,1,0:T(8,128)S(1)} %collective-permute-done.8.refs_2_) | copy-start | bytes 983044
  73.2 0.8 copy-start.6
  73.7 0.7 copy-start.7
  73.7 0.9 %copy-start = (f32[15,32,256]{2,1,0:T(8,128)}, f32[15,32,256]{2,1,0:T(8,128)S(1)}, u32[]{:S(2)}) copy-start(f32[15,32,256]{2,1,0:T(8,128)S(1)} %collective-permute-done.5.refs_0_) | copy-start | bytes 1474564
  73.7 1.1 %copy-start.1 = (f32[15,32,256]{2,1,0:T(8,128)}, f32[15,32,256]{2,1,0:T(8,128)S(1)}, u32[]{:S(2)}) copy-start(f32[15,32,256]{2,1,0:T(8,128)S(1)} %collective-permute-done.7.refs_1_) | copy-start | bytes 1474564

commit v3 on v2

--- a/solution.py
+++ b/solution.py
@@ -11,9 +11,11 @@
 SUB = 8
 LANES = 128
 EDGE_ROWS = 4
-VMEM_BYTES = 56 * 1024 * 1024
+VMEM_BYTES = 50 * 1024 * 1024
+SMALL_VMEM_BYTES = 50 * 1024 * 1024
 F32 = jnp.float32
 LOAD_PARTS = 4
+PIECES = 3
 SMALL_COST = pl.CostEstimate(flops=1, bytes_accessed=1, transcendentals=0)
 
 
@@ -54,9 +56,9 @@
 
 
 def halo_kernel(
-    quality_ref, ranges_ref, strips_ref, top_ref, bottom_ref, inner_ref, cosine_ref, limits_ref,
-    first_ref, last_ref, sems,
+    strips_ref, top_ref, bottom_ref, inner_ref, cosine_ref, token_ref, first_ref, last_ref, sems
 ):
+    token_ref[...] = jnp.zeros((SUB, LANES), F32)
     strip_count, row_block, col_count = strips_ref.shape
     copies = []
     for tile in range(col_count // LANES):
@@ -76,15 +78,6 @@
         latitude = -1.0 + 2.0 * (row.astype(F32) + 0.5) / total_rows
         cosine_ref[tile * SUB:(tile + 1) * SUB, :] = jnp.cos(latitude)
 
-    def spread(strip, carry):
-        here = pl.ds(strip, 1)
-        for kind in range(4):
-            value = ranges_ref[kind, strip].astype(F32)
-            limits_ref[kind, here, :] = jnp.full((1, LANES), value, F32)
-        limits_ref[4, here, :] = jnp.full((1, LANES), quality_ref[strip], F32)
-        return carry
-
-    lax.fori_loop(0, strip_count, spread, 0)
     first_rows = first_ref.reshape(col_count // LANES, strip_count * SUB, LANES)
     last_rows = last_ref.reshape(col_count // LANES, strip_count * SUB, LANES)
     for tile in range(col_count // LANES):
@@ -101,29 +94,28 @@
                 inner_ref[2 + row, strips, lanes] = last_rows[tile, pl.ds(at + 4 + row, SUB, stride=SUB), :]
 
 
-def halo_rows(quality, ranges, strips):
+def halo_rows(strips):
     strip_count, row_block, col_count = strips.shape
     tiles = col_count // LANES
     pair = jax.ShapeDtypeStruct((2, strip_count, col_count), F32)
     inner = jax.ShapeDtypeStruct((4, strip_count, col_count), F32)
     cosine = jax.ShapeDtypeStruct((row_block, LANES), F32)
-    limits = jax.ShapeDtypeStruct((5, strip_count, LANES), F32)
     vmem = pl.BlockSpec(memory_space=pltpu.VMEM)
-    smem = pl.BlockSpec(memory_space=pltpu.SMEM)
+    hbm = pl.BlockSpec(memory_space=pltpu.HBM)
     return pl.pallas_call(
         halo_kernel,
-        out_shape=(pair, pair, inner, cosine, limits),
-        in_specs=[smem, smem, pl.BlockSpec(memory_space=pl.ANY)],
+        out_shape=(pair, pair, inner, cosine, jax.ShapeDtypeStruct((SUB, LANES), F32)),
+        in_specs=[hbm],
         out_specs=(vmem,) * 5,
         scratch_shapes=[
             pltpu.VMEM((tiles, strip_count, SUB, LANES), F32),
             pltpu.VMEM((tiles, strip_count, SUB, LANES), F32),
             pltpu.SemaphoreType.DMA((2, tiles)),
         ],
-        compiler_params=pltpu.CompilerParams(vmem_limit_bytes=VMEM_BYTES),
+        compiler_params=pltpu.CompilerParams(vmem_limit_bytes=SMALL_VMEM_BYTES),
         cost_estimate=SMALL_COST,
         name="halo_rows",
-    )(quality, ranges, strips)
+    )(strips)
 
 
 def column_weights():
@@ -139,11 +131,23 @@
     return jnp.where(target < LANES, slope, second).astype(jnp.bfloat16)
 
 
-def moment_kernel(
-    quality_ref, ranges_ref, cosine_ref, strips_ref, first_order_ref, second_order_ref, mine_ref,
-    *refs, remote, first_row, row_count, pieces,
-):
+def moment_kernel(*refs, remote, first_row, row_count, pieces, spread):
+    if spread:
+        small_sems = refs[-1]
+        quality_ref, ranges_ref = refs[-3:-1]
+        small_copies = [
+            pltpu.make_async_copy(refs[kind], refs[kind - 3], small_sems.at[kind]) for kind in range(2)
+        ]
+        refs = refs[2:-3]
+    else:
+        limits_ref = refs[0]
+        refs = refs[1:]
+    cosine_ref, strips_ref, first_order_ref, second_order_ref, mine_ref = refs[:5]
+    refs = refs[5:]
     other_refs, token_ref = refs[:pieces], refs[pieces]
+    if spread:
+        limits_ref = refs[pieces + 1]
+        refs = refs[1:]
     elevation, high_part, low_part, row_mask, col_mask, weights, first_slot, second_slot, sems = refs[pieces + 1:]
     del first_order_ref, second_order_ref
     token_ref[...] = jnp.zeros((SUB, LANES), F32)
@@ -212,22 +216,38 @@
     for which in range(LOAD_PARTS):
         for step in range(3):
             start(initial + step, which)
+    if spread:
+        for copy in small_copies:
+            copy.start()
     blank(0)
     blank(half + 1)
 
     weights[...] = column_weights()
 
+    def spread_out(strip, carry):
+        here = pl.ds(strip, 1)
+        for kind in range(4):
+            value = ranges_ref[kind, strip].astype(F32)
+            limits_ref[kind, here, :] = jnp.full((1, LANES), value, F32)
+        limits_ref[4, here, :] = jnp.full((1, LANES), quality_ref[strip], F32)
+        return carry
+
+    if spread:
+        for copy in small_copies:
+            copy.wait()
+        lax.fori_loop(0, strip_count, spread_out, 0)
+
     def prepare(strip, carry):
-        quality = quality_ref[strip]
-        row_low, row_high = ranges_ref[0, strip], ranges_ref[1, strip]
-        col_low, col_high = ranges_ref[2, strip], ranges_ref[3, strip]
+        row_low, row_high, col_low, col_high, quality = (
+            limits_ref[kind, pl.ds(strip, 1), :] for kind in range(5)
+        )
         for tile in range(row_count // SUB):
-            row = lax.broadcasted_iota(jnp.int32, (SUB, LANES), 0) + (row_start + tile * SUB)
+            row = (lax.broadcasted_iota(jnp.int32, (SUB, LANES), 0) + (row_start + tile * SUB)).astype(F32)
             row_mask[strip, tile * SUB:(tile + 1) * SUB, :] = jnp.where(
                 (row >= row_low) & (row < row_high), quality, 0.0
             )
         for tile in range(half):
-            col = lax.broadcasted_iota(jnp.int32, (SUB, LANES), 1) + (base + tile) * LANES
+            col = (lax.broadcasted_iota(jnp.int32, (SUB, LANES), 1) + (base + tile) * LANES).astype(F32)
             col_mask[strip, tile] = jnp.where((col >= col_low) & (col < col_high), 1.0, 0.0)
         if low == first_row:
             for tile in range(half + 2):
@@ -330,22 +350,23 @@
     column_tile(1, later + 2, None, store_mine, slice(LANES, 2 * LANES))
 
 
-def moments_of(quality, ranges, cosine, strips, order, remote, first_row, row_count, pieces):
+def moments_of(limits, cosine, strips, order, remote, first_row, row_count, pieces):
+    spread = len(limits) == 2
     strip_count, row_block, col_count = strips.shape
     half = col_count // LANES // 2
     out = jax.ShapeDtypeStruct((MOMENTS, row_count, col_count // 4), F32)
     piece = jax.ShapeDtypeStruct((MOMENTS // pieces, row_count, col_count // 4), F32)
     token = jax.ShapeDtypeStruct((SUB, LANES), F32)
     vmem = pl.BlockSpec(memory_space=pltpu.VMEM)
-    smem = pl.BlockSpec(memory_space=pltpu.SMEM)
     anywhere = pl.BlockSpec(memory_space=pl.ANY)
+    lanes = jax.ShapeDtypeStruct((5, strip_count, LANES), F32)
     parts = pltpu.VMEM((strip_count, half + 2, row_count, LANES), jnp.bfloat16)
     slot = pltpu.VMEM((strip_count, row_count, 2 * LANES), F32)
     return pl.pallas_call(
-        functools.partial(moment_kernel, remote=remote, first_row=first_row, row_count=row_count, pieces=pieces),
-        out_shape=(out,) + (piece,) * pieces + (token,),
-        in_specs=[smem, smem, vmem, anywhere, anywhere, anywhere],
-        out_specs=(vmem,) * (pieces + 2),
+        functools.partial(moment_kernel, remote=remote, first_row=first_row, row_count=row_count, pieces=pieces, spread=spread),
+        out_shape=(out,) + (piece,) * pieces + (token,) + (lanes,) * spread,
+        in_specs=[anywhere] * 2 * spread + [vmem] * (2 - spread) + [anywhere, vmem, vmem],
+        out_specs=(vmem,) * (pieces + 2 + spread),
         scratch_shapes=[
             pltpu.VMEM((strip_count, half + 2, row_count + 2 * SUB, LANES), F32),
             parts,
@@ -356,18 +377,24 @@
             slot,
             slot,
             pltpu.SemaphoreType.DMA((half + 2, LOAD_PARTS)),
-        ],
+        ]
+        + [
+            pltpu.SMEM((strip_count,), F32),
+            pltpu.SMEM((4, strip_count), jnp.int32),
+            pltpu.SemaphoreType.DMA((2,)),
+        ]
+        * spread,
         compiler_params=pltpu.CompilerParams(vmem_limit_bytes=VMEM_BYTES),
         cost_estimate=SMALL_COST,
         name="moments_remote" if remote else "moments_own",
-    )(quality, ranges, cosine, strips, *order)
+    )(*limits, cosine, strips, *order)
 
 
 def edge_kernel(
     limits_ref, cosine_ref, above_ref, top_ref, inner_ref, bottom_ref, below_ref,
-    order_ref, mine_ref, other_ref, token_ref,
+    first_order_ref, second_order_ref, mine_ref, other_ref, token_ref,
 ):
-    del order_ref
+    del first_order_ref, second_order_ref
     token_ref[...] = jnp.zeros((SUB, LANES), F32)
     pair, strip_count, col_count = top_ref.shape
     row_block = cosine_ref.shape[0]
@@ -427,31 +454,61 @@
             lax.fori_loop(0, quarter, column_tile, 0)
 
 
-def edge_moments(limits, cosine, above, top, inner, bottom, below, order):
+def edge_moments(limits, cosine, above, top, inner, bottom, below, *order):
     pair, strip_count, col_count = top.shape
     out = jax.ShapeDtypeStruct((2, -(-MOMENTS * EDGE_ROWS // SUB) * SUB, col_count // 4), F32)
     vmem = pl.BlockSpec(memory_space=pltpu.VMEM)
     return pl.pallas_call(
         edge_kernel,
         out_shape=(out, out, jax.ShapeDtypeStruct((SUB, LANES), F32)),
-        in_specs=[vmem] * 7 + [pl.BlockSpec(memory_space=pl.ANY)],
+        in_specs=[vmem] * 9,
         out_specs=(vmem, vmem, vmem),
-        compiler_params=pltpu.CompilerParams(vmem_limit_bytes=VMEM_BYTES),
+        compiler_params=pltpu.CompilerParams(vmem_limit_bytes=SMALL_VMEM_BYTES),
         cost_estimate=SMALL_COST,
         name="moments_edge",
-    )(limits, cosine, above, top, inner, bottom, below, order)
-
-
-def finish_kernel(pieces, cosine_ref, mine_ref, edge_mine_ref, edge_core_ref, edge_far_ref, *refs):
+    )(limits, cosine, above, top, inner, bottom, below, *order)
+
+
+def combine_kernel(mine_ref, *refs, pieces, edges):
+    near_refs, rest = refs[:pieces], refs[pieces:]
+    out_ref, token_ref = rest[-2:]
+    token_ref[...] = jnp.zeros((SUB, LANES), F32)
+    share, row_count, width = near_refs[0].shape
+    for piece, near_ref in enumerate(near_refs):
+        for moment in range(share):
+            at = piece * share + moment
+            out_ref[at * row_count:(at + 1) * row_count, :] = mine_ref[at] + near_ref[moment]
+    if edges:
+        edge_mine_ref, edge_core_ref = rest[:2]
+        out_ref[pieces * share * row_count:, :] = edge_mine_ref[0] + edge_core_ref[0]
+
+
+def combine(mine, near, edges, order):
+    moments, row_count, width = mine.shape
+    rows = moments * row_count + sum(edge.shape[1] for edge in edges[:1])
+    vmem = pl.BlockSpec(memory_space=pltpu.VMEM)
+    return pl.pallas_call(
+        functools.partial(combine_kernel, pieces=len(near), edges=bool(edges)),
+        out_shape=(jax.ShapeDtypeStruct((rows, width), F32), jax.ShapeDtypeStruct((SUB, LANES), F32)),
+        in_specs=[vmem] * (1 + len(near) + len(edges) + len(order)),
+        out_specs=(vmem, vmem),
+        compiler_params=pltpu.CompilerParams(vmem_limit_bytes=SMALL_VMEM_BYTES),
+        cost_estimate=SMALL_COST,
+        name="combine",
+    )(mine, *near, *edges, *order)
+
+
+def finish_kernel(pieces, cosine_ref, mine_ref, edge_mine_ref, edge_core_ref, *refs):
     far_refs, core_refs = refs[:len(pieces)], refs[len(pieces):-2]
     mean_ref, covariance_ref = refs[-2:]
     row_block, width = mean_ref.shape
     share = MOMENTS // len(core_refs)
     sub = lax.broadcasted_iota(jnp.int32, (SUB, LANES), 0)
+    piece_rows = row_block // len(pieces)
+    edge_start = MOMENTS * piece_rows
     for first_row, far_ref in zip(pieces, far_refs):
-        for tile_row in range(first_row, first_row + far_ref.shape[1], SUB):
+        for tile_row in range(first_row, first_row + piece_rows, SUB):
             rows = slice(tile_row, tile_row + SUB)
-            far_rows = slice(tile_row - first_row, tile_row - first_row + SUB)
             cosine = cosine_ref[rows, :]
             scales = (1.0, 1.0 / (12.0 * cosine), 1.0 / 12.0, 1.0 / 12.0)
             spots = {0: ((0, 0), (1, 1)), row_block - SUB: ((SUB - 2, 2), (SUB - 1, 3))}.get(tile_row, ())
@@ -460,11 +517,13 @@
 
                 def total(moment):
                     near = core_refs[moment // share][moment % share, rows, lanes]
-                    value = (mine_ref[moment, rows, lanes] + near) + far_ref[moment, far_rows, lanes]
+                    far_row = moment * piece_rows + tile_row - first_row
+                    value = (mine_ref[moment, rows, lanes] + near) + far_ref[far_row:far_row + SUB, lanes]
                     for at, edge in spots:
                         spot = moment * EDGE_ROWS + edge
+                        edge_far = far_refs[-1][edge_start + spot:edge_start + spot + 1, lanes]
                         spot = slice(spot, spot + 1)
-                        line = (edge_mine_ref[1, spot, lanes] + edge_core_ref[1, spot, lanes]) + edge_far_ref[spot, lanes]
+                        line = (edge_mine_ref[1, spot, lanes] + edge_core_ref[1, spot, lanes]) + edge_far
                         value = jnp.where(sub == at, line, value)
                     return value
 
@@ -481,7 +540,7 @@
                         entry += 1
 
 
-def finish(pieces, cosine, mine, edge_mine, edge_core, edge_far, far, core):
+def finish(pieces, cosine, mine, edge_mine, edge_core, far, core):
     moments, row_block, width = mine.shape
     vmem = pl.BlockSpec(memory_space=pltpu.VMEM)
     entries = FEATURES * (FEATURES + 1) // 2
@@ -491,12 +550,12 @@
             jax.ShapeDtypeStruct((row_block, width), F32),
             jax.ShapeDtypeStruct((entries, row_block, width), F32),
         ),
-        in_specs=[vmem] * (5 + len(far) + len(core)),
+        in_specs=[vmem] * (4 + len(far) + len(core)),
         out_specs=(vmem, vmem),
-        compiler_params=pltpu.CompilerParams(vmem_limit_bytes=VMEM_BYTES),
+        compiler_params=pltpu.CompilerParams(vmem_limit_bytes=SMALL_VMEM_BYTES),
         cost_estimate=SMALL_COST,
         name="finish",
-    )(cosine, mine, edge_mine, edge_core, edge_far, *far, *core)
+    )(cosine, mine, edge_mine, edge_core, *far, *core)
 
 
 def exchange(value, distance):
@@ -511,25 +570,29 @@
     piece_rows = row_block // 2
     pieces = tuple(range(0, row_block, piece_rows))
 
-    top, bottom, inner, cosine, limits = halo_rows(strip_quality, ranges, strips)
+    top, bottom, inner, cosine, token = halo_rows(strips)
     forward = [(i, i + 1) for i in range(tile_count - 1)]
     backward = [(target, source) for source, target in forward]
     above = lax.ppermute(bottom, "tile", forward)
     below = lax.ppermute(top, "tile", backward)
 
-    def compute(order, remote, first_row, row_count, count):
-        return moments_of(strip_quality, ranges, cosine, strips, order, remote, first_row, row_count, count)
-
-    mine, other, token = compute((top, top), True, pieces[0], piece_rows, 1)
-    far = [exchange(mine + exchange(other, 1), 2)]
-    edge_mine, edge_other, token = edge_moments(limits, cosine, above, top, inner, bottom, below, token)
+    def compute(order, remote, first_row, row_count, source):
+        return moments_of(source, cosine, strips, order, remote, first_row, row_count, PIECES)
+
+    def swap(parts):
+        return [exchange(part, 1) for part in parts]
+
+    mine, *other, token, limits = compute((token, token), True, pieces[0], piece_rows, (strip_quality, ranges))
+    payload, token = combine(mine, swap(other), (), (above, below))
+    far = [exchange(payload, 2)]
+    mine, *other, token = compute((token, token), True, pieces[1], piece_rows, (limits,))
+    near = swap(other)
+    edge_mine, edge_other, token = edge_moments(limits, cosine, above, top, inner, bottom, below, token, far[0])
     edge_core = exchange(edge_other, 1)
-    edge_far = exchange(edge_mine[0] + edge_core[0], 2)
-    mine, other, token = compute((token, token), True, pieces[1], piece_rows, 1)
-    far.append(exchange(mine + exchange(other, 1), 2))
-    mine, *other, token = compute((token, token), False, 0, row_block, 3)
-    core = [exchange(piece, 1) for piece in other]
-    return finish(pieces, cosine, mine, edge_mine, edge_core, edge_far, far, core)
+    payload, token = combine(mine, near, (edge_mine, edge_core), (token,))
+    far.append(exchange(payload, 2))
+    mine, *other, token = compute((token, token), False, 0, row_block, (limits,))
+    return finish(pieces, cosine, mine, edge_mine, edge_core, far, swap(other))
 
 
 def solution(mesh):

time: 79.3 us -> 67.5 us (0.85)
  the two profiles are of different devices: /device:TPU:12 before, /device:TPU:25 now
where the time goes in v3:
time: 67.5 us; the launch traced here: 67.3 us
  Pallas kernels  47.8 us (71%)
  starting transfers between devices  13.7 us (20%)
  waiting for transfers between devices  5.08 us (8%)
  between operations  0.74 us (1%)
    pallas_call x3, Pallas kernels, moments_of(): pl.pallas_call(functools.partial(moment_kernel, remote=remote, first_row=...  41.7 us
    ppermute x12, starting transfers between devices, exchange(): lax.ppermute(value, 'acq', [(source, source ^ distance) for source in ran...  7.55 us
    ppermute x12, waiting for transfers between devices, exchange(): lax.ppermute(value, 'acq', [(source, source ^ distance) for source in ran...  3.79 us
    ppermute x1, starting transfers between devices, local(): above = lax.ppermute(bottom, 'tile', forward)  3.15 us
    ppermute x1, starting transfers between devices, local(): below = lax.ppermute(top, 'tile', backward)  3.03 us
    pallas_call x1, Pallas kernels, edge_moments(): pl.pallas_call(edge_kernel, out_shape=(out, out, jax.ShapeDtypeStruct((SU...  2.66 us
    pallas_call x1, Pallas kernels, halo_rows(): pl.pallas_call(halo_kernel, out_shape=(pair, pair, inner, cosine, jax.Sha...  2.17 us
  transfers between devices with their start and end apart: 14, of which 8 were waited for; matrix products, arithmetic and copies ran while one was open for 0% of the time, Pallas kernels for 66%

profile of v3, /device:TPU:25, one launch (start us, length us, event | category | flops | bytes accessed | tf_op | source)
XLA Modules:
  0.0 67.3 jit_solution(10043040658244862331)
XLA Ops:
  0.6 0.0 copy-start
  0.6 0.0 copy-start.1
  0.6 2.2 %halo_rows.1 = (f32[2,48,1024]{2,1,0:T(8,128)S(1)}, f32[2,48,1024]{2,1,0:T(8,128)S(1)}, f32[4,48,1024]{2,1,0:T(8,128)S(1)}, f32[64,128]{1,0:T(8,128)S(1)}, f32[8,128]{1,0:T(8,128)S(1)}) custom-call(f32[48,64,1024]{2,1,0:T(8,128)} %refs_2_.3), custom_call_target="tpu_custom_call" | custom-call | flops 1 | bytes 1 | tf_op jit(solution)/shard_map/halo_rows/pallas_call | solution.py:105
  2.8 3.1 %collective-permute-start.3 = (f32[2,48,1024]{2,1,0:T(8,128)S(1)}, f32[2,48,1024]{2,1,0:T(8,128)S(1)}, u32[]{:S(2)}, u32[]{:S(2)}) collective-permute-start(f32[2,48,1024]{2,1,0:T(8,128)S(1)} %get-tuple-element.35.bottom_ref), channel_id=1, source_target_pairs={{0,4},{4,8},{8,12},{12,16},{16,20},{20,24},{24,28},{1,5},{5,9},{9,... | collective-permute-start | bytes 1179656 | tf_op jit(solution)/shard_map/ppermute | solution.py:576
  6.0 3.0 %collective-permute-start.4 = (f32[2,48,1024]{2,1,0:T(8,128)S(1)}, f32[2,48,1024]{2,1,0:T(8,128)S(1)}, u32[]{:S(2)}, u32[]{:S(2)}) collective-permute-start(f32[2,48,1024]{2,1,0:T(8,128)S(1)} %get-tuple-element.36.top_ref), channel_id=1, source_target_pairs={{4,0},{8,4},{12,8},{16,12},{20,16},{24,20},{28,24},{5,1},{9,5},{13... | collective-permute-start | bytes 1179656 | tf_op jit(solution)/shard_map/ppermute | solution.py:577
  9.0 0.0 copy-done
  9.0 0.0 copy-done.1
  9.0 11.8 %moments_remote.2 = (f32[15,32,256]{2,1,0:T(8,128)S(1)}, f32[5,32,256]{2,1,0:T(8,128)S(1)}, f32[5,32,256]{2,1,0:T(8,128)S(1)}, f32[5,32,256]{2,1,0:T(8,128)S(1)}...) custom-call(f32[48]{0:T(128)S(1)} %copy-done.1, s32[4,48]{1,0:T(4,128)S(1)} %bitcast.1, ...), custom_call_target="tpu_custom_call" | custom-call | flops 1 | bytes 1 | tf_op jit(solution)/shard_map/moments_remote/pallas_call | solution.py:365
  20.9 1.3 %collective-permute-start = (f32[5,32,256]{2,1,0:T(8,128)S(1)}, f32[5,32,256]{2,1,0:T(8,128)S(1)}, u32[]{:S(2)}, u32[]{:S(2)}) collective-permute-start(f32[5,32,256]{2,1,0:T(8,128)S(1)} %get-tuple-element.32), channel_id=1, source_target_pairs={{0,1},{1,0},{2,3},{3,2},{4,5},{5,4},{6,7},{7,6},{8,9},{9,8},{10,11... | collective-permute-start | bytes 491528 | tf_op jit(solution)/shard_map/ppermute | solution.py:563
  22.2 0.1 collective-permute-start.1
  22.2 0.4 collective-permute-start.2
  22.7 0.5 collective-permute-done.refs_0_
  23.2 0.4 collective-permute-done.1.refs_1_
  23.6 0.2 collective-permute-done.2.refs_2_
  23.8 0.0 collective-permute-done.3.refs_3_.above_ref
  23.8 1.3 %collective-permute-done.4.refs_4_.below_ref = f32[2,48,1024]{2,1,0:T(8,128)S(1)} collective-permute-done((f32[2,48,1024]{2,1,0:T(8,128)S(1)}, f32[2,48,1024]{2,1,0:T(8,128)S(1)}, u32[]{:S(2)}, u32[]{:S(2)}) %collective-permute-start.4) | collective-permute-done | bytes 393248 | tf_op jit(solution)/shard_map/ppermute | solution.py:577
  25.1 0.1 combine.2
  25.1 1.3 %collective-permute-start.8 = (f32[480,256]{1,0:T(8,128)S(1)}, f32[480,256]{1,0:T(8,128)S(1)}, u32[]{:S(2)}, u32[]{:S(2)}) collective-permute-start(f32[480,256]{1,0:T(8,128)S(1)} %get-tuple-element.44), channel_id=1, source_target_pairs={{0,2},{1,3},{2,0},{3,1},{4,6},{5,7},{6,4},{7,5},{8,10},{9,11},{10,... | collective-permute-start | bytes 1474568 | tf_op jit(solution)/shard_map/ppermute | solution.py:563
  26.4 10.5 %moments_remote.3 = (f32[15,32,256]{2,1,0:T(8,128)S(1)}, f32[5,32,256]{2,1,0:T(8,128)S(1)}, f32[5,32,256]{2,1,0:T(8,128)S(1)}, f32[5,32,256]{2,1,0:T(8,128)S(1)}, f32[8,128]{1,0:T(8,128)S(1)}) custom-call(f32[5,48,128]{2,1,0:T(8,128)S(1)} %get-tuple-element.30.refs_0_.limits_ref, f32[64,128]{1,0:T(8,128)S(1)} %get-tuple-element.28.refs_2_.refs_1_.cosine_ref, ...), custom_call_target="tpu_custom_call" | custom-call | flops 1 | bytes 1 | tf_op jit(solution)/shard_map/moments_remote/pallas_call | solution.py:365
  36.9 0.8 %collective-permute-start.5 = (f32[5,32,256]{2,1,0:T(8,128)S(1)}, f32[5,32,256]{2,1,0:T(8,128)S(1)}, u32[]{:S(2)}, u32[]{:S(2)}) collective-permute-start(f32[5,32,256]{2,1,0:T(8,128)S(1)} %get-tuple-element.39), channel_id=1, source_target_pairs={{0,1},{1,0},{2,3},{3,2},{4,5},{5,4},{6,7},{7,6},{8,9},{9,8},{10,11... | collective-permute-start | bytes 491528 | tf_op jit(solution)/shard_map/ppermute | solution.py:563
  37.8 0.1 collective-permute-start.6
  37.8 0.4 collective-permute-start.7
  38.3 0.0 collective-permute-done.8.second_order_ref.refs_0_
  38.3 2.7 %moments_edge.1 = (f32[2,64,256]{2,1,0:T(8,128)S(1)}, f32[2,64,256]{2,1,0:T(8,128)S(1)}, f32[8,128]{1,0:T(8,128)S(1)}) custom-call(f32[5,48,128]{2,1,0:T(8,128)S(1)} %get-tuple-element.30.refs_0_.limits_ref, f32[64,128]{1,0:T(8,128)S(1)} %get-tuple-element.28.refs_2_.refs_1_.cosine_ref, f32[2,48,1024]{2,1,0:T(8,128)S(1)} %collective-permute-done.3.refs_3_.above_ref, ...), custom_call_target="tpu_custom_call" | custom-call | flops 1 | bytes 1 | tf_op jit(solution)/shard_map/moments_edge/pallas_call | solution.py:461
  40.9 0.6 collective-permute-start.9
  41.6 0.0 collective-permute-done.5.refs_0_
  41.6 0.0 collective-permute-done.6.refs_1_
  41.6 0.0 collective-permute-done.7.refs_2_
  41.6 1.0 %collective-permute-done.9.refs_4_.edge_core_ref = f32[2,64,256]{2,1,0:T(8,128)S(1)} collective-permute-done((f32[2,64,256]{2,1,0:T(8,128)S(1)}, f32[2,64,256]{2,1,0:T(8,128)S(1)}, u32[]{:S(2)}, u32[]{:S(2)}) %collective-permute-start.9) | collective-permute-done | bytes 131104 | tf_op jit(solution)/shard_map/ppermute | solution.py:563
  42.6 0.1 combine.3
  42.6 1.3 %collective-permute-start.10 = (f32[544,256]{1,0:T(8,128)S(1)}, f32[544,256]{1,0:T(8,128)S(1)}, u32[]{:S(2)}, u32[]{:S(2)}) collective-permute-start(f32[544,256]{1,0:T(8,128)S(1)} %get-tuple-element.50), channel_id=1, source_target_pairs={{0,2},{1,3},{2,0},{3,1},{4,6},{5,7},{6,4},{7,5},{8,10},{9,11},{10,... | collective-permute-start | bytes 1671176 | tf_op jit(solution)/shard_map/ppermute | solution.py:563
  43.9 19.3 %moments_own.1 = (f32[15,64,256]{2,1,0:T(8,128)S(1)}, f32[5,64,256]{2,1,0:T(8,128)S(1)}, f32[5,64,256]{2,1,0:T(8,128)S(1)}, f32[5,64,256]{2,1,0:T(8,128)S(1)}, f32[8,128]{1,0:T(8,128)}) custom-call(f32[5,48,128]{2,1,0:T(8,128)S(1)} %get-tuple-element.30.refs_0_.limits_ref, f32[64,128]{1,0:T(8,128)S(1)} %get-tuple-element.28.refs_2_.refs_1_.cosine_ref, ...), custom_call_target="tpu_custom_call" | custom-call | flops 1 | bytes 1 | tf_op jit(solution)/shard_map/moments_own/pallas_call | solution.py:365
  63.3 0.7 %collective-permute-start.11 = (f32[5,64,256]{2,1,0:T(8,128)S(1)}, f32[5,64,256]{2,1,0:T(8,128)S(1)}, u32[]{:S(2)}, u32[]{:S(2)}) collective-permute-start(f32[5,64,256]{2,1,0:T(8,128)S(1)} %get-tuple-element.51), channel_id=1, source_target_pairs={{0,1},{1,0},{2,3},{3,2},{4,5},{5,4},{6,7},{7,6},{8,9},{9,8},{10,11... | collective-permute-start | bytes 983048 | tf_op jit(solution)/shard_map/ppermute | solution.py:563
  64.0 0.1 collective-permute-start.12
  64.0 0.4 collective-permute-start.13
  64.5 0.7 %collective-permute-done.11.refs_2_ = f32[5,64,256]{2,1,0:T(8,128)S(1)} collective-permute-done((f32[5,64,256]{2,1,0:T(8,128)S(1)}, f32[5,64,256]{2,1,0:T(8,128)S(1)}, u32[]{:S(2)}, u32[]{:S(2)}) %collective-permute-start.11) | collective-permute-done | bytes 327712 | tf_op jit(solution)/shard_map/ppermute | solution.py:563
  65.2 0.5 collective-permute-done.12.refs_3_
  65.7 0.5 collective-permute-done.13.refs_4_
  66.2 0.0 collective-permute-done.10.refs_1_
  66.2 1.2 %finish.1 = (f32[64,256]{1,0:T(8,128)}, f32[10,64,256]{2,1,0:T(8,128)}) custom-call(f32[64,128]{1,0:T(8,128)S(1)} %get-tuple-element.28.refs_2_.refs_1_.cosine_ref, f32[15,64,256]{2,1,0:T(8,128)S(1)} %get-tuple-element.49.mine_ref, f32[2,64,256]{2,1,0:T(8,128)S(1)} %get-tuple-element.45.refs_3_.edge_mine_ref, ...), custom_call_target="tpu_custom_call" | custom-call | flops 1 | bytes 1 | tf_op jit(solution)/shard_map/finish/pallas_call | solution.py:547
Async XLA Ops:
  0.6 8.4 %copy-start = (s32[48,4]{0,1:T(4,128)S(1)}, s32[48,4]{0,1:T(4,128)}, u32[]{:S(2)}) copy-start(s32[48,4]{0,1:T(4,128)} %param.5) | copy-start | bytes 2308
  0.6 8.4 %copy-start.1 = (f32[48]{0:T(128)S(1)}, f32[48]{0:T(128)}, u32[]{:S(2)}) copy-start(f32[48]{0:T(128)} %refs_0_.1) | copy-start | bytes 580
  2.8 21.0 %collective-permute-start.3 = (f32[2,48,1024]{2,1,0:T(8,128)S(1)}, f32[2,48,1024]{2,1,0:T(8,128)S(1)}, u32[]{:S(2)}, u32[]{:S(2)}) collective-permute-start(f32[2,48,1024]{2,1,0:T(8,128)S(1)} %get-tuple-element.35.bottom_ref), channel_id=1, source_target_pairs={{0,4},{4,8},{8,12},{12,16},{16,20},{20,24},{24,28},{1,5},{5,9},{9,... | collective-permute-start | bytes 1179656 | tf_op jit(solution)/shard_map/ppermute | solution.py:576
  6.0 19.1 %collective-permute-start.4 = (f32[2,48,1024]{2,1,0:T(8,128)S(1)}, f32[2,48,1024]{2,1,0:T(8,128)S(1)}, u32[]{:S(2)}, u32[]{:S(2)}) collective-permute-start(f32[2,48,1024]{2,1,0:T(8,128)S(1)} %get-tuple-element.36.top_ref), channel_id=1, source_target_pairs={{4,0},{8,4},{12,8},{16,12},{20,16},{24,20},{28,24},{5,1},{9,5},{13... | collective-permute-start | bytes 1179656 | tf_op jit(solution)/shard_map/ppermute | solution.py:577
  20.9 2.3 %collective-permute-start = (f32[5,32,256]{2,1,0:T(8,128)S(1)}, f32[5,32,256]{2,1,0:T(8,128)S(1)}, u32[]{:S(2)}, u32[]{:S(2)}) collective-permute-start(f32[5,32,256]{2,1,0:T(8,128)S(1)} %get-tuple-element.32), channel_id=1, source_target_pairs={{0,1},{1,0},{2,3},{3,2},{4,5},{5,4},{6,7},{7,6},{8,9},{9,8},{10,11... | collective-permute-start | bytes 491528 | tf_op jit(solution)/shard_map/ppermute | solution.py:563
  22.2 1.4 %collective-permute-start.1 = (f32[5,32,256]{2,1,0:T(8,128)S(1)}, f32[5,32,256]{2,1,0:T(8,128)S(1)}, u32[]{:S(2)}, u32[]{:S(2)}) collective-permute-start(f32[5,32,256]{2,1,0:T(8,128)S(1)} %get-tuple-element.33), channel_id=1, source_target_pairs={{0,1},{1,0},{2,3},{3,2},{4,5},{5,4},{6,7},{7,6},{8,9},{9,8},{10,11... | collective-permute-start | bytes 491528 | tf_op jit(solution)/shard_map/ppermute | solution.py:563
  22.2 1.6 %collective-permute-start.2 = (f32[5,32,256]{2,1,0:T(8,128)S(1)}, f32[5,32,256]{2,1,0:T(8,128)S(1)}, u32[]{:S(2)}, u32[]{:S(2)}) collective-permute-start(f32[5,32,256]{2,1,0:T(8,128)S(1)} %get-tuple-element.34), channel_id=1, source_target_pairs={{0,1},{1,0},{2,3},{3,2},{4,5},{5,4},{6,7},{7,6},{8,9},{9,8},{10,11... | collective-permute-start | bytes 491528 | tf_op jit(solution)/shard_map/ppermute | solution.py:563
  25.1 13.1 %collective-permute-start.8 = (f32[480,256]{1,0:T(8,128)S(1)}, f32[480,256]{1,0:T(8,128)S(1)}, u32[]{:S(2)}, u32[]{:S(2)}) collective-permute-start(f32[480,256]{1,0:T(8,128)S(1)} %get-tuple-element.44), channel_id=1, source_target_pairs={{0,2},{1,3},{2,0},{3,1},{4,6},{5,7},{6,4},{7,5},{8,10},{9,11},{10,... | collective-permute-start | bytes 1474568 | tf_op jit(solution)/shard_map/ppermute | solution.py:563
  36.9 4.7 %collective-permute-start.5 = (f32[5,32,256]{2,1,0:T(8,128)S(1)}, f32[5,32,256]{2,1,0:T(8,128)S(1)}, u32[]{:S(2)}, u32[]{:S(2)}) collective-permute-start(f32[5,32,256]{2,1,0:T(8,128)S(1)} %get-tuple-element.39), channel_id=1, source_target_pairs={{0,1},{1,0},{2,3},{3,2},{4,5},{5,4},{6,7},{7,6},{8,9},{9,8},{10,11... | collective-permute-start | bytes 491528 | tf_op jit(solution)/shard_map/ppermute | solution.py:563
  37.8 3.8 %collective-permute-start.6 = (f32[5,32,256]{2,1,0:T(8,128)S(1)}, f32[5,32,256]{2,1,0:T(8,128)S(1)}, u32[]{:S(2)}, u32[]{:S(2)}) collective-permute-start(f32[5,32,256]{2,1,0:T(8,128)S(1)} %get-tuple-element.40), channel_id=1, source_target_pairs={{0,1},{1,0},{2,3},{3,2},{4,5},{5,4},{6,7},{7,6},{8,9},{9,8},{10,11... | collective-permute-start | bytes 491528 | tf_op jit(solution)/shard_map/ppermute | solution.py:563
  37.8 3.7 %collective-permute-start.7 = (f32[5,32,256]{2,1,0:T(8,128)S(1)}, f32[5,32,256]{2,1,0:T(8,128)S(1)}, u32[]{:S(2)}, u32[]{:S(2)}) collective-permute-start(f32[5,32,256]{2,1,0:T(8,128)S(1)} %get-tuple-element.41), channel_id=1, source_target_pairs={{0,1},{1,0},{2,3},{3,2},{4,5},{5,4},{6,7},{7,6},{8,9},{9,8},{10,11... | collective-permute-start | bytes 491528 | tf_op jit(solution)/shard_map/ppermute | solution.py:563
  40.9 1.6 %collective-permute-start.9 = (f32[2,64,256]{2,1,0:T(8,128)S(1)}, f32[2,64,256]{2,1,0:T(8,128)S(1)}, u32[]{:S(2)}, u32[]{:S(2)}) collective-permute-start(f32[2,64,256]{2,1,0:T(8,128)S(1)} %get-tuple-element.46), channel_id=1, source_target_pairs={{0,1},{1,0},{2,3},{3,2},{4,5},{5,4},{6,7},{7,6},{8,9},{9,8},{10,11... | collective-permute-start | bytes 393224 | tf_op jit(solution)/shard_map/ppermute | solution.py:563
  42.6 23.5 %collective-permute-start.10 = (f32[544,256]{1,0:T(8,128)S(1)}, f32[544,256]{1,0:T(8,128)S(1)}, u32[]{:S(2)}, u32[]{:S(2)}) collective-permute-start(f32[544,256]{1,0:T(8,128)S(1)} %get-tuple-element.50), channel_id=1, source_target_pairs={{0,2},{1,3},{2,0},{3,1},{4,6},{5,7},{6,4},{7,5},{8,10},{9,11},{10,... | collective-permute-start | bytes 1671176 | tf_op jit(solution)/shard_map/ppermute | solution.py:563
  63.3 2.0 %collective-permute-start.11 = (f32[5,64,256]{2,1,0:T(8,128)S(1)}, f32[5,64,256]{2,1,0:T(8,128)S(1)}, u32[]{:S(2)}, u32[]{:S(2)}) collective-permute-start(f32[5,64,256]{2,1,0:T(8,128)S(1)} %get-tuple-element.51), channel_id=1, source_target_pairs={{0,1},{1,0},{2,3},{3,2},{4,5},{5,4},{6,7},{7,6},{8,9},{9,8},{10,11... | collective-permute-start | bytes 983048 | tf_op jit(solution)/shard_map/ppermute | solution.py:563
  64.0 1.7 %collective-permute-start.12 = (f32[5,64,256]{2,1,0:T(8,128)S(1)}, f32[5,64,256]{2,1,0:T(8,128)S(1)}, u32[]{:S(2)}, u32[]{:S(2)}) collective-permute-start(f32[5,64,256]{2,1,0:T(8,128)S(1)} %get-tuple-element.52), channel_id=1, source_target_pairs={{0,1},{1,0},{2,3},{3,2},{4,5},{5,4},{6,7},{7,6},{8,9},{9,8},{10,11... | collective-permute-start | bytes 983048 | tf_op jit(solution)/shard_map/ppermute | solution.py:563
  64.0 2.1 %collective-permute-start.13 = (f32[5,64,256]{2,1,0:T(8,128)S(1)}, f32[5,64,256]{2,1,0:T(8,128)S(1)}, u32[]{:S(2)}, u32[]{:S(2)}) collective-permute-start(f32[5,64,256]{2,1,0:T(8,128)S(1)} %get-tuple-element.53), channel_id=1, source_target_pairs={{0,1},{1,0},{2,3},{3,2},{4,5},{5,4},{6,7},{7,6},{8,9},{9,8},{10,11... | collective-permute-start | bytes 983048 | tf_op jit(solution)/shard_map/ppermute | solution.py:563

commit v4 on v3

--- a/solution.py
+++ b/solution.py
@@ -567,8 +567,6 @@
     strip_count, row_block, col_count = strips.shape
     tile_count = lax.axis_size("tile")
     ranges = valid_ranges.T
-    piece_rows = row_block // 2
-    pieces = tuple(range(0, row_block, piece_rows))
 
     top, bottom, inner, cosine, token = halo_rows(strips)
     forward = [(i, i + 1) for i in range(tile_count - 1)]
@@ -582,17 +580,14 @@
     def swap(parts):
         return [exchange(part, 1) for part in parts]
 
-    mine, *other, token, limits = compute((token, token), True, pieces[0], piece_rows, (strip_quality, ranges))
-    payload, token = combine(mine, swap(other), (), (above, below))
-    far = [exchange(payload, 2)]
-    mine, *other, token = compute((token, token), True, pieces[1], piece_rows, (limits,))
+    mine, *other, token, limits = compute((token, token), True, 0, row_block, (strip_quality, ranges))
     near = swap(other)
-    edge_mine, edge_other, token = edge_moments(limits, cosine, above, top, inner, bottom, below, token, far[0])
+    edge_mine, edge_other, token = edge_moments(limits, cosine, above, top, inner, bottom, below, token, token)
     edge_core = exchange(edge_other, 1)
     payload, token = combine(mine, near, (edge_mine, edge_core), (token,))
-    far.append(exchange(payload, 2))
+    far = exchange(payload, 2)
     mine, *other, token = compute((token, token), False, 0, row_block, (limits,))
-    return finish(pieces, cosine, mine, edge_mine, edge_core, far, swap(other))
+    return finish((0,), cosine, mine, edge_mine, edge_core, [far], swap(other))
 
 
 def solution(mesh):

time: 67.5 us -> 60.8 us (0.901)
  the two profiles are of different devices: /device:TPU:25 before, /device:TPU:12 now
where the time goes in v4:
time: 60.8 us; the launch traced here: 59.8 us
  Pallas kernels  44.9 us (74%)
  starting transfers between devices  9.21 us (15%)
  waiting for transfers between devices  4.91 us (8%)
  between operations  0.73 us (1%)
    pallas_call x2, Pallas kernels, moments_of(): pl.pallas_call(functools.partial(moment_kernel, remote=remote, first_row=...  38.8 us
    ppermute x8, waiting for transfers between devices, exchange(): lax.ppermute(value, 'acq', [(source, source ^ distance) for source in ran...  4.9 us
    ppermute x1, starting transfers between devices, local(): above = lax.ppermute(bottom, 'tile', forward)  3.43 us
    ppermute x8, starting transfers between devices, exchange(): lax.ppermute(value, 'acq', [(source, source ^ distance) for source in ran...  3.37 us
    pallas_call x1, Pallas kernels, edge_moments(): pl.pallas_call(edge_kernel, out_shape=(out, out, jax.ShapeDtypeStruct((SU...  2.63 us
    ppermute x1, starting transfers between devices, local(): below = lax.ppermute(top, 'tile', backward)  2.41 us
    pallas_call x1, Pallas kernels, halo_rows(): pl.pallas_call(halo_kernel, out_shape=(pair, pair, inner, cosine, jax.Sha...  2.17 us
  transfers between devices with their start and end apart: 10, of which 5 were waited for; matrix products, arithmetic and copies ran while one was open for 0% of the time, Pallas kernels for 69%

profile of v4, /device:TPU:12, one launch (start us, length us, event | category | flops | bytes accessed | tf_op | source)
XLA Modules:
  0.0 59.8 jit_solution(13284508818103407405)
XLA Ops:
  0.6 0.0 copy-start.1
  0.6 0.0 copy-start
  0.6 2.2 %halo_rows.1 = (f32[2,48,1024]{2,1,0:T(8,128)S(1)}, f32[2,48,1024]{2,1,0:T(8,128)S(1)}, f32[4,48,1024]{2,1,0:T(8,128)S(1)}, f32[64,128]{1,0:T(8,128)S(1)}, f32[8,128]{1,0:T(8,128)S(1)}) custom-call(f32[48,64,1024]{2,1,0:T(8,128)} %refs_2_.1), custom_call_target="tpu_custom_call" | custom-call | flops 1 | bytes 1 | tf_op jit(solution)/shard_map/halo_rows/pallas_call | solution.py:105
  2.8 3.4 %collective-permute-start.3 = (f32[2,48,1024]{2,1,0:T(8,128)S(1)}, f32[2,48,1024]{2,1,0:T(8,128)S(1)}, u32[]{:S(2)}, u32[]{:S(2)}) collective-permute-start(f32[2,48,1024]{2,1,0:T(8,128)S(1)} %get-tuple-element.29.bottom_ref), channel_id=1, source_target_pairs={{0,4},{4,8},{8,12},{12,16},{16,20},{20,24},{24,28},{1,5},{5,9},{9,... | collective-permute-start | bytes 1179656 | tf_op jit(solution)/shard_map/ppermute | solution.py:574
  6.3 2.4 %collective-permute-start.4 = (f32[2,48,1024]{2,1,0:T(8,128)S(1)}, f32[2,48,1024]{2,1,0:T(8,128)S(1)}, u32[]{:S(2)}, u32[]{:S(2)}) collective-permute-start(f32[2,48,1024]{2,1,0:T(8,128)S(1)} %get-tuple-element.30.top_ref), channel_id=1, source_target_pairs={{4,0},{8,4},{12,8},{16,12},{20,16},{24,20},{28,24},{5,1},{9,5},{13... | collective-permute-start | bytes 1179656 | tf_op jit(solution)/shard_map/ppermute | solution.py:575
  8.7 0.0 copy-done.1
  8.7 0.0 copy-done
  8.7 19.5 %moments_remote.1 = (f32[15,64,256]{2,1,0:T(8,128)S(1)}, f32[5,64,256]{2,1,0:T(8,128)S(1)}, f32[5,64,256]{2,1,0:T(8,128)S(1)}, f32[5,64,256]{2,1,0:T(8,128)S(1)}...) custom-call(f32[48]{0:T(128)S(1)} %copy-done.1, s32[4,48]{1,0:T(4,128)S(1)} %bitcast.1, ...), custom_call_target="tpu_custom_call" | custom-call | flops 1 | bytes 1 | tf_op jit(solution)/shard_map/moments_remote/pallas_call | solution.py:365
  28.2 0.1 collective-permute-start
  28.3 0.5 collective-permute-start.1
  28.8 0.1 collective-permute-start.2
  28.9 0.0 collective-permute-done.3.above_ref
  28.9 0.0 collective-permute-done.4.below_ref
  28.9 2.6 %moments_edge.1 = (f32[2,64,256]{2,1,0:T(8,128)S(1)}, f32[2,64,256]{2,1,0:T(8,128)S(1)}, f32[8,128]{1,0:T(8,128)S(1)}) custom-call(f32[5,48,128]{2,1,0:T(8,128)S(1)} %get-tuple-element.24.limits_ref.refs_0_, f32[64,128]{1,0:T(8,128)S(1)} %get-tuple-element.22.refs_2_.cosine_ref.refs_1_, f32[2,48,1024]{2,1,0:T(8,128)S(1)} %collective-permute-done.3.above_ref, ...), custom_call_target="tpu_custom_call" | custom-call | flops 1 | bytes 1 | tf_op jit(solution)/shard_map/moments_edge/pallas_call | solution.py:461
  31.5 0.5 collective-permute-start.5
  32.0 0.0 collective-permute-done.refs_0_
  32.0 0.0 collective-permute-done.1.refs_1_
  32.0 0.0 collective-permute-done.2.refs_2_
  32.0 1.0 %collective-permute-done.5.refs_4_.edge_core_ref = f32[2,64,256]{2,1,0:T(8,128)S(1)} collective-permute-done((f32[2,64,256]{2,1,0:T(8,128)S(1)}, f32[2,64,256]{2,1,0:T(8,128)S(1)}, u32[]{:S(2)}, u32[]{:S(2)}) %collective-permute-start.5) | collective-permute-done | bytes 131104 | tf_op jit(solution)/shard_map/ppermute | solution.py:563
  33.0 0.1 combine.1
  33.1 1.6 %collective-permute-start.6 = (f32[1024,256]{1,0:T(8,128)S(1)}, f32[1024,256]{1,0:T(8,128)S(1)}, u32[]{:S(2)}, u32[]{:S(2)}) collective-permute-start(f32[1024,256]{1,0:T(8,128)S(1)} %get-tuple-element.38), channel_id=1, source_target_pairs={{0,2},{1,3},{2,0},{3,1},{4,6},{5,7},{6,4},{7,5},{8,10},{9,11},{10,... | collective-permute-start | bytes 3145736 | tf_op jit(solution)/shard_map/ppermute | solution.py:563
  34.7 19.3 %moments_own.1 = (f32[15,64,256]{2,1,0:T(8,128)S(1)}, f32[5,64,256]{2,1,0:T(8,128)S(1)}, f32[5,64,256]{2,1,0:T(8,128)S(1)}, f32[5,64,256]{2,1,0:T(8,128)S(1)}, f32[8,128]{1,0:T(8,128)}) custom-call(f32[5,48,128]{2,1,0:T(8,128)S(1)} %get-tuple-element.24.limits_ref.refs_0_, f32[64,128]{1,0:T(8,128)S(1)} %get-tuple-element.22.refs_2_.cosine_ref.refs_1_, ...), custom_call_target="tpu_custom_call" | custom-call | flops 1 | bytes 1 | tf_op jit(solution)/shard_map/moments_own/pallas_call | solution.py:365
  54.0 0.1 collective-permute-start.7
  54.2 0.4 collective-permute-start.8
  54.6 0.1 collective-permute-start.9
  54.7 1.0 %collective-permute-done.7.refs_1_ = f32[5,64,256]{2,1,0:T(8,128)S(1)} collective-permute-done((f32[5,64,256]{2,1,0:T(8,128)S(1)}, f32[5,64,256]{2,1,0:T(8,128)S(1)}, u32[]{:S(2)}, u32[]{:S(2)}) %collective-permute-start.7) | collective-permute-done | bytes 327712 | tf_op jit(solution)/shard_map/ppermute | solution.py:563
  55.7 0.5 collective-permute-done.8.refs_2_
  56.2 0.5 collective-permute-done.9.refs_3_
  56.7 1.9 %collective-permute-done.6.refs_0_ = f32[1024,256]{1,0:T(8,128)S(1)} collective-permute-done((f32[1024,256]{1,0:T(8,128)S(1)}, f32[1024,256]{1,0:T(8,128)S(1)}, u32[]{:S(2)}, u32[]{:S(2)}) %collective-permute-start.6) | collective-permute-done | bytes 1048608 | tf_op jit(solution)/shard_map/ppermute | solution.py:563
  58.6 1.2 %finish.1 = (f32[64,256]{1,0:T(8,128)}, f32[10,64,256]{2,1,0:T(8,128)}) custom-call(f32[64,128]{1,0:T(8,128)S(1)} %get-tuple-element.22.refs_2_.cosine_ref.refs_1_, f32[15,64,256]{2,1,0:T(8,128)S(1)} %get-tuple-element.37.mine_ref, f32[2,64,256]{2,1,0:T(8,128)S(1)} %get-tuple-element.33.refs_3_.edge_mine_ref, ...), custom_call_target="tpu_custom_call" | custom-call | flops 1 | bytes 1 | tf_op jit(solution)/shard_map/finish/pallas_call | solution.py:547
Async XLA Ops:
  0.6 8.1 %copy-start.1 = (f32[48]{0:T(128)S(1)}, f32[48]{0:T(128)}, u32[]{:S(2)}) copy-start(f32[48]{0:T(128)} %refs_0_.1) | copy-start | bytes 580
  0.6 8.1 %copy-start = (s32[48,4]{0,1:T(4,128)S(1)}, s32[48,4]{0,1:T(4,128)}, u32[]{:S(2)}) copy-start(s32[48,4]{0,1:T(4,128)} %param.5) | copy-start | bytes 2308
  2.8 26.0 %collective-permute-start.3 = (f32[2,48,1024]{2,1,0:T(8,128)S(1)}, f32[2,48,1024]{2,1,0:T(8,128)S(1)}, u32[]{:S(2)}, u32[]{:S(2)}) collective-permute-start(f32[2,48,1024]{2,1,0:T(8,128)S(1)} %get-tuple-element.29.bottom_ref), channel_id=1, source_target_pairs={{0,4},{4,8},{8,12},{12,16},{16,20},{20,24},{24,28},{1,5},{5,9},{9,... | collective-permute-start | bytes 1179656 | tf_op jit(solution)/shard_map/ppermute | solution.py:574
  6.3 22.6 %collective-permute-start.4 = (f32[2,48,1024]{2,1,0:T(8,128)S(1)}, f32[2,48,1024]{2,1,0:T(8,128)S(1)}, u32[]{:S(2)}, u32[]{:S(2)}) collective-permute-start(f32[2,48,1024]{2,1,0:T(8,128)S(1)} %get-tuple-element.30.top_ref), channel_id=1, source_target_pairs={{4,0},{8,4},{12,8},{16,12},{20,16},{24,20},{28,24},{5,1},{9,5},{13... | collective-permute-start | bytes 1179656 | tf_op jit(solution)/shard_map/ppermute | solution.py:575
  28.2 3.8 %collective-permute-start = (f32[5,64,256]{2,1,0:T(8,128)S(1)}, f32[5,64,256]{2,1,0:T(8,128)S(1)}, u32[]{:S(2)}, u32[]{:S(2)}) collective-permute-start(f32[5,64,256]{2,1,0:T(8,128)S(1)} %get-tuple-element.26), channel_id=1, source_target_pairs={{0,1},{1,0},{2,3},{3,2},{4,5},{5,4},{6,7},{7,6},{8,9},{9,8},{10,11... | collective-permute-start | bytes 983048 | tf_op jit(solution)/shard_map/ppermute | solution.py:563
  28.3 3.7 %collective-permute-start.1 = (f32[5,64,256]{2,1,0:T(8,128)S(1)}, f32[5,64,256]{2,1,0:T(8,128)S(1)}, u32[]{:S(2)}, u32[]{:S(2)}) collective-permute-start(f32[5,64,256]{2,1,0:T(8,128)S(1)} %get-tuple-element.27), channel_id=1, source_target_pairs={{0,1},{1,0},{2,3},{3,2},{4,5},{5,4},{6,7},{7,6},{8,9},{9,8},{10,11... | collective-permute-start | bytes 983048 | tf_op jit(solution)/shard_map/ppermute | solution.py:563
  28.8 3.2 %collective-permute-start.2 = (f32[5,64,256]{2,1,0:T(8,128)S(1)}, f32[5,64,256]{2,1,0:T(8,128)S(1)}, u32[]{:S(2)}, u32[]{:S(2)}) collective-permute-start(f32[5,64,256]{2,1,0:T(8,128)S(1)} %get-tuple-element.28), channel_id=1, source_target_pairs={{0,1},{1,0},{2,3},{3,2},{4,5},{5,4},{6,7},{7,6},{8,9},{9,8},{10,11... | collective-permute-start | bytes 983048 | tf_op jit(solution)/shard_map/ppermute | solution.py:563
  31.5 1.5 %collective-permute-start.5 = (f32[2,64,256]{2,1,0:T(8,128)S(1)}, f32[2,64,256]{2,1,0:T(8,128)S(1)}, u32[]{:S(2)}, u32[]{:S(2)}) collective-permute-start(f32[2,64,256]{2,1,0:T(8,128)S(1)} %get-tuple-element.34), channel_id=1, source_target_pairs={{0,1},{1,0},{2,3},{3,2},{4,5},{5,4},{6,7},{7,6},{8,9},{9,8},{10,11... | collective-permute-start | bytes 393224 | tf_op jit(solution)/shard_map/ppermute | solution.py:563
  33.1 25.5 %collective-permute-start.6 = (f32[1024,256]{1,0:T(8,128)S(1)}, f32[1024,256]{1,0:T(8,128)S(1)}, u32[]{:S(2)}, u32[]{:S(2)}) collective-permute-start(f32[1024,256]{1,0:T(8,128)S(1)} %get-tuple-element.38), channel_id=1, source_target_pairs={{0,2},{1,3},{2,0},{3,1},{4,6},{5,7},{6,4},{7,5},{8,10},{9,11},{10,... | collective-permute-start | bytes 3145736 | tf_op jit(solution)/shard_map/ppermute | solution.py:563
  54.0 1.7 %collective-permute-start.7 = (f32[5,64,256]{2,1,0:T(8,128)S(1)}, f32[5,64,256]{2,1,0:T(8,128)S(1)}, u32[]{:S(2)}, u32[]{:S(2)}) collective-permute-start(f32[5,64,256]{2,1,0:T(8,128)S(1)} %get-tuple-element.39), channel_id=1, source_target_pairs={{0,1},{1,0},{2,3},{3,2},{4,5},{5,4},{6,7},{7,6},{8,9},{9,8},{10,11... | collective-permute-start | bytes 983048 | tf_op jit(solution)/shard_map/ppermute | solution.py:563
  54.2 2.0 %collective-permute-start.8 = (f32[5,64,256]{2,1,0:T(8,128)S(1)}, f32[5,64,256]{2,1,0:T(8,128)S(1)}, u32[]{:S(2)}, u32[]{:S(2)}) collective-permute-start(f32[5,64,256]{2,1,0:T(8,128)S(1)} %get-tuple-element.40), channel_id=1, source_target_pairs={{0,1},{1,0},{2,3},{3,2},{4,5},{5,4},{6,7},{7,6},{8,9},{9,8},{10,11... | collective-permute-start | bytes 983048 | tf_op jit(solution)/shard_map/ppermute | solution.py:563
  54.6 2.1 %collective-permute-start.9 = (f32[5,64,256]{2,1,0:T(8,128)S(1)}, f32[5,64,256]{2,1,0:T(8,128)S(1)}, u32[]{:S(2)}, u32[]{:S(2)}) collective-permute-start(f32[5,64,256]{2,1,0:T(8,128)S(1)} %get-tuple-element.41), channel_id=1, source_target_pairs={{0,1},{1,0},{2,3},{3,2},{4,5},{5,4},{6,7},{7,6},{8,9},{9,8},{10,11... | collective-permute-start | bytes 983048 | tf_op jit(solution)/shard_map/ppermute | solution.py:563

commit v5 on v4

--- a/solution.py
+++ b/solution.py
@@ -6,7 +6,7 @@
 from jax.experimental.pallas import tpu as pltpu
 from jax.sharding import PartitionSpec as P
 
-MOMENTS = 15
+MOMENTS = 14
 FEATURES = 4
 SUB = 8
 LANES = 128
@@ -15,7 +15,7 @@
 SMALL_VMEM_BYTES = 50 * 1024 * 1024
 F32 = jnp.float32
 LOAD_PARTS = 4
-PIECES = 3
+PIECES = 2
 SMALL_COST = pl.CostEstimate(flops=1, bytes_accessed=1, transcendentals=0)
 
 
@@ -28,7 +28,7 @@
     weight = mask / steepness
     features = (z, slope_x, slope_y, curvature)
     weighted = [weight * feature for feature in features]
-    terms = [weight] + weighted
+    terms = list(weighted)
     for first in range(FEATURES):
         for second in range(first, FEATURES):
             terms.append(weighted[first] * features[second])
@@ -146,8 +146,8 @@
     refs = refs[5:]
     other_refs, token_ref = refs[:pieces], refs[pieces]
     if spread:
-        limits_ref = refs[pieces + 1]
-        refs = refs[1:]
+        limits_ref, compact_ref = refs[pieces + 1:pieces + 3]
+        refs = refs[2:]
     elevation, high_part, low_part, row_mask, col_mask, weights, first_slot, second_slot, sems = refs[pieces + 1:]
     del first_order_ref, second_order_ref
     token_ref[...] = jnp.zeros((SUB, LANES), F32)
@@ -224,18 +224,21 @@
 
     weights[...] = column_weights()
 
-    def spread_out(strip, carry):
+    def spread_out(strip, rows):
         here = pl.ds(strip, 1)
-        for kind in range(4):
-            value = ranges_ref[kind, strip].astype(F32)
+        values = [ranges_ref[kind, strip].astype(F32) for kind in range(4)] + [quality_ref[strip]]
+        lane = lax.broadcasted_iota(jnp.int32, (1, LANES), 1)
+        for kind, value in enumerate(values):
             limits_ref[kind, here, :] = jnp.full((1, LANES), value, F32)
-        limits_ref[4, here, :] = jnp.full((1, LANES), quality_ref[strip], F32)
-        return carry
+        return tuple(jnp.where(lane == strip, value, row) for row, value in zip(rows, values))
 
     if spread:
         for copy in small_copies:
             copy.wait()
-        lax.fori_loop(0, strip_count, spread_out, 0)
+        rows = lax.fori_loop(0, strip_count, spread_out, (jnp.zeros((1, LANES), F32),) * 5)
+        compact_ref[...] = jnp.zeros((SUB, 2 * LANES), F32)
+        for kind, row in enumerate(rows):
+            compact_ref[kind:kind + 1, :LANES] = row
 
     def prepare(strip, carry):
         row_low, row_high, col_low, col_high, quality = (
@@ -284,12 +287,12 @@
             cosine = cosine_ref[pl.ds(first_row + row, SUB), :]
             inverse_square = 1.0 / (cosine * cosine)
 
-            if following is not None:
-                columns_into(1 - slot, following, tile * share, share)
             unroll = strip_count if following is not None else 16
 
             def add_strips(chunk, sums):
                 for index in range(unroll):
+                    if following is not None and index in (0, 16):
+                        columns_into(1 - slot, following, tile * share + (share // 2) * (index > 0), share // 2)
                     strip = chunk * unroll + index
 
                     def load(shift):
@@ -322,7 +325,8 @@
     def first_columns(which, carry):
         for step in range(3):
             arrive(initial + step, which)
-        columns_into(0, initial + 1, which * part, part)
+        for step in range(2):
+            columns_into(0, initial + 1, which * part + step * (part // 2), part // 2)
         return carry
 
     lax.fori_loop(0, LOAD_PARTS, first_columns, 0)
@@ -360,13 +364,14 @@
     vmem = pl.BlockSpec(memory_space=pltpu.VMEM)
     anywhere = pl.BlockSpec(memory_space=pl.ANY)
     lanes = jax.ShapeDtypeStruct((5, strip_count, LANES), F32)
+    compact = jax.ShapeDtypeStruct((SUB, 2 * LANES), F32)
     parts = pltpu.VMEM((strip_count, half + 2, row_count, LANES), jnp.bfloat16)
     slot = pltpu.VMEM((strip_count, row_count, 2 * LANES), F32)
     return pl.pallas_call(
         functools.partial(moment_kernel, remote=remote, first_row=first_row, row_count=row_count, pieces=pieces, spread=spread),
-        out_shape=(out,) + (piece,) * pieces + (token,) + (lanes,) * spread,
+        out_shape=(out,) + (piece,) * pieces + (token,) + (lanes, compact) * spread,
         in_specs=[anywhere] * 2 * spread + [vmem] * (2 - spread) + [anywhere, vmem, vmem],
-        out_specs=(vmem,) * (pieces + 2 + spread),
+        out_specs=(vmem,) * (pieces + 2 + 2 * spread),
         scratch_shapes=[
             pltpu.VMEM((strip_count, half + 2, row_count + 2 * SUB, LANES), F32),
             parts,
@@ -391,7 +396,7 @@
 
 
 def edge_kernel(
-    limits_ref, cosine_ref, above_ref, top_ref, inner_ref, bottom_ref, below_ref,
+    limits_ref, compact_ref, cosine_ref, above_ref, top_ref, inner_ref, bottom_ref, below_ref,
     first_order_ref, second_order_ref, mine_ref, other_ref, token_ref,
 ):
     del first_order_ref, second_order_ref
@@ -410,9 +415,7 @@
     edges = ((0, 2), (1, 3), (row_block - 2, 8), (row_block - 1, 9))
     for out_ref, owner in ((mine_ref, core), (other_ref, 1 - core)):
         for part, owner_side in enumerate((1 - side, side)):
-            out_ref[part, MOMENTS * EDGE_ROWS:, :] = jnp.zeros(
-                (out_ref.shape[1] - MOMENTS * EDGE_ROWS, quarter * LANES), F32
-            )
+            out_ref[part, MOMENTS * EDGE_ROWS:MOMENTS * EDGE_ROWS + SUB, :] = compact_ref[...]
 
             def column_tile(tile, carry, out_ref=out_ref, part=part, first=(owner_side * 2 + owner) * quarter):
                 at = first + tile
@@ -454,19 +457,19 @@
             lax.fori_loop(0, quarter, column_tile, 0)
 
 
-def edge_moments(limits, cosine, above, top, inner, bottom, below, *order):
+def edge_moments(limits, compact, cosine, above, top, inner, bottom, below, *order):
     pair, strip_count, col_count = top.shape
-    out = jax.ShapeDtypeStruct((2, -(-MOMENTS * EDGE_ROWS // SUB) * SUB, col_count // 4), F32)
+    out = jax.ShapeDtypeStruct((2, MOMENTS * EDGE_ROWS + SUB, col_count // 4), F32)
     vmem = pl.BlockSpec(memory_space=pltpu.VMEM)
     return pl.pallas_call(
         edge_kernel,
         out_shape=(out, out, jax.ShapeDtypeStruct((SUB, LANES), F32)),
-        in_specs=[vmem] * 9,
+        in_specs=[vmem] * 10,
         out_specs=(vmem, vmem, vmem),
         compiler_params=pltpu.CompilerParams(vmem_limit_bytes=SMALL_VMEM_BYTES),
         cost_estimate=SMALL_COST,
         name="moments_edge",
-    )(limits, cosine, above, top, inner, bottom, below, *order)
+    )(limits, compact, cosine, above, top, inner, bottom, below, *order)
 
 
 def combine_kernel(mine_ref, *refs, pieces, edges):
@@ -480,12 +483,15 @@
             out_ref[at * row_count:(at + 1) * row_count, :] = mine_ref[at] + near_ref[moment]
     if edges:
         edge_mine_ref, edge_core_ref = rest[:2]
-        out_ref[pieces * share * row_count:, :] = edge_mine_ref[0] + edge_core_ref[0]
+        start, count = pieces * share * row_count, MOMENTS * EDGE_ROWS
+        out_ref[start:start + count, :] = edge_mine_ref[0, :count] + edge_core_ref[0, :count]
+        out_ref[start + count:start + count + SUB, :] = edge_mine_ref[0, count:]
+        out_ref[start + count + SUB:, :] = edge_core_ref[0, count:]
 
 
 def combine(mine, near, edges, order):
     moments, row_count, width = mine.shape
-    rows = moments * row_count + sum(edge.shape[1] for edge in edges[:1])
+    rows = moments * row_count + sum(edge.shape[1] + SUB for edge in edges[:1])
     vmem = pl.BlockSpec(memory_space=pltpu.VMEM)
     return pl.pallas_call(
         functools.partial(combine_kernel, pieces=len(near), edges=bool(edges)),
@@ -499,13 +505,30 @@
 
 
 def finish_kernel(pieces, cosine_ref, mine_ref, edge_mine_ref, edge_core_ref, *refs):
-    far_refs, core_refs = refs[:len(pieces)], refs[len(pieces):-2]
-    mean_ref, covariance_ref = refs[-2:]
+    far_refs, core_refs = refs[:len(pieces)], refs[len(pieces):-3]
+    mean_ref, covariance_ref, available_ref = refs[-3:]
     row_block, width = mean_ref.shape
     share = MOMENTS // len(core_refs)
+    edge_start = MOMENTS * row_block
+    compact_start = edge_start + MOMENTS * EDGE_ROWS
+    at_row = lax.broadcasted_iota(jnp.int32, (row_block, LANES), 0) + lax.axis_index("tile") * row_block
+    at_col = lax.broadcasted_iota(jnp.int32, (width, LANES), 0) + lax.axis_index("acq") * width
+    at_row, at_col = at_row.astype(F32), at_col.astype(F32)
+    near_start = compact_start - edge_start
+    compacts = [ref[1, near_start:near_start + SUB, :LANES] for ref in (edge_mine_ref, edge_core_ref)]
+    compacts += [far_refs[-1][compact_start + SUB * part:compact_start + SUB * (part + 1), :LANES] for part in range(2)]
+    rows_in, cols_in = [], []
+    for compact in compacts:
+        row_low, row_high, col_low, col_high, quality = (compact[kind:kind + 1, :] for kind in range(5))
+        rows_in.append(jnp.where((at_row >= row_low) & (at_row < row_high), quality, 0.0))
+        cols_in.append(jnp.where((at_col >= col_low) & (at_col < col_high), 1.0, 0.0))
+    available = lax.dot_general(
+        jnp.concatenate(rows_in, axis=1), jnp.concatenate(cols_in, axis=1), (((1,), (1,)), ((), ())),
+        precision=lax.Precision.HIGHEST, preferred_element_type=F32,
+    )
+    available_ref[...] = available
     sub = lax.broadcasted_iota(jnp.int32, (SUB, LANES), 0)
     piece_rows = row_block // len(pieces)
-    edge_start = MOMENTS * piece_rows
     for first_row, far_ref in zip(pieces, far_refs):
         for tile_row in range(first_row, first_row + piece_rows, SUB):
             rows = slice(tile_row, tile_row + SUB)
@@ -527,15 +550,17 @@
                         value = jnp.where(sub == at, line, value)
                     return value
 
-                inverse = 144.0 / jnp.maximum(144.0 * total(0), 1.0)
-                means = [total(1 + first) * inverse * scales[first] for first in range(FEATURES)]
+                along, across = total(FEATURES + 4), total(FEATURES + 7)
+                steep = along / (cosine * cosine) + across
+                inverse = 144.0 / jnp.maximum(available_ref[rows, lanes] - steep, 1.0)
+                means = [total(first) * inverse * scales[first] for first in range(FEATURES)]
                 mean_ref[rows, lanes] = means[0]
                 entry = 0
                 for first in range(FEATURES):
                     for second in range(first, FEATURES):
                         scale = scales[first] * scales[second]
                         covariance_ref[entry, rows, lanes] = (
-                            total(5 + entry) * inverse * scale - means[first] * means[second]
+                            total(FEATURES + entry) * inverse * scale - means[first] * means[second]
                         )
                         entry += 1
 
@@ -552,6 +577,7 @@
         ),
         in_specs=[vmem] * (4 + len(far) + len(core)),
         out_specs=(vmem, vmem),
+        scratch_shapes=[pltpu.VMEM((row_block, width), F32)],
         compiler_params=pltpu.CompilerParams(vmem_limit_bytes=SMALL_VMEM_BYTES),
         cost_estimate=SMALL_COST,
         name="finish",
@@ -580,9 +606,11 @@
     def swap(parts):
         return [exchange(part, 1) for part in parts]
 
-    mine, *other, token, limits = compute((token, token), True, 0, row_block, (strip_quality, ranges))
+    mine, *other, token, limits, compact = compute((token, token), True, 0, row_block, (strip_quality, ranges))
     near = swap(other)
-    edge_mine, edge_other, token = edge_moments(limits, cosine, above, top, inner, bottom, below, token, token)
+    edge_mine, edge_other, token = edge_moments(
+        limits, compact, cosine, above, top, inner, bottom, below, token, token
+    )
     edge_core = exchange(edge_other, 1)
     payload, token = combine(mine, near, (edge_mine, edge_core), (token,))
     far = exchange(payload, 2)

time: 60.8 us -> 58.5 us (0.962)
  Pallas kernels: 44.9 us -> 42.8 us
    pallas_call x2, Pallas kernels: 38.8 us -> 36.2 us  [moments_of(): pl.pallas_call(functools.partial(moment_kernel, remote=remote, first_row=...]
    pallas_call x1, Pallas kernels: 1.15 us -> 1.79 us  [finish(): pl.pallas_call(functools.partial(finish_kernel, pieces), out_shape=(jax.S...]
    ppermute x8 -> x6, starting transfers between devices: 3.37 us -> 2.84 us  [exchange(): lax.ppermute(value, 'acq', [(source, source ^ distance) for source in ran...]
    ppermute x8 -> x6, waiting for transfers between devices: 4.9 us -> 5.17 us  [exchange(): lax.ppermute(value, 'acq', [(source, source ^ distance) for source in ran...]
  transfers between devices with their start and end apart: 10 -> 8, of which waited for: 5 -> 4; matrix products, arithmetic and copies ran while one was open for 0% -> 0% of each run, Pallas kernels for 69% -> 67%
where the time goes in v5:
time: 58.5 us; the launch traced here: 57.4 us
  Pallas kernels  42.8 us (73%)
  starting transfers between devices  8.68 us (15%)
  waiting for transfers between devices  5.18 us (9%)
  between operations  0.73 us (1%)
    pallas_call x2, Pallas kernels, moments_of(): pl.pallas_call(functools.partial(moment_kernel, remote=remote, first_row=...  36.2 us
    ppermute x6, waiting for transfers between devices, exchange(): lax.ppermute(value, 'acq', [(source, source ^ distance) for source in ran...  5.17 us
    ppermute x1, starting transfers between devices, local(): above = lax.ppermute(bottom, 'tile', forward)  3.43 us
    ppermute x6, starting transfers between devices, exchange(): lax.ppermute(value, 'acq', [(source, source ^ distance) for source in ran...  2.84 us
    pallas_call x1, Pallas kernels, edge_moments(): pl.pallas_call(edge_kernel, out_shape=(out, out, jax.ShapeDtypeStruct((SU...  2.54 us
    ppermute x1, starting transfers between devices, local(): below = lax.ppermute(top, 'tile', backward)  2.41 us
    pallas_call x1, Pallas kernels, halo_rows(): pl.pallas_call(halo_kernel, out_shape=(pair, pair, inner, cosine, jax.Sha...  2.17 us
    pallas_call x1, Pallas kernels, finish(): pl.pallas_call(functools.partial(finish_kernel, pieces), out_shape=(jax.S...  1.79 us
  transfers between devices with their start and end apart: 8, of which 4 were waited for; matrix products, arithmetic and copies ran while one was open for 0% of the time, Pallas kernels for 67%

profile of v5, /device:TPU:12, one launch (start us, length us, event | category | flops | bytes accessed | tf_op | source)
XLA Modules:
  0.0 57.4 jit_solution(9752740498375173819)
XLA Ops:
  0.6 0.0 copy-start.1
  0.6 0.0 copy-start
  0.6 2.2 %halo_rows.1 = (f32[2,48,1024]{2,1,0:T(8,128)S(1)}, f32[2,48,1024]{2,1,0:T(8,128)S(1)}, f32[4,48,1024]{2,1,0:T(8,128)S(1)}, f32[64,128]{1,0:T(8,128)S(1)}, f32[8,128]{1,0:T(8,128)S(1)}) custom-call(f32[48,64,1024]{2,1,0:T(8,128)} %refs_2_.1), custom_call_target="tpu_custom_call" | custom-call | flops 1 | bytes 1 | tf_op jit(solution)/shard_map/halo_rows/pallas_call | solution.py:105
  2.8 3.4 %collective-permute-start.2 = (f32[2,48,1024]{2,1,0:T(8,128)S(1)}, f32[2,48,1024]{2,1,0:T(8,128)S(1)}, u32[]{:S(2)}, u32[]{:S(2)}) collective-permute-start(f32[2,48,1024]{2,1,0:T(8,128)S(1)} %get-tuple-element.28.bottom_ref), channel_id=1, source_target_pairs={{0,4},{4,8},{8,12},{12,16},{16,20},{20,24},{24,28},{1,5},{5,9},{9,... | collective-permute-start | bytes 1179656 | tf_op jit(solution)/shard_map/ppermute | solution.py:600
  6.3 2.4 %collective-permute-start.3 = (f32[2,48,1024]{2,1,0:T(8,128)S(1)}, f32[2,48,1024]{2,1,0:T(8,128)S(1)}, u32[]{:S(2)}, u32[]{:S(2)}) collective-permute-start(f32[2,48,1024]{2,1,0:T(8,128)S(1)} %get-tuple-element.29.top_ref), channel_id=1, source_target_pairs={{4,0},{8,4},{12,8},{16,12},{20,16},{24,20},{28,24},{5,1},{9,5},{13... | collective-permute-start | bytes 1179656 | tf_op jit(solution)/shard_map/ppermute | solution.py:601
  8.7 0.0 copy-done.1
  8.7 0.0 copy-done
  8.7 18.2 %moments_remote.1 = (f32[14,64,256]{2,1,0:T(8,128)S(1)}, f32[7,64,256]{2,1,0:T(8,128)S(1)}, f32[7,64,256]{2,1,0:T(8,128)S(1)}, f32[8,128]{1,0:T(8,128)S(1)}, f32...) custom-call(f32[48]{0:T(128)S(1)} %copy-done.1, s32[4,48]{1,0:T(4,128)S(1)} %bitcast.1, ...), custom_call_target="tpu_custom_call" | custom-call | flops 1 | bytes 1 | tf_op jit(solution)/shard_map/moments_remote/pallas_call | solution.py:370
  26.9 0.1 collective-permute-start
  27.0 0.5 collective-permute-start.1
  27.5 0.0 collective-permute-done.2.above_ref
  27.5 0.0 collective-permute-done.3.below_ref
  27.5 2.5 %moments_edge.1 = (f32[2,64,256]{2,1,0:T(8,128)S(1)}, f32[2,64,256]{2,1,0:T(8,128)S(1)}, f32[8,128]{1,0:T(8,128)S(1)}) custom-call(f32[5,48,128]{2,1,0:T(8,128)S(1)} %get-tuple-element.23.limits_ref.refs_0_, f32[8,256]{1,0:T(8,128)S(1)} %get-tuple-element.27.compact_ref, f32[64,128]{1,0:T(8,128)S(1)} %get-tuple-element.21.refs_2_.cosine_ref.refs_1_, ...), custom_call_target="tpu_custom_call" | custom-call | flops 1 | bytes 1 | tf_op jit(solution)/shard_map/moments_edge/pallas_call | solution.py:464
  30.0 0.1 collective-permute-start.4
  30.1 0.0 collective-permute-done.refs_0_
  30.2 0.0 collective-permute-done.1.refs_1_
  30.2 1.3 %collective-permute-done.4.refs_3_.edge_core_ref = f32[2,64,256]{2,1,0:T(8,128)S(1)} collective-permute-done((f32[2,64,256]{2,1,0:T(8,128)S(1)}, f32[2,64,256]{2,1,0:T(8,128)S(1)}, u32[]{:S(2)}, u32[]{:S(2)}) %collective-permute-start.4) | collective-permute-done | bytes 131104 | tf_op jit(solution)/shard_map/ppermute | solution.py:589
  31.4 0.1 combine.1
  31.6 1.6 %collective-permute-start.5 = (f32[968,256]{1,0:T(8,128)S(1)}, f32[968,256]{1,0:T(8,128)S(1)}, u32[]{:S(2)}, u32[]{:S(2)}) collective-permute-start(f32[968,256]{1,0:T(8,128)S(1)} %get-tuple-element.37), channel_id=1, source_target_pairs={{0,2},{1,3},{2,0},{3,1},{4,6},{5,7},{6,4},{7,5},{8,10},{9,11},{10,... | collective-permute-start | bytes 2973704 | tf_op jit(solution)/shard_map/ppermute | solution.py:589
  33.1 18.0 %moments_own.1 = (f32[14,64,256]{2,1,0:T(8,128)S(1)}, f32[7,64,256]{2,1,0:T(8,128)S(1)}, f32[7,64,256]{2,1,0:T(8,128)S(1)}, f32[8,128]{1,0:T(8,128)}) custom-call(f32[5,48,128]{2,1,0:T(8,128)S(1)} %get-tuple-element.23.limits_ref.refs_0_, f32[64,128]{1,0:T(8,128)S(1)} %get-tuple-element.21.refs_2_.cosine_ref.refs_1_, f32[48,64,1024]{2,1,0:T(8,128)} %refs_2_.1, ...), custom_call_target="tpu_custom_call" | custom-call | flops 1 | bytes 1 | tf_op jit(solution)/shard_map/moments_own/pallas_call | solution.py:370
  51.1 0.1 collective-permute-start.6
  51.2 0.5 collective-permute-start.7
  51.7 1.3 %collective-permute-done.6.refs_1_ = f32[7,64,256]{2,1,0:T(8,128)S(1)} collective-permute-done((f32[7,64,256]{2,1,0:T(8,128)S(1)}, f32[7,64,256]{2,1,0:T(8,128)S(1)}, u32[]{:S(2)}, u32[]{:S(2)}) %collective-permute-start.6) | collective-permute-done | bytes 458784 | tf_op jit(solution)/shard_map/ppermute | solution.py:589
  53.0 0.7 %collective-permute-done.7.refs_2_ = f32[7,64,256]{2,1,0:T(8,128)S(1)} collective-permute-done((f32[7,64,256]{2,1,0:T(8,128)S(1)}, f32[7,64,256]{2,1,0:T(8,128)S(1)}, u32[]{:S(2)}, u32[]{:S(2)}) %collective-permute-start.7) | collective-permute-done | bytes 458784 | tf_op jit(solution)/shard_map/ppermute | solution.py:589
  53.7 1.9 %collective-permute-done.5.refs_0_ = f32[968,256]{1,0:T(8,128)S(1)} collective-permute-done((f32[968,256]{1,0:T(8,128)S(1)}, f32[968,256]{1,0:T(8,128)S(1)}, u32[]{:S(2)}, u32[]{:S(2)}) %collective-permute-start.5) | collective-permute-done | bytes 991264 | tf_op jit(solution)/shard_map/ppermute | solution.py:589
  55.6 1.8 %finish.1 = (f32[64,256]{1,0:T(8,128)}, f32[10,64,256]{2,1,0:T(8,128)}) custom-call(f32[64,128]{1,0:T(8,128)S(1)} %get-tuple-element.21.refs_2_.cosine_ref.refs_1_, f32[14,64,256]{2,1,0:T(8,128)S(1)} %get-tuple-element.36.mine_ref, f32[2,64,256]{2,1,0:T(8,128)S(1)} %get-tuple-element.32.refs_2_.edge_mine_ref, ...), custom_call_target="tpu_custom_call" | custom-call | flops 1 | bytes 1 | tf_op jit(solution)/shard_map/finish/pallas_call | solution.py:572
Async XLA Ops:
  0.6 8.1 %copy-start.1 = (f32[48]{0:T(128)S(1)}, f32[48]{0:T(128)}, u32[]{:S(2)}) copy-start(f32[48]{0:T(128)} %refs_0_.1) | copy-start | bytes 580
  0.6 8.1 %copy-start = (s32[48,4]{0,1:T(4,128)S(1)}, s32[48,4]{0,1:T(4,128)}, u32[]{:S(2)}) copy-start(s32[48,4]{0,1:T(4,128)} %param.5) | copy-start | bytes 2308
  2.8 24.6 %collective-permute-start.2 = (f32[2,48,1024]{2,1,0:T(8,128)S(1)}, f32[2,48,1024]{2,1,0:T(8,128)S(1)}, u32[]{:S(2)}, u32[]{:S(2)}) collective-permute-start(f32[2,48,1024]{2,1,0:T(8,128)S(1)} %get-tuple-element.28.bottom_ref), channel_id=1, source_target_pairs={{0,4},{4,8},{8,12},{12,16},{16,20},{20,24},{24,28},{1,5},{5,9},{9,... | collective-permute-start | bytes 1179656 | tf_op jit(solution)/shard_map/ppermute | solution.py:600
  6.3 21.2 %collective-permute-start.3 = (f32[2,48,1024]{2,1,0:T(8,128)S(1)}, f32[2,48,1024]{2,1,0:T(8,128)S(1)}, u32[]{:S(2)}, u32[]{:S(2)}) collective-permute-start(f32[2,48,1024]{2,1,0:T(8,128)S(1)} %get-tuple-element.29.top_ref), channel_id=1, source_target_pairs={{4,0},{8,4},{12,8},{16,12},{20,16},{24,20},{28,24},{5,1},{9,5},{13... | collective-permute-start | bytes 1179656 | tf_op jit(solution)/shard_map/ppermute | solution.py:601
  26.9 3.3 %collective-permute-start = (f32[7,64,256]{2,1,0:T(8,128)S(1)}, f32[7,64,256]{2,1,0:T(8,128)S(1)}, u32[]{:S(2)}, u32[]{:S(2)}) collective-permute-start(f32[7,64,256]{2,1,0:T(8,128)S(1)} %get-tuple-element.25), channel_id=1, source_target_pairs={{0,1},{1,0},{2,3},{3,2},{4,5},{5,4},{6,7},{7,6},{8,9},{9,8},{10,11... | collective-permute-start | bytes 1376264 | tf_op jit(solution)/shard_map/ppermute | solution.py:589
  27.0 3.2 %collective-permute-start.1 = (f32[7,64,256]{2,1,0:T(8,128)S(1)}, f32[7,64,256]{2,1,0:T(8,128)S(1)}, u32[]{:S(2)}, u32[]{:S(2)}) collective-permute-start(f32[7,64,256]{2,1,0:T(8,128)S(1)} %get-tuple-element.26), channel_id=1, source_target_pairs={{0,1},{1,0},{2,3},{3,2},{4,5},{5,4},{6,7},{7,6},{8,9},{9,8},{10,11... | collective-permute-start | bytes 1376264 | tf_op jit(solution)/shard_map/ppermute | solution.py:589
  30.0 1.4 %collective-permute-start.4 = (f32[2,64,256]{2,1,0:T(8,128)S(1)}, f32[2,64,256]{2,1,0:T(8,128)S(1)}, u32[]{:S(2)}, u32[]{:S(2)}) collective-permute-start(f32[2,64,256]{2,1,0:T(8,128)S(1)} %get-tuple-element.33), channel_id=1, source_target_pairs={{0,1},{1,0},{2,3},{3,2},{4,5},{5,4},{6,7},{7,6},{8,9},{9,8},{10,11... | collective-permute-start | bytes 393224 | tf_op jit(solution)/shard_map/ppermute | solution.py:589
  31.6 24.0 %collective-permute-start.5 = (f32[968,256]{1,0:T(8,128)S(1)}, f32[968,256]{1,0:T(8,128)S(1)}, u32[]{:S(2)}, u32[]{:S(2)}) collective-permute-start(f32[968,256]{1,0:T(8,128)S(1)} %get-tuple-element.37), channel_id=1, source_target_pairs={{0,2},{1,3},{2,0},{3,1},{4,6},{5,7},{6,4},{7,5},{8,10},{9,11},{10,... | collective-permute-start | bytes 2973704 | tf_op jit(solution)/shard_map/ppermute | solution.py:589
  51.1 1.9 %collective-permute-start.6 = (f32[7,64,256]{2,1,0:T(8,128)S(1)}, f32[7,64,256]{2,1,0:T(8,128)S(1)}, u32[]{:S(2)}, u32[]{:S(2)}) collective-permute-start(f32[7,64,256]{2,1,0:T(8,128)S(1)} %get-tuple-element.38), channel_id=1, source_target_pairs={{0,1},{1,0},{2,3},{3,2},{4,5},{5,4},{6,7},{7,6},{8,9},{9,8},{10,11... | collective-permute-start | bytes 1376264 | tf_op jit(solution)/shard_map/ppermute | solution.py:589
  51.2 2.5 %collective-permute-start.7 = (f32[7,64,256]{2,1,0:T(8,128)S(1)}, f32[7,64,256]{2,1,0:T(8,128)S(1)}, u32[]{:S(2)}, u32[]{:S(2)}) collective-permute-start(f32[7,64,256]{2,1,0:T(8,128)S(1)} %get-tuple-element.39), channel_id=1, source_target_pairs={{0,1},{1,0},{2,3},{3,2},{4,5},{5,4},{6,7},{7,6},{8,9},{9,8},{10,11... | collective-permute-start | bytes 1376264 | tf_op jit(solution)/shard_map/ppermute | solution.py:589

commit v6 on v5

--- a/solution.py
+++ b/solution.py
@@ -56,7 +56,8 @@
 
 
 def halo_kernel(
-    strips_ref, top_ref, bottom_ref, inner_ref, cosine_ref, token_ref, first_ref, last_ref, sems
+    strips_ref, top_ref, bottom_ref, inner_ref, cosine_ref, weights_ref, token_ref,
+    first_ref, last_ref, sems,
 ):
     token_ref[...] = jnp.zeros((SUB, LANES), F32)
     strip_count, row_block, col_count = strips_ref.shape
@@ -71,6 +72,7 @@
             )
     for copy in copies:
         copy.start()
+    weights_ref[...] = column_weights()
     total_rows = row_block * lax.axis_size("tile")
     row_start = lax.axis_index("tile") * row_block
     for tile in range(row_block // SUB):
@@ -100,13 +102,14 @@
     pair = jax.ShapeDtypeStruct((2, strip_count, col_count), F32)
     inner = jax.ShapeDtypeStruct((4, strip_count, col_count), F32)
     cosine = jax.ShapeDtypeStruct((row_block, LANES), F32)
+    weights = jax.ShapeDtypeStruct((4 * LANES, 2 * LANES), jnp.bfloat16)
     vmem = pl.BlockSpec(memory_space=pltpu.VMEM)
     hbm = pl.BlockSpec(memory_space=pltpu.HBM)
     return pl.pallas_call(
         halo_kernel,
-        out_shape=(pair, pair, inner, cosine, jax.ShapeDtypeStruct((SUB, LANES), F32)),
+        out_shape=(pair, pair, inner, cosine, weights, jax.ShapeDtypeStruct((SUB, LANES), F32)),
         in_specs=[hbm],
-        out_specs=(vmem,) * 5,
+        out_specs=(vmem,) * 6,
         scratch_shapes=[
             pltpu.VMEM((tiles, strip_count, SUB, LANES), F32),
             pltpu.VMEM((tiles, strip_count, SUB, LANES), F32),
@@ -140,15 +143,15 @@
         ]
         refs = refs[2:-3]
     else:
-        limits_ref = refs[0]
-        refs = refs[1:]
-    cosine_ref, strips_ref, first_order_ref, second_order_ref, mine_ref = refs[:5]
-    refs = refs[5:]
+        limits_ref, row_mask = refs[:2]
+        refs = refs[2:]
+    cosine_ref, weights, strips_ref, first_order_ref, second_order_ref, mine_ref = refs[:6]
+    refs = refs[6:]
     other_refs, token_ref = refs[:pieces], refs[pieces]
     if spread:
-        limits_ref, compact_ref = refs[pieces + 1:pieces + 3]
-        refs = refs[2:]
-    elevation, high_part, low_part, row_mask, col_mask, weights, first_slot, second_slot, sems = refs[pieces + 1:]
+        limits_ref, compact_ref, row_mask = refs[pieces + 1:pieces + 4]
+        refs = refs[3:]
+    elevation, high_part, low_part, col_mask, first_slot, second_slot, sems = refs[pieces + 1:]
     del first_order_ref, second_order_ref
     token_ref[...] = jnp.zeros((SUB, LANES), F32)
     strip_count, row_block, col_count = strips_ref.shape
@@ -222,8 +225,6 @@
     blank(0)
     blank(half + 1)
 
-    weights[...] = column_weights()
-
     def spread_out(strip, rows):
         here = pl.ds(strip, 1)
         values = [ranges_ref[kind, strip].astype(F32) for kind in range(4)] + [quality_ref[strip]]
@@ -244,7 +245,7 @@
         row_low, row_high, col_low, col_high, quality = (
             limits_ref[kind, pl.ds(strip, 1), :] for kind in range(5)
         )
-        for tile in range(row_count // SUB):
+        for tile in range(row_count // SUB if spread else 0):
             row = (lax.broadcasted_iota(jnp.int32, (SUB, LANES), 0) + (row_start + tile * SUB)).astype(F32)
             row_mask[strip, tile * SUB:(tile + 1) * SUB, :] = jnp.where(
                 (row >= row_low) & (row < row_high), quality, 0.0
@@ -354,8 +355,7 @@
     column_tile(1, later + 2, None, store_mine, slice(LANES, 2 * LANES))
 
 
-def moments_of(limits, cosine, strips, order, remote, first_row, row_count, pieces):
-    spread = len(limits) == 2
+def moments_of(limits, spread, cosine, weights, strips, order, remote, first_row, row_count, pieces):
     strip_count, row_block, col_count = strips.shape
     half = col_count // LANES // 2
     out = jax.ShapeDtypeStruct((MOMENTS, row_count, col_count // 4), F32)
@@ -365,20 +365,19 @@
     anywhere = pl.BlockSpec(memory_space=pl.ANY)
     lanes = jax.ShapeDtypeStruct((5, strip_count, LANES), F32)
     compact = jax.ShapeDtypeStruct((SUB, 2 * LANES), F32)
+    mask = jax.ShapeDtypeStruct((strip_count, row_count, LANES), F32)
     parts = pltpu.VMEM((strip_count, half + 2, row_count, LANES), jnp.bfloat16)
     slot = pltpu.VMEM((strip_count, row_count, 2 * LANES), F32)
     return pl.pallas_call(
         functools.partial(moment_kernel, remote=remote, first_row=first_row, row_count=row_count, pieces=pieces, spread=spread),
-        out_shape=(out,) + (piece,) * pieces + (token,) + (lanes, compact) * spread,
-        in_specs=[anywhere] * 2 * spread + [vmem] * (2 - spread) + [anywhere, vmem, vmem],
-        out_specs=(vmem,) * (pieces + 2 + 2 * spread),
+        out_shape=(out,) + (piece,) * pieces + (token,) + (lanes, compact, mask) * spread,
+        in_specs=[anywhere if spread else vmem] * 2 + [vmem, vmem, anywhere, vmem, vmem],
+        out_specs=(vmem,) * (pieces + 2 + 3 * spread),
         scratch_shapes=[
             pltpu.VMEM((strip_count, half + 2, row_count + 2 * SUB, LANES), F32),
             parts,
             parts,
-            pltpu.VMEM((strip_count, row_count, LANES), F32),
             pltpu.VMEM((strip_count, half, SUB, LANES), F32),
-            pltpu.VMEM((4 * LANES, 2 * LANES), jnp.bfloat16),
             slot,
             slot,
             pltpu.SemaphoreType.DMA((half + 2, LOAD_PARTS)),
@@ -392,14 +391,14 @@
         compiler_params=pltpu.CompilerParams(vmem_limit_bytes=VMEM_BYTES),
         cost_estimate=SMALL_COST,
         name="moments_remote" if remote else "moments_own",
-    )(*limits, cosine, strips, *order)
+    )(*limits, cosine, weights, strips, *order)
 
 
 def edge_kernel(
     limits_ref, compact_ref, cosine_ref, above_ref, top_ref, inner_ref, bottom_ref, below_ref,
-    first_order_ref, second_order_ref, mine_ref, other_ref, token_ref,
+    order_ref, mine_ref, other_ref, token_ref, *, remote,
 ):
-    del first_order_ref, second_order_ref
+    del order_ref
     token_ref[...] = jnp.zeros((SUB, LANES), F32)
     pair, strip_count, col_count = top_ref.shape
     row_block = cosine_ref.shape[0]
@@ -414,7 +413,7 @@
     sources += [(inner_ref, 2), (inner_ref, 3), (bottom_ref, 0), (bottom_ref, 1), (below_ref, 0), (below_ref, 1)]
     edges = ((0, 2), (1, 3), (row_block - 2, 8), (row_block - 1, 9))
     for out_ref, owner in ((mine_ref, core), (other_ref, 1 - core)):
-        for part, owner_side in enumerate((1 - side, side)):
+        for part, owner_side in enumerate((1 - side if remote else side,)):
             out_ref[part, MOMENTS * EDGE_ROWS:MOMENTS * EDGE_ROWS + SUB, :] = compact_ref[...]
 
             def column_tile(tile, carry, out_ref=out_ref, part=part, first=(owner_side * 2 + owner) * quarter):
@@ -457,19 +456,19 @@
             lax.fori_loop(0, quarter, column_tile, 0)
 
 
-def edge_moments(limits, compact, cosine, above, top, inner, bottom, below, *order):
+def edge_moments(limits, compact, cosine, above, top, inner, bottom, below, order, remote):
     pair, strip_count, col_count = top.shape
-    out = jax.ShapeDtypeStruct((2, MOMENTS * EDGE_ROWS + SUB, col_count // 4), F32)
+    out = jax.ShapeDtypeStruct((1, MOMENTS * EDGE_ROWS + SUB, col_count // 4), F32)
     vmem = pl.BlockSpec(memory_space=pltpu.VMEM)
     return pl.pallas_call(
-        edge_kernel,
+        functools.partial(edge_kernel, remote=remote),
         out_shape=(out, out, jax.ShapeDtypeStruct((SUB, LANES), F32)),
-        in_specs=[vmem] * 10,
+        in_specs=[vmem] * 9,
         out_specs=(vmem, vmem, vmem),
         compiler_params=pltpu.CompilerParams(vmem_limit_bytes=SMALL_VMEM_BYTES),
         cost_estimate=SMALL_COST,
-        name="moments_edge",
-    )(limits, compact, cosine, above, top, inner, bottom, below, *order)
+        name="edges_remote" if remote else "edges_own",
+    )(limits, compact, cosine, above, top, inner, bottom, below, order)
 
 
 def combine_kernel(mine_ref, *refs, pieces, edges):
@@ -505,8 +504,8 @@
 
 
 def finish_kernel(pieces, cosine_ref, mine_ref, edge_mine_ref, edge_core_ref, *refs):
-    far_refs, core_refs = refs[:len(pieces)], refs[len(pieces):-3]
-    mean_ref, covariance_ref, available_ref = refs[-3:]
+    far_refs, core_refs = refs[:len(pieces)], refs[len(pieces):-6]
+    mean_out, covariance_out, mean_ref, covariance_ref, available_ref, sems = refs[-6:]
     row_block, width = mean_ref.shape
     share = MOMENTS // len(core_refs)
     edge_start = MOMENTS * row_block
@@ -515,7 +514,7 @@
     at_col = lax.broadcasted_iota(jnp.int32, (width, LANES), 0) + lax.axis_index("acq") * width
     at_row, at_col = at_row.astype(F32), at_col.astype(F32)
     near_start = compact_start - edge_start
-    compacts = [ref[1, near_start:near_start + SUB, :LANES] for ref in (edge_mine_ref, edge_core_ref)]
+    compacts = [ref[0, near_start:near_start + SUB, :LANES] for ref in (edge_mine_ref, edge_core_ref)]
     compacts += [far_refs[-1][compact_start + SUB * part:compact_start + SUB * (part + 1), :LANES] for part in range(2)]
     rows_in, cols_in = [], []
     for compact in compacts:
@@ -529,6 +528,7 @@
     available_ref[...] = available
     sub = lax.broadcasted_iota(jnp.int32, (SUB, LANES), 0)
     piece_rows = row_block // len(pieces)
+    copies = []
     for first_row, far_ref in zip(pieces, far_refs):
         for tile_row in range(first_row, first_row + piece_rows, SUB):
             rows = slice(tile_row, tile_row + SUB)
@@ -546,7 +546,7 @@
                         spot = moment * EDGE_ROWS + edge
                         edge_far = far_refs[-1][edge_start + spot:edge_start + spot + 1, lanes]
                         spot = slice(spot, spot + 1)
-                        line = (edge_mine_ref[1, spot, lanes] + edge_core_ref[1, spot, lanes]) + edge_far
+                        line = (edge_mine_ref[0, spot, lanes] + edge_core_ref[0, spot, lanes]) + edge_far
                         value = jnp.where(sub == at, line, value)
                     return value
 
@@ -563,6 +563,19 @@
                             total(FEATURES + entry) * inverse * scale - means[first] * means[second]
                         )
                         entry += 1
+            if (tile_row + SUB) % (row_block // 2) == 0:
+                which = tile_row // (row_block // 2)
+                block = pl.ds(which * (row_block // 2), row_block // 2)
+                copies += [
+                    pltpu.make_async_copy(mean_ref.at[block], mean_out.at[block], sems.at[0, which]),
+                    pltpu.make_async_copy(
+                        covariance_ref.at[:, block], covariance_out.at[:, block], sems.at[1, which]
+                    ),
+                ]
+                for copy in copies[-2:]:
+                    copy.start()
+    for copy in copies:
+        copy.wait()
 
 
 def finish(pieces, cosine, mine, edge_mine, edge_core, far, core):
@@ -576,8 +589,13 @@
             jax.ShapeDtypeStruct((entries, row_block, width), F32),
         ),
         in_specs=[vmem] * (4 + len(far) + len(core)),
-        out_specs=(vmem, vmem),
-        scratch_shapes=[pltpu.VMEM((row_block, width), F32)],
+        out_specs=(pl.BlockSpec(memory_space=pl.ANY),) * 2,
+        scratch_shapes=[
+            pltpu.VMEM((row_block, width), F32),
+            pltpu.VMEM((entries, row_block, width), F32),
+            pltpu.VMEM((row_block, width), F32),
+            pltpu.SemaphoreType.DMA((2, 2)),
+        ],
         compiler_params=pltpu.CompilerParams(vmem_limit_bytes=SMALL_VMEM_BYTES),
         cost_estimate=SMALL_COST,
         name="finish",
@@ -594,28 +612,29 @@
     tile_count = lax.axis_size("tile")
     ranges = valid_ranges.T
 
-    top, bottom, inner, cosine, token = halo_rows(strips)
+    top, bottom, inner, cosine, weights, token = halo_rows(strips)
     forward = [(i, i + 1) for i in range(tile_count - 1)]
     backward = [(target, source) for source, target in forward]
     above = lax.ppermute(bottom, "tile", forward)
     below = lax.ppermute(top, "tile", backward)
 
-    def compute(order, remote, first_row, row_count, source):
-        return moments_of(source, cosine, strips, order, remote, first_row, row_count, PIECES)
+    def compute(order, remote, source):
+        return moments_of(source, remote, cosine, weights, strips, order, remote, 0, row_block, PIECES)
+
+    def edges(order, remote):
+        return edge_moments(limits, compact, cosine, above, top, inner, bottom, below, order, remote)
 
     def swap(parts):
         return [exchange(part, 1) for part in parts]
 
-    mine, *other, token, limits, compact = compute((token, token), True, 0, row_block, (strip_quality, ranges))
+    mine, *other, token, limits, compact, mask = compute((token, token), True, (strip_quality, ranges))
     near = swap(other)
-    edge_mine, edge_other, token = edge_moments(
-        limits, compact, cosine, above, top, inner, bottom, below, token, token
-    )
-    edge_core = exchange(edge_other, 1)
-    payload, token = combine(mine, near, (edge_mine, edge_core), (token,))
+    edge_mine, edge_other, token = edges(token, True)
+    payload, token = combine(mine, near, (edge_mine, exchange(edge_other, 1)), (token,))
     far = exchange(payload, 2)
-    mine, *other, token = compute((token, token), False, 0, row_block, (limits,))
-    return finish((0,), cosine, mine, edge_mine, edge_core, [far], swap(other))
+    edge_mine, edge_other, token = edges(token, False)
+    mine, *other, token = compute((token, token), False, (limits, mask))
+    return finish((0,), cosine, mine, edge_mine, exchange(edge_other, 1), [far], swap(other))
 
 
 def solution(mesh):

time: 58.5 us -> 57.3 us (0.979)
  waiting for transfers between devices: 5.18 us -> 3.79 us
    ppermute x6 -> x7, waiting for transfers between devices: 5.17 us -> 3.78 us  [exchange(): lax.ppermute(value, 'acq', [(source, source ^ distance) for source in ran...]
    ppermute x6 -> x7, starting transfers between devices: 2.84 us -> 2.89 us  [exchange(): lax.ppermute(value, 'acq', [(source, source ^ distance) for source in ran...]
    pallas_call x2 -> x3, Pallas kernels: 4.71 us -> 4.71 us  [the longest x2 2.54 us: edge_moments(): pl.pallas_call(functools.partial(edge_kernel, remote=remote), out_shape=(...]
  transfers between devices with their start and end apart: 8 -> 9, of which waited for: 4 -> 3; matrix products, arithmetic and copies ran while one was open for 0% -> 0% of each run, Pallas kernels for 67% -> 69%
where the time goes in v6:
time: 57.3 us; the launch traced here: 56.2 us
  Pallas kernels  42.9 us (75%)
  starting transfers between devices  8.73 us (15%)
  waiting for transfers between devices  3.79 us (7%)
  between operations  0.74 us (1%)
    pallas_call x2, Pallas kernels, moments_of(): pl.pallas_call(functools.partial(moment_kernel, remote=remote, first_row=...  36.3 us
    ppermute x7, waiting for transfers between devices, exchange(): lax.ppermute(value, 'acq', [(source, source ^ distance) for source in ran...  3.78 us
    ppermute x1, starting transfers between devices, local(): above = lax.ppermute(bottom, 'tile', forward)  3.43 us
    ppermute x7, starting transfers between devices, exchange(): lax.ppermute(value, 'acq', [(source, source ^ distance) for source in ran...  2.89 us
    pallas_call x2, Pallas kernels, edge_moments(): pl.pallas_call(functools.partial(edge_kernel, remote=remote), out_shape=(...  2.54 us
    ppermute x1, starting transfers between devices, local(): below = lax.ppermute(top, 'tile', backward)  2.41 us
    pallas_call x1, Pallas kernels, halo_rows(): pl.pallas_call(halo_kernel, out_shape=(pair, pair, inner, cosine, weights...  2.17 us
    pallas_call x1, Pallas kernels, finish(): pl.pallas_call(functools.partial(finish_kernel, pieces), out_shape=(jax.S...  1.76 us
  transfers between devices with their start and end apart: 9, of which 3 were waited for; matrix products, arithmetic and copies ran while one was open for 0% of the time, Pallas kernels for 69%

profile of v6, /device:TPU:12, one launch (start us, length us, event | category | flops | bytes accessed | tf_op | source)
XLA Modules:
  0.0 56.2 jit_solution(7645668036821503327)
XLA Ops:
  0.6 0.0 copy-start
  0.6 0.0 copy-start.1
  0.6 2.2 %halo_rows.1 = (f32[2,48,1024]{2,1,0:T(8,128)S(1)}, f32[2,48,1024]{2,1,0:T(8,128)S(1)}, f32[4,48,1024]{2,1,0:T(8,128)S(1)}, f32[64,128]{1,0:T(8,128)S(1)}, bf16[...) custom-call(f32[48,64,1024]{2,1,0:T(8,128)} %refs_4_.3), custom_call_target="tpu_custom_call" | custom-call | flops 1 | bytes 1 | tf_op jit(solution)/shard_map/halo_rows/pallas_call | solution.py:108
  2.8 3.4 %collective-permute-start = (f32[2,48,1024]{2,1,0:T(8,128)S(1)}, f32[2,48,1024]{2,1,0:T(8,128)S(1)}, u32[]{:S(2)}, u32[]{:S(2)}) collective-permute-start(f32[2,48,1024]{2,1,0:T(8,128)S(1)} %get-tuple-element.32.bottom_ref), channel_id=1, source_target_pairs={{0,4},{4,8},{8,12},{12,16},{16,20},{20,24},{24,28},{1,5},{5,9},{9,... | collective-permute-start | bytes 1179656 | tf_op jit(solution)/shard_map/ppermute | solution.py:618
  6.3 2.4 %collective-permute-start.1 = (f32[2,48,1024]{2,1,0:T(8,128)S(1)}, f32[2,48,1024]{2,1,0:T(8,128)S(1)}, u32[]{:S(2)}, u32[]{:S(2)}) collective-permute-start(f32[2,48,1024]{2,1,0:T(8,128)S(1)} %get-tuple-element.33.top_ref), channel_id=1, source_target_pairs={{4,0},{8,4},{12,8},{16,12},{20,16},{24,20},{28,24},{5,1},{9,5},{13... | collective-permute-start | bytes 1179656 | tf_op jit(solution)/shard_map/ppermute | solution.py:619
  8.7 0.0 copy-done
  8.7 0.0 copy-done.1
  8.7 18.3 %moments_remote.1 = (f32[14,64,256]{2,1,0:T(8,128)S(1)}, f32[7,64,256]{2,1,0:T(8,128)S(1)}, f32[7,64,256]{2,1,0:T(8,128)S(1)}, f32[8,128]{1,0:T(8,128)S(1)}, f32...) custom-call(f32[48]{0:T(128)S(1)} %copy-done.1, s32[4,48]{1,0:T(4,128)S(1)} %bitcast.1, ...), custom_call_target="tpu_custom_call" | custom-call | flops 1 | bytes 1 | tf_op jit(solution)/shard_map/moments_remote/pallas_call | solution.py:371
  27.0 0.1 collective-permute-start.2
  27.1 0.5 collective-permute-start.3
  27.6 0.0 collective-permute-done.above_ref
  27.6 0.0 collective-permute-done.1.below_ref
  27.6 1.3 %edges_remote.1 = (f32[1,64,256]{2,1,0:T(8,128)S(1)}, f32[1,64,256]{2,1,0:T(8,128)S(1)}, f32[8,128]{1,0:T(8,128)S(1)}) custom-call(f32[5,48,128]{2,1,0:T(8,128)S(1)} %get-tuple-element.29.limits_ref.refs_0_, f32[8,256]{1,0:T(8,128)S(1)} %get-tuple-element.31.compact_ref, f32[64,128]{1,0:T(8,128)S(1)} %get-tuple-element.26.refs_2_.cosine_ref, ...), custom_call_target="tpu_custom_call" | custom-call | flops 1 | bytes 1 | tf_op jit(solution)/shard_map/edges_remote/pallas_call | solution.py:463
  28.9 0.1 collective-permute-start.4
  29.1 1.2 %collective-permute-done.4.refs_3_ = f32[1,64,256]{2,1,0:T(8,128)S(1)} collective-permute-done((f32[1,64,256]{2,1,0:T(8,128)S(1)}, f32[1,64,256]{2,1,0:T(8,128)S(1)}, u32[]{:S(2)}, u32[]{:S(2)}) %collective-permute-start.4) | collective-permute-done | bytes 65568 | tf_op jit(solution)/shard_map/ppermute | solution.py:607
  30.2 0.0 collective-permute-done.2.refs_0_
  30.2 0.0 collective-permute-done.3.refs_1_
  30.2 0.1 combine.1
  30.4 1.5 %collective-permute-start.6 = (f32[968,256]{1,0:T(8,128)S(1)}, f32[968,256]{1,0:T(8,128)S(1)}, u32[]{:S(2)}, u32[]{:S(2)}) collective-permute-start(f32[968,256]{1,0:T(8,128)S(1)} %get-tuple-element.47), channel_id=1, source_target_pairs={{0,2},{1,3},{2,0},{3,1},{4,6},{5,7},{6,4},{7,5},{8,10},{9,11},{10,... | collective-permute-start | bytes 2973704 | tf_op jit(solution)/shard_map/ppermute | solution.py:607
  31.9 1.3 %edges_own.1 = (f32[1,64,256]{2,1,0:T(8,128)S(1)}, f32[1,64,256]{2,1,0:T(8,128)S(1)}, f32[8,128]{1,0:T(8,128)S(1)}) custom-call(f32[5,48,128]{2,1,0:T(8,128)S(1)} %get-tuple-element.29.limits_ref.refs_0_, f32[8,256]{1,0:T(8,128)S(1)} %get-tuple-element.31.compact_ref, f32[64,128]{1,0:T(8,128)S(1)} %get-tuple-element.26.refs_2_.cosine_ref, ...), custom_call_target="tpu_custom_call" | custom-call | flops 1 | bytes 1 | tf_op jit(solution)/shard_map/edges_own/pallas_call | solution.py:463
  33.2 18.0 %moments_own.1 = (f32[14,64,256]{2,1,0:T(8,128)S(1)}, f32[7,64,256]{2,1,0:T(8,128)S(1)}, f32[7,64,256]{2,1,0:T(8,128)S(1)}, f32[8,128]{1,0:T(8,128)}) custom-call(f32[5,48,128]{2,1,0:T(8,128)S(1)} %get-tuple-element.29.limits_ref.refs_0_, f32[48,64,128]{2,1,0:T(8,128)S(1)} %get-tuple-element.30.refs_1_, f32[64,128]{1,0:T(8,128)S(1)} %get-tuple-element.26.refs_2_.cosine_ref, ...), custom_call_target="tpu_custom_call" | custom-call | flops 1 | bytes 1 | tf_op jit(solution)/shard_map/moments_own/pallas_call | solution.py:371
  51.2 0.1 collective-permute-start.7
  51.2 0.5 collective-permute-start.8
  51.7 0.1 collective-permute-start.5
  51.8 2.0 %collective-permute-done.5.edge_core_ref = f32[1,64,256]{2,1,0:T(8,128)S(1)} collective-permute-done((f32[1,64,256]{2,1,0:T(8,128)S(1)}, f32[1,64,256]{2,1,0:T(8,128)S(1)}, u32[]{:S(2)}, u32[]{:S(2)}) %collective-permute-start.5) | collective-permute-done | bytes 65568 | tf_op jit(solution)/shard_map/ppermute | solution.py:607
  53.8 0.0 collective-permute-done.7.refs_1_
  53.8 0.0 collective-permute-done.8.refs_2_
  53.8 0.6 %collective-permute-done.6.refs_0_ = f32[968,256]{1,0:T(8,128)S(1)} collective-permute-done((f32[968,256]{1,0:T(8,128)S(1)}, f32[968,256]{1,0:T(8,128)S(1)}, u32[]{:S(2)}, u32[]{:S(2)}) %collective-permute-start.6) | collective-permute-done | bytes 991264 | tf_op jit(solution)/shard_map/ppermute | solution.py:607
  54.4 1.8 %finish.1 = (f32[64,256]{1,0:T(8,128)}, f32[10,64,256]{2,1,0:T(8,128)}) custom-call(f32[64,128]{1,0:T(8,128)S(1)} %get-tuple-element.26.refs_2_.cosine_ref, f32[14,64,256]{2,1,0:T(8,128)S(1)} %get-tuple-element.44.mine_ref, f32[1,64,256]{2,1,0:T(8,128)S(1)} %get-tuple-element.45.edge_mine_ref, f32[1,64,256]{2,1,0:T(8,128)S(1)} %collective-permute-done.5.edge_core_ref, ...), custom_call_target="tpu_custom_call" | custom-call | flops 1 | bytes 1 | tf_op jit(solution)/shard_map/finish/pallas_call | solution.py:585
Async XLA Ops:
  0.6 8.1 %copy-start = (s32[48,4]{0,1:T(4,128)S(1)}, s32[48,4]{0,1:T(4,128)}, u32[]{:S(2)}) copy-start(s32[48,4]{0,1:T(4,128)} %param.5) | copy-start | bytes 2308
  0.6 8.1 %copy-start.1 = (f32[48]{0:T(128)S(1)}, f32[48]{0:T(128)}, u32[]{:S(2)}) copy-start(f32[48]{0:T(128)} %refs_0_.1) | copy-start | bytes 580
  2.8 24.8 %collective-permute-start = (f32[2,48,1024]{2,1,0:T(8,128)S(1)}, f32[2,48,1024]{2,1,0:T(8,128)S(1)}, u32[]{:S(2)}, u32[]{:S(2)}) collective-permute-start(f32[2,48,1024]{2,1,0:T(8,128)S(1)} %get-tuple-element.32.bottom_ref), channel_id=1, source_target_pairs={{0,4},{4,8},{8,12},{12,16},{16,20},{20,24},{24,28},{1,5},{5,9},{9,... | collective-permute-start | bytes 1179656 | tf_op jit(solution)/shard_map/ppermute | solution.py:618
  6.3 21.4 %collective-permute-start.1 = (f32[2,48,1024]{2,1,0:T(8,128)S(1)}, f32[2,48,1024]{2,1,0:T(8,128)S(1)}, u32[]{:S(2)}, u32[]{:S(2)}) collective-permute-start(f32[2,48,1024]{2,1,0:T(8,128)S(1)} %get-tuple-element.33.top_ref), channel_id=1, source_target_pairs={{4,0},{8,4},{12,8},{16,12},{20,16},{24,20},{28,24},{5,1},{9,5},{13... | collective-permute-start | bytes 1179656 | tf_op jit(solution)/shard_map/ppermute | solution.py:619
  27.0 3.2 %collective-permute-start.2 = (f32[7,64,256]{2,1,0:T(8,128)S(1)}, f32[7,64,256]{2,1,0:T(8,128)S(1)}, u32[]{:S(2)}, u32[]{:S(2)}) collective-permute-start(f32[7,64,256]{2,1,0:T(8,128)S(1)} %get-tuple-element.36), channel_id=1, source_target_pairs={{0,1},{1,0},{2,3},{3,2},{4,5},{5,4},{6,7},{7,6},{8,9},{9,8},{10,11... | collective-permute-start | bytes 1376264 | tf_op jit(solution)/shard_map/ppermute | solution.py:607
  27.1 3.1 %collective-permute-start.3 = (f32[7,64,256]{2,1,0:T(8,128)S(1)}, f32[7,64,256]{2,1,0:T(8,128)S(1)}, u32[]{:S(2)}, u32[]{:S(2)}) collective-permute-start(f32[7,64,256]{2,1,0:T(8,128)S(1)} %get-tuple-element.37), channel_id=1, source_target_pairs={{0,1},{1,0},{2,3},{3,2},{4,5},{5,4},{6,7},{7,6},{8,9},{9,8},{10,11... | collective-permute-start | bytes 1376264 | tf_op jit(solution)/shard_map/ppermute | solution.py:607
  28.9 1.3 %collective-permute-start.4 = (f32[1,64,256]{2,1,0:T(8,128)S(1)}, f32[1,64,256]{2,1,0:T(8,128)S(1)}, u32[]{:S(2)}, u32[]{:S(2)}) collective-permute-start(f32[1,64,256]{2,1,0:T(8,128)S(1)} %get-tuple-element.40), channel_id=1, source_target_pairs={{0,1},{1,0},{2,3},{3,2},{4,5},{5,4},{6,7},{7,6},{8,9},{9,8},{10,11... | collective-permute-start | bytes 196616 | tf_op jit(solution)/shard_map/ppermute | solution.py:607
  30.4 24.1 %collective-permute-start.6 = (f32[968,256]{1,0:T(8,128)S(1)}, f32[968,256]{1,0:T(8,128)S(1)}, u32[]{:S(2)}, u32[]{:S(2)}) collective-permute-start(f32[968,256]{1,0:T(8,128)S(1)} %get-tuple-element.47), channel_id=1, source_target_pairs={{0,2},{1,3},{2,0},{3,1},{4,6},{5,7},{6,4},{7,5},{8,10},{9,11},{10,... | collective-permute-start | bytes 2973704 | tf_op jit(solution)/shard_map/ppermute | solution.py:607
  51.2 2.6 %collective-permute-start.7 = (f32[7,64,256]{2,1,0:T(8,128)S(1)}, f32[7,64,256]{2,1,0:T(8,128)S(1)}, u32[]{:S(2)}, u32[]{:S(2)}) collective-permute-start(f32[7,64,256]{2,1,0:T(8,128)S(1)} %get-tuple-element.48), channel_id=1, source_target_pairs={{0,1},{1,0},{2,3},{3,2},{4,5},{5,4},{6,7},{7,6},{8,9},{9,8},{10,11... | collective-permute-start | bytes 1376264 | tf_op jit(solution)/shard_map/ppermute | solution.py:607
  51.2 2.6 %collective-permute-start.8 = (f32[7,64,256]{2,1,0:T(8,128)S(1)}, f32[7,64,256]{2,1,0:T(8,128)S(1)}, u32[]{:S(2)}, u32[]{:S(2)}) collective-permute-start(f32[7,64,256]{2,1,0:T(8,128)S(1)} %get-tuple-element.49), channel_id=1, source_target_pairs={{0,1},{1,0},{2,3},{3,2},{4,5},{5,4},{6,7},{7,6},{8,9},{9,8},{10,11... | collective-permute-start | bytes 1376264 | tf_op jit(solution)/shard_map/ppermute | solution.py:607
  51.7 2.1 %collective-permute-start.5 = (f32[1,64,256]{2,1,0:T(8,128)S(1)}, f32[1,64,256]{2,1,0:T(8,128)S(1)}, u32[]{:S(2)}, u32[]{:S(2)}) collective-permute-start(f32[1,64,256]{2,1,0:T(8,128)S(1)} %get-tuple-element.46), channel_id=1, source_target_pairs={{0,1},{1,0},{2,3},{3,2},{4,5},{5,4},{6,7},{7,6},{8,9},{9,8},{10,11... | collective-permute-start | bytes 196616 | tf_op jit(solution)/shard_map/ppermute | solution.py:607

commit v7 on v6

--- a/solution.py
+++ b/solution.py
@@ -56,7 +56,7 @@
 
 
 def halo_kernel(
-    strips_ref, top_ref, bottom_ref, inner_ref, cosine_ref, weights_ref, token_ref,
+    strips_ref, first_out, second_out, inner_ref, cosine_ref, weights_ref, token_ref,
     first_ref, last_ref, sems,
 ):
     token_ref[...] = jnp.zeros((SUB, LANES), F32)
@@ -75,6 +75,7 @@
     weights_ref[...] = column_weights()
     total_rows = row_block * lax.axis_size("tile")
     row_start = lax.axis_index("tile") * row_block
+    even = lax.axis_index("tile") % 2 == 0
     for tile in range(row_block // SUB):
         row = lax.broadcasted_iota(jnp.int32, (SUB, LANES), 0) + (row_start + tile * SUB)
         latitude = -1.0 + 2.0 * (row.astype(F32) + 0.5) / total_rows
@@ -90,8 +91,10 @@
             strips = slice(group * SUB, (group + 1) * SUB)
             for row in range(2):
                 at = group * SUB * SUB
-                top_ref[row, strips, lanes] = first_rows[tile, pl.ds(at + row, SUB, stride=SUB), :]
-                bottom_ref[row, strips, lanes] = last_rows[tile, pl.ds(at + 6 + row, SUB, stride=SUB), :]
+                top = first_rows[tile, pl.ds(at + row, SUB, stride=SUB), :]
+                bottom = last_rows[tile, pl.ds(at + 6 + row, SUB, stride=SUB), :]
+                first_out[row, strips, lanes] = jnp.where(even, bottom, top)
+                second_out[row, strips, lanes] = jnp.where(even, top, bottom)
                 inner_ref[row, strips, lanes] = first_rows[tile, pl.ds(at + 2 + row, SUB, stride=SUB), :]
                 inner_ref[2 + row, strips, lanes] = last_rows[tile, pl.ds(at + 4 + row, SUB, stride=SUB), :]
 
@@ -395,13 +398,14 @@
 
 
 def edge_kernel(
-    limits_ref, compact_ref, cosine_ref, above_ref, top_ref, inner_ref, bottom_ref, below_ref,
+    limits_ref, compact_ref, cosine_ref, first_in, second_in, first_out, second_out, inner_ref,
     order_ref, mine_ref, other_ref, token_ref, *, remote,
 ):
     del order_ref
     token_ref[...] = jnp.zeros((SUB, LANES), F32)
-    pair, strip_count, col_count = top_ref.shape
+    pair, strip_count, col_count = first_out.shape
     row_block = cosine_ref.shape[0]
+    even = lax.axis_index("tile") % 2 == 0
     tiles = col_count // LANES
     quarter = tiles // 4
     position = lax.axis_index("acq")
@@ -409,8 +413,11 @@
     core = position % 2
     row_start = lax.axis_index("tile") * row_block
     lane = lax.broadcasted_iota(jnp.int32, (SUB, LANES), 1)
-    sources = [(above_ref, 0), (above_ref, 1), (top_ref, 0), (top_ref, 1), (inner_ref, 0), (inner_ref, 1)]
-    sources += [(inner_ref, 2), (inner_ref, 3), (bottom_ref, 0), (bottom_ref, 1), (below_ref, 0), (below_ref, 1)]
+    above, top = (second_in, first_in), (second_out, first_out)
+    below, bottom = (first_in, second_in), (first_out, second_out)
+    inner = (inner_ref,)
+    sources = [(above, 0), (above, 1), (top, 0), (top, 1), (inner, 0), (inner, 1)]
+    sources += [(inner, 2), (inner, 3), (bottom, 0), (bottom, 1), (below, 0), (below, 1)]
     edges = ((0, 2), (1, 3), (row_block - 2, 8), (row_block - 1, 9))
     for out_ref, owner in ((mine_ref, core), (other_ref, 1 - core)):
         for part, owner_side in enumerate((1 - side if remote else side,)):
@@ -433,8 +440,9 @@
                         strips = slice(group * SUB, (group + 1) * SUB)
 
                         def load(shift, where):
-                            ref, index = sources[source + shift]
-                            return ref[index, strips, where]
+                            refs, index = sources[source + shift]
+                            values = [ref[index, strips, where] for ref in refs]
+                            return jnp.where(even, values[0], values[-1]) if len(refs) == 2 else values[0]
 
                         z = load(0, here)
                         cols = shifted_columns(
@@ -456,8 +464,8 @@
             lax.fori_loop(0, quarter, column_tile, 0)
 
 
-def edge_moments(limits, compact, cosine, above, top, inner, bottom, below, order, remote):
-    pair, strip_count, col_count = top.shape
+def edge_moments(limits, compact, cosine, arrived, sent, inner, order, remote):
+    pair, strip_count, col_count = inner.shape
     out = jax.ShapeDtypeStruct((1, MOMENTS * EDGE_ROWS + SUB, col_count // 4), F32)
     vmem = pl.BlockSpec(memory_space=pltpu.VMEM)
     return pl.pallas_call(
@@ -468,7 +476,7 @@
         compiler_params=pltpu.CompilerParams(vmem_limit_bytes=SMALL_VMEM_BYTES),
         cost_estimate=SMALL_COST,
         name="edges_remote" if remote else "edges_own",
-    )(limits, compact, cosine, above, top, inner, bottom, below, order)
+    )(limits, compact, cosine, *arrived, *sent, inner, order)
 
 
 def combine_kernel(mine_ref, *refs, pieces, edges):
@@ -612,17 +620,18 @@
     tile_count = lax.axis_size("tile")
     ranges = valid_ranges.T
 
-    top, bottom, inner, cosine, weights, token = halo_rows(strips)
-    forward = [(i, i + 1) for i in range(tile_count - 1)]
-    backward = [(target, source) for source, target in forward]
-    above = lax.ppermute(bottom, "tile", forward)
-    below = lax.ppermute(top, "tile", backward)
+    *sent, inner, cosine, weights, token = halo_rows(strips)
+    arrived = []
+    for first, value in enumerate(sent):
+        pairs = [(i, i + 1) for i in range(first, tile_count - 1, 2)]
+        swaps = pairs + [(target, source) for source, target in pairs]
+        arrived.append(lax.ppermute(value, "tile", swaps))
 
     def compute(order, remote, source):
         return moments_of(source, remote, cosine, weights, strips, order, remote, 0, row_block, PIECES)
 
     def edges(order, remote):
-        return edge_moments(limits, compact, cosine, above, top, inner, bottom, below, order, remote)
+        return edge_moments(limits, compact, cosine, arrived, sent, inner, order, remote)
 
     def swap(parts):
         return [exchange(part, 1) for part in parts]

time: 57.3 us -> 55.6 us (0.970); the launches traced: 56.2 us -> 55.4 us
  starting transfers between devices: 8.73 us -> 7.91 us
    ppermute x2, starting transfers between devices: 5.84 us -> 5 us  [local(): arrived.append(lax.ppermute(value, 'tile', swaps))]
  transfers between devices with their start and end apart: 9 -> 9, of which waited for: 3 -> 3; matrix products, arithmetic and copies ran while one was open for 0% -> 0% of each run, Pallas kernels for 69% -> 70%
where the time goes in v7:
time: 55.6 us; the launch traced here: 55.4 us
  Pallas kernels  43 us (77%)
  starting transfers between devices  7.91 us (14%)
  waiting for transfers between devices  3.7 us (7%)
  between operations  0.73 us (1%)
    pallas_call x2, Pallas kernels, moments_of(): pl.pallas_call(functools.partial(moment_kernel, remote=remote, first_row=...  36.3 us
    ppermute x2, starting transfers between devices, local(): arrived.append(lax.ppermute(value, 'tile', swaps))  5 us
    ppermute x7, waiting for transfers between devices, exchange(): lax.ppermute(value, 'acq', [(source, source ^ distance) for source in ran...  3.69 us
    ppermute x7, starting transfers between devices, exchange(): lax.ppermute(value, 'acq', [(source, source ^ distance) for source in ran...  2.91 us
    pallas_call x2, Pallas kernels, edge_moments(): pl.pallas_call(functools.partial(edge_kernel, remote=remote), out_shape=(...  2.68 us
    pallas_call x1, Pallas kernels, halo_rows(): pl.pallas_call(halo_kernel, out_shape=(pair, pair, inner, cosine, weights...  2.16 us
    pallas_call x1, Pallas kernels, finish(): pl.pallas_call(functools.partial(finish_kernel, pieces), out_shape=(jax.S...  1.76 us
  transfers between devices with their start and end apart: 9, of which 3 were waited for; matrix products, arithmetic and copies ran while one was open for 0% of the time, Pallas kernels for 70%

profile of v7, /device:TPU:12, one launch (start us, length us, event | category | flops | bytes accessed | tf_op | source)
XLA Modules:
  0.0 55.4 jit_solution(5201841447927276297)
XLA Ops:
  0.6 0.0 copy-start
  0.6 0.0 copy-start.1
  0.6 2.2 %halo_rows.1 = (f32[2,48,1024]{2,1,0:T(8,128)S(1)}, f32[2,48,1024]{2,1,0:T(8,128)S(1)}, f32[4,48,1024]{2,1,0:T(8,128)S(1)}, f32[64,128]{1,0:T(8,128)S(1)}, bf16[...) custom-call(f32[48,64,1024]{2,1,0:T(8,128)} %refs_4_.3), custom_call_target="tpu_custom_call" | custom-call | flops 1 | bytes 1 | tf_op jit(solution)/shard_map/halo_rows/pallas_call | solution.py:111
  2.8 0.6 %collective-permute-start = (f32[2,48,1024]{2,1,0:T(8,128)S(1)}, f32[2,48,1024]{2,1,0:T(8,128)S(1)}, u32[]{:S(2)}, u32[]{:S(2)}) collective-permute-start(f32[2,48,1024]{2,1,0:T(8,128)S(1)} %get-tuple-element.32.first_out), channel_id=1, source_target_pairs={{0,4},{8,12},{16,20},{24,28},{4,0},{12,8},{20,16},{28,24},{1,5},{9... | collective-permute-start | bytes 1179656 | tf_op jit(solution)/shard_map/ppermute | solution.py:628
  3.4 4.4 %collective-permute-start.1 = (f32[2,48,1024]{2,1,0:T(8,128)S(1)}, f32[2,48,1024]{2,1,0:T(8,128)S(1)}, u32[]{:S(2)}, u32[]{:S(2)}) collective-permute-start(f32[2,48,1024]{2,1,0:T(8,128)S(1)} %get-tuple-element.33.second_out), channel_id=1, source_target_pairs={{4,8},{12,16},{20,24},{8,4},{16,12},{24,20},{5,9},{13,17},{21,25},... | collective-permute-start | bytes 1179656 | tf_op jit(solution)/shard_map/ppermute | solution.py:628
  7.8 0.0 copy-done
  7.8 0.0 copy-done.1
  7.8 18.3 %moments_remote.1 = (f32[14,64,256]{2,1,0:T(8,128)S(1)}, f32[7,64,256]{2,1,0:T(8,128)S(1)}, f32[7,64,256]{2,1,0:T(8,128)S(1)}, f32[8,128]{1,0:T(8,128)S(1)}, f32...) custom-call(f32[48]{0:T(128)S(1)} %copy-done.1, s32[4,48]{1,0:T(4,128)S(1)} %bitcast.1, ...), custom_call_target="tpu_custom_call" | custom-call | flops 1 | bytes 1 | tf_op jit(solution)/shard_map/moments_remote/pallas_call | solution.py:374
  26.2 0.1 collective-permute-start.2
  26.3 0.5 collective-permute-start.3
  26.8 0.0 collective-permute-done.first_in
  26.8 0.0 collective-permute-done.1.second_in
  26.8 1.3 %edges_remote.1 = (f32[1,64,256]{2,1,0:T(8,128)S(1)}, f32[1,64,256]{2,1,0:T(8,128)S(1)}, f32[8,128]{1,0:T(8,128)S(1)}) custom-call(f32[5,48,128]{2,1,0:T(8,128)S(1)} %get-tuple-element.29.limits_ref.refs_0_, f32[8,256]{1,0:T(8,128)S(1)} %get-tuple-element.31.compact_ref, f32[64,128]{1,0:T(8,128)S(1)} %get-tuple-element.26.refs_2_.cosine_ref, ...), custom_call_target="tpu_custom_call" | custom-call | flops 1 | bytes 1 | tf_op jit(solution)/shard_map/edges_remote/pallas_call | solution.py:471
  28.1 0.1 collective-permute-start.4
  28.3 1.2 %collective-permute-done.4.refs_3_ = f32[1,64,256]{2,1,0:T(8,128)S(1)} collective-permute-done((f32[1,64,256]{2,1,0:T(8,128)S(1)}, f32[1,64,256]{2,1,0:T(8,128)S(1)}, u32[]{:S(2)}, u32[]{:S(2)}) %collective-permute-start.4) | collective-permute-done | bytes 65568 | tf_op jit(solution)/shard_map/ppermute | solution.py:615
  29.4 0.0 collective-permute-done.2.refs_0_
  29.4 0.0 collective-permute-done.3.refs_1_
  29.5 0.1 combine.1
  29.6 1.6 %collective-permute-start.6 = (f32[968,256]{1,0:T(8,128)S(1)}, f32[968,256]{1,0:T(8,128)S(1)}, u32[]{:S(2)}, u32[]{:S(2)}) collective-permute-start(f32[968,256]{1,0:T(8,128)S(1)} %get-tuple-element.47), channel_id=1, source_target_pairs={{0,2},{1,3},{2,0},{3,1},{4,6},{5,7},{6,4},{7,5},{8,10},{9,11},{10,... | collective-permute-start | bytes 2973704 | tf_op jit(solution)/shard_map/ppermute | solution.py:615
  31.1 1.3 %edges_own.1 = (f32[1,64,256]{2,1,0:T(8,128)S(1)}, f32[1,64,256]{2,1,0:T(8,128)S(1)}, f32[8,128]{1,0:T(8,128)S(1)}) custom-call(f32[5,48,128]{2,1,0:T(8,128)S(1)} %get-tuple-element.29.limits_ref.refs_0_, f32[8,256]{1,0:T(8,128)S(1)} %get-tuple-element.31.compact_ref, f32[64,128]{1,0:T(8,128)S(1)} %get-tuple-element.26.refs_2_.cosine_ref, ...), custom_call_target="tpu_custom_call" | custom-call | flops 1 | bytes 1 | tf_op jit(solution)/shard_map/edges_own/pallas_call | solution.py:471
  32.5 18.0 %moments_own.1 = (f32[14,64,256]{2,1,0:T(8,128)S(1)}, f32[7,64,256]{2,1,0:T(8,128)S(1)}, f32[7,64,256]{2,1,0:T(8,128)S(1)}, f32[8,128]{1,0:T(8,128)}) custom-call(f32[5,48,128]{2,1,0:T(8,128)S(1)} %get-tuple-element.29.limits_ref.refs_0_, f32[48,64,128]{2,1,0:T(8,128)S(1)} %get-tuple-element.30.refs_1_, f32[64,128]{1,0:T(8,128)S(1)} %get-tuple-element.26.refs_2_.cosine_ref, ...), custom_call_target="tpu_custom_call" | custom-call | flops 1 | bytes 1 | tf_op jit(solution)/shard_map/moments_own/pallas_call | solution.py:374
  50.5 0.1 collective-permute-start.7
  50.6 0.5 collective-permute-start.8
  51.0 0.1 collective-permute-start.5
  51.1 2.0 %collective-permute-done.5.edge_core_ref = f32[1,64,256]{2,1,0:T(8,128)S(1)} collective-permute-done((f32[1,64,256]{2,1,0:T(8,128)S(1)}, f32[1,64,256]{2,1,0:T(8,128)S(1)}, u32[]{:S(2)}, u32[]{:S(2)}) %collective-permute-start.5) | collective-permute-done | bytes 65568 | tf_op jit(solution)/shard_map/ppermute | solution.py:615
  53.1 0.0 collective-permute-done.7.refs_1_
  53.1 0.0 collective-permute-done.8.refs_2_
  53.1 0.5 collective-permute-done.6.refs_0_
  53.6 1.8 %finish.1 = (f32[64,256]{1,0:T(8,128)}, f32[10,64,256]{2,1,0:T(8,128)}) custom-call(f32[64,128]{1,0:T(8,128)S(1)} %get-tuple-element.26.refs_2_.cosine_ref, f32[14,64,256]{2,1,0:T(8,128)S(1)} %get-tuple-element.44.mine_ref, f32[1,64,256]{2,1,0:T(8,128)S(1)} %get-tuple-element.45.edge_mine_ref, f32[1,64,256]{2,1,0:T(8,128)S(1)} %collective-permute-done.5.edge_core_ref, ...), custom_call_target="tpu_custom_call" | custom-call | flops 1 | bytes 1 | tf_op jit(solution)/shard_map/finish/pallas_call | solution.py:593
Async XLA Ops:
  0.6 7.2 %copy-start = (s32[48,4]{0,1:T(4,128)S(1)}, s32[48,4]{0,1:T(4,128)}, u32[]{:S(2)}) copy-start(s32[48,4]{0,1:T(4,128)} %param.5) | copy-start | bytes 2308
  0.6 7.2 %copy-start.1 = (f32[48]{0:T(128)S(1)}, f32[48]{0:T(128)}, u32[]{:S(2)}) copy-start(f32[48]{0:T(128)} %refs_0_.1) | copy-start | bytes 580
  2.8 24.0 %collective-permute-start = (f32[2,48,1024]{2,1,0:T(8,128)S(1)}, f32[2,48,1024]{2,1,0:T(8,128)S(1)}, u32[]{:S(2)}, u32[]{:S(2)}) collective-permute-start(f32[2,48,1024]{2,1,0:T(8,128)S(1)} %get-tuple-element.32.first_out), channel_id=1, source_target_pairs={{0,4},{8,12},{16,20},{24,28},{4,0},{12,8},{20,16},{28,24},{1,5},{9... | collective-permute-start | bytes 1179656 | tf_op jit(solution)/shard_map/ppermute | solution.py:628
  3.4 23.4 %collective-permute-start.1 = (f32[2,48,1024]{2,1,0:T(8,128)S(1)}, f32[2,48,1024]{2,1,0:T(8,128)S(1)}, u32[]{:S(2)}, u32[]{:S(2)}) collective-permute-start(f32[2,48,1024]{2,1,0:T(8,128)S(1)} %get-tuple-element.33.second_out), channel_id=1, source_target_pairs={{4,8},{12,16},{20,24},{8,4},{16,12},{24,20},{5,9},{13,17},{21,25},... | collective-permute-start | bytes 1179656 | tf_op jit(solution)/shard_map/ppermute | solution.py:628
  26.2 3.3 %collective-permute-start.2 = (f32[7,64,256]{2,1,0:T(8,128)S(1)}, f32[7,64,256]{2,1,0:T(8,128)S(1)}, u32[]{:S(2)}, u32[]{:S(2)}) collective-permute-start(f32[7,64,256]{2,1,0:T(8,128)S(1)} %get-tuple-element.36), channel_id=1, source_target_pairs={{0,1},{1,0},{2,3},{3,2},{4,5},{5,4},{6,7},{7,6},{8,9},{9,8},{10,11... | collective-permute-start | bytes 1376264 | tf_op jit(solution)/shard_map/ppermute | solution.py:615
  26.3 3.2 %collective-permute-start.3 = (f32[7,64,256]{2,1,0:T(8,128)S(1)}, f32[7,64,256]{2,1,0:T(8,128)S(1)}, u32[]{:S(2)}, u32[]{:S(2)}) collective-permute-start(f32[7,64,256]{2,1,0:T(8,128)S(1)} %get-tuple-element.37), channel_id=1, source_target_pairs={{0,1},{1,0},{2,3},{3,2},{4,5},{5,4},{6,7},{7,6},{8,9},{9,8},{10,11... | collective-permute-start | bytes 1376264 | tf_op jit(solution)/shard_map/ppermute | solution.py:615
  28.1 1.3 %collective-permute-start.4 = (f32[1,64,256]{2,1,0:T(8,128)S(1)}, f32[1,64,256]{2,1,0:T(8,128)S(1)}, u32[]{:S(2)}, u32[]{:S(2)}) collective-permute-start(f32[1,64,256]{2,1,0:T(8,128)S(1)} %get-tuple-element.40), channel_id=1, source_target_pairs={{0,1},{1,0},{2,3},{3,2},{4,5},{5,4},{6,7},{7,6},{8,9},{9,8},{10,11... | collective-permute-start | bytes 196616 | tf_op jit(solution)/shard_map/ppermute | solution.py:615
  29.6 24.1 %collective-permute-start.6 = (f32[968,256]{1,0:T(8,128)S(1)}, f32[968,256]{1,0:T(8,128)S(1)}, u32[]{:S(2)}, u32[]{:S(2)}) collective-permute-start(f32[968,256]{1,0:T(8,128)S(1)} %get-tuple-element.47), channel_id=1, source_target_pairs={{0,2},{1,3},{2,0},{3,1},{4,6},{5,7},{6,4},{7,5},{8,10},{9,11},{10,... | collective-permute-start | bytes 2973704 | tf_op jit(solution)/shard_map/ppermute | solution.py:615
  50.5 2.6 %collective-permute-start.7 = (f32[7,64,256]{2,1,0:T(8,128)S(1)}, f32[7,64,256]{2,1,0:T(8,128)S(1)}, u32[]{:S(2)}, u32[]{:S(2)}) collective-permute-start(f32[7,64,256]{2,1,0:T(8,128)S(1)} %get-tuple-element.48), channel_id=1, source_target_pairs={{0,1},{1,0},{2,3},{3,2},{4,5},{5,4},{6,7},{7,6},{8,9},{9,8},{10,11... | collective-permute-start | bytes 1376264 | tf_op jit(solution)/shard_map/ppermute | solution.py:615
  50.6 2.6 %collective-permute-start.8 = (f32[7,64,256]{2,1,0:T(8,128)S(1)}, f32[7,64,256]{2,1,0:T(8,128)S(1)}, u32[]{:S(2)}, u32[]{:S(2)}) collective-permute-start(f32[7,64,256]{2,1,0:T(8,128)S(1)} %get-tuple-element.49), channel_id=1, source_target_pairs={{0,1},{1,0},{2,3},{3,2},{4,5},{5,4},{6,7},{7,6},{8,9},{9,8},{10,11... | collective-permute-start | bytes 1376264 | tf_op jit(solution)/shard_map/ppermute | solution.py:615
  51.0 2.1 %collective-permute-start.5 = (f32[1,64,256]{2,1,0:T(8,128)S(1)}, f32[1,64,256]{2,1,0:T(8,128)S(1)}, u32[]{:S(2)}, u32[]{:S(2)}) collective-permute-start(f32[1,64,256]{2,1,0:T(8,128)S(1)} %get-tuple-element.46), channel_id=1, source_target_pairs={{0,1},{1,0},{2,3},{3,2},{4,5},{5,4},{6,7},{7,6},{8,9},{9,8},{10,11... | collective-permute-start | bytes 196616 | tf_op jit(solution)/shard_map/ppermute | solution.py:615

commit v8 on v7

--- a/solution.py
+++ b/solution.py
@@ -291,7 +291,7 @@
             cosine = cosine_ref[pl.ds(first_row + row, SUB), :]
             inverse_square = 1.0 / (cosine * cosine)
 
-            unroll = strip_count if following is not None else 16
+            unroll = strip_count if following is not None else strip_count // 2
 
             def add_strips(chunk, sums):
                 for index in range(unroll):
@@ -492,13 +492,13 @@
         edge_mine_ref, edge_core_ref = rest[:2]
         start, count = pieces * share * row_count, MOMENTS * EDGE_ROWS
         out_ref[start:start + count, :] = edge_mine_ref[0, :count] + edge_core_ref[0, :count]
-        out_ref[start + count:start + count + SUB, :] = edge_mine_ref[0, count:]
-        out_ref[start + count + SUB:, :] = edge_core_ref[0, count:]
+        out_ref[start + count:, :LANES] = edge_mine_ref[0, count:, :LANES]
+        out_ref[start + count:, LANES:] = edge_core_ref[0, count:, :LANES]
 
 
 def combine(mine, near, edges, order):
     moments, row_count, width = mine.shape
-    rows = moments * row_count + sum(edge.shape[1] + SUB for edge in edges[:1])
+    rows = moments * row_count + sum(edge.shape[1] for edge in edges[:1])
     vmem = pl.BlockSpec(memory_space=pltpu.VMEM)
     return pl.pallas_call(
         functools.partial(combine_kernel, pieces=len(near), edges=bool(edges)),
@@ -523,16 +523,21 @@
     at_row, at_col = at_row.astype(F32), at_col.astype(F32)
     near_start = compact_start - edge_start
     compacts = [ref[0, near_start:near_start + SUB, :LANES] for ref in (edge_mine_ref, edge_core_ref)]
-    compacts += [far_refs[-1][compact_start + SUB * part:compact_start + SUB * (part + 1), :LANES] for part in range(2)]
+    compacts += [far_refs[-1][compact_start:, part * LANES:(part + 1) * LANES] for part in range(2)]
     rows_in, cols_in = [], []
     for compact in compacts:
         row_low, row_high, col_low, col_high, quality = (compact[kind:kind + 1, :] for kind in range(5))
         rows_in.append(jnp.where((at_row >= row_low) & (at_row < row_high), quality, 0.0))
         cols_in.append(jnp.where((at_col >= col_low) & (at_col < col_high), 1.0, 0.0))
-    available = lax.dot_general(
-        jnp.concatenate(rows_in, axis=1), jnp.concatenate(cols_in, axis=1), (((1,), (1,)), ((), ())),
-        precision=lax.Precision.HIGHEST, preferred_element_type=F32,
-    )
+    rest = jnp.concatenate(rows_in, axis=1)
+    cols_in = jnp.concatenate(cols_in, axis=1).astype(jnp.bfloat16)
+    available = jnp.zeros((row_block, width), F32)
+    for _ in range(3):
+        part = rest.astype(jnp.bfloat16)
+        rest = rest - part.astype(F32)
+        available += lax.dot_general(
+            part, cols_in, (((1,), (1,)), ((), ())), preferred_element_type=F32
+        )
     available_ref[...] = available
     sub = lax.broadcasted_iota(jnp.int32, (SUB, LANES), 0)
     piece_rows = row_block // len(pieces)

time: 55.6 us -> 55 us (0.989)
  transfers between devices with their start and end apart: 9 -> 9, of which waited for: 3 -> 3; matrix products, arithmetic and copies ran while one was open for 0% -> 0% of each run, Pallas kernels for 70% -> 71%
where the time goes in v8:
time: 55 us; the launch traced here: 54.8 us
  Pallas kernels  42.6 us (77%)
  starting transfers between devices  7.89 us (14%)
  waiting for transfers between devices  3.64 us (7%)
  between operations  0.73 us (1%)
    pallas_call x2, Pallas kernels, moments_of(): pl.pallas_call(functools.partial(moment_kernel, remote=remote, first_row=...  36.1 us
    ppermute x2, starting transfers between devices, local(): arrived.append(lax.ppermute(value, 'tile', swaps))  5 us
    ppermute x7, waiting for transfers between devices, exchange(): lax.ppermute(value, 'acq', [(source, source ^ distance) for source in ran...  3.64 us
    ppermute x7, starting transfers between devices, exchange(): lax.ppermute(value, 'acq', [(source, source ^ distance) for source in ran...  2.89 us
    pallas_call x2, Pallas kernels, edge_moments(): pl.pallas_call(functools.partial(edge_kernel, remote=remote), out_shape=(...  2.68 us
    pallas_call x1, Pallas kernels, halo_rows(): pl.pallas_call(halo_kernel, out_shape=(pair, pair, inner, cosine, weights...  2.16 us
    pallas_call x1, Pallas kernels, finish(): pl.pallas_call(functools.partial(finish_kernel, pieces), out_shape=(jax.S...  1.47 us
  transfers between devices with their start and end apart: 9, of which 3 were waited for; matrix products, arithmetic and copies ran while one was open for 0% of the time, Pallas kernels for 71%

profile of v8, /device:TPU:12, one launch (start us, length us, event | category | flops | bytes accessed | tf_op | source)
XLA Modules:
  0.0 54.8 jit_solution(12575507610231680649)
XLA Ops:
  0.6 0.0 copy-start
  0.6 0.0 copy-start.1
  0.6 2.2 %halo_rows.1 = (f32[2,48,1024]{2,1,0:T(8,128)S(1)}, f32[2,48,1024]{2,1,0:T(8,128)S(1)}, f32[4,48,1024]{2,1,0:T(8,128)S(1)}, f32[64,128]{1,0:T(8,128)S(1)}, bf16[...) custom-call(f32[48,64,1024]{2,1,0:T(8,128)} %refs_4_.3), custom_call_target="tpu_custom_call" | custom-call | flops 1 | bytes 1 | tf_op jit(solution)/shard_map/halo_rows/pallas_call | solution.py:111
  2.8 0.6 %collective-permute-start = (f32[2,48,1024]{2,1,0:T(8,128)S(1)}, f32[2,48,1024]{2,1,0:T(8,128)S(1)}, u32[]{:S(2)}, u32[]{:S(2)}) collective-permute-start(f32[2,48,1024]{2,1,0:T(8,128)S(1)} %get-tuple-element.32.first_out), channel_id=1, source_target_pairs={{0,4},{8,12},{16,20},{24,28},{4,0},{12,8},{20,16},{28,24},{1,5},{9... | collective-permute-start | bytes 1179656 | tf_op jit(solution)/shard_map/ppermute | solution.py:633
  3.4 4.4 %collective-permute-start.1 = (f32[2,48,1024]{2,1,0:T(8,128)S(1)}, f32[2,48,1024]{2,1,0:T(8,128)S(1)}, u32[]{:S(2)}, u32[]{:S(2)}) collective-permute-start(f32[2,48,1024]{2,1,0:T(8,128)S(1)} %get-tuple-element.33.second_out), channel_id=1, source_target_pairs={{4,8},{12,16},{20,24},{8,4},{16,12},{24,20},{5,9},{13,17},{21,25},... | collective-permute-start | bytes 1179656 | tf_op jit(solution)/shard_map/ppermute | solution.py:633
  7.8 0.0 copy-done
  7.8 0.0 copy-done.1
  7.8 18.2 %moments_remote.1 = (f32[14,64,256]{2,1,0:T(8,128)S(1)}, f32[7,64,256]{2,1,0:T(8,128)S(1)}, f32[7,64,256]{2,1,0:T(8,128)S(1)}, f32[8,128]{1,0:T(8,128)S(1)}, f32...) custom-call(f32[48]{0:T(128)S(1)} %copy-done.1, s32[4,48]{1,0:T(4,128)S(1)} %bitcast.1, ...), custom_call_target="tpu_custom_call" | custom-call | flops 1 | bytes 1 | tf_op jit(solution)/shard_map/moments_remote/pallas_call | solution.py:374
  26.1 0.1 collective-permute-start.2
  26.2 0.5 collective-permute-start.3
  26.7 0.0 collective-permute-done.first_in
  26.7 0.0 collective-permute-done.1.second_in
  26.7 1.3 %edges_remote.1 = (f32[1,64,256]{2,1,0:T(8,128)S(1)}, f32[1,64,256]{2,1,0:T(8,128)S(1)}, f32[8,128]{1,0:T(8,128)S(1)}) custom-call(f32[5,48,128]{2,1,0:T(8,128)S(1)} %get-tuple-element.29.limits_ref.refs_0_, f32[8,256]{1,0:T(8,128)S(1)} %get-tuple-element.31.compact_ref, f32[64,128]{1,0:T(8,128)S(1)} %get-tuple-element.26.refs_2_.cosine_ref, ...), custom_call_target="tpu_custom_call" | custom-call | flops 1 | bytes 1 | tf_op jit(solution)/shard_map/edges_remote/pallas_call | solution.py:471
  28.0 0.1 collective-permute-start.4
  28.2 1.2 %collective-permute-done.4.refs_3_ = f32[1,64,256]{2,1,0:T(8,128)S(1)} collective-permute-done((f32[1,64,256]{2,1,0:T(8,128)S(1)}, f32[1,64,256]{2,1,0:T(8,128)S(1)}, u32[]{:S(2)}, u32[]{:S(2)}) %collective-permute-start.4) | collective-permute-done | bytes 65568 | tf_op jit(solution)/shard_map/ppermute | solution.py:620
  29.3 0.0 collective-permute-done.2.refs_0_
  29.3 0.0 collective-permute-done.3.refs_1_
  29.3 0.1 combine.1
  29.5 1.5 %collective-permute-start.6 = (f32[960,256]{1,0:T(8,128)S(1)}, f32[960,256]{1,0:T(8,128)S(1)}, u32[]{:S(2)}, u32[]{:S(2)}) collective-permute-start(f32[960,256]{1,0:T(8,128)S(1)} %get-tuple-element.47), channel_id=1, source_target_pairs={{0,2},{1,3},{2,0},{3,1},{4,6},{5,7},{6,4},{7,5},{8,10},{9,11},{10,... | collective-permute-start | bytes 2949128 | tf_op jit(solution)/shard_map/ppermute | solution.py:620
  31.0 1.3 %edges_own.1 = (f32[1,64,256]{2,1,0:T(8,128)S(1)}, f32[1,64,256]{2,1,0:T(8,128)S(1)}, f32[8,128]{1,0:T(8,128)S(1)}) custom-call(f32[5,48,128]{2,1,0:T(8,128)S(1)} %get-tuple-element.29.limits_ref.refs_0_, f32[8,256]{1,0:T(8,128)S(1)} %get-tuple-element.31.compact_ref, f32[64,128]{1,0:T(8,128)S(1)} %get-tuple-element.26.refs_2_.cosine_ref, ...), custom_call_target="tpu_custom_call" | custom-call | flops 1 | bytes 1 | tf_op jit(solution)/shard_map/edges_own/pallas_call | solution.py:471
  32.3 17.9 %moments_own.1 = (f32[14,64,256]{2,1,0:T(8,128)S(1)}, f32[7,64,256]{2,1,0:T(8,128)S(1)}, f32[7,64,256]{2,1,0:T(8,128)S(1)}, f32[8,128]{1,0:T(8,128)}) custom-call(f32[5,48,128]{2,1,0:T(8,128)S(1)} %get-tuple-element.29.limits_ref.refs_0_, f32[48,64,128]{2,1,0:T(8,128)S(1)} %get-tuple-element.30.refs_1_, f32[64,128]{1,0:T(8,128)S(1)} %get-tuple-element.26.refs_2_.cosine_ref, ...), custom_call_target="tpu_custom_call" | custom-call | flops 1 | bytes 1 | tf_op jit(solution)/shard_map/moments_own/pallas_call | solution.py:374
  50.2 0.1 collective-permute-start.7
  50.3 0.5 collective-permute-start.8
  50.8 0.1 collective-permute-start.5
  50.9 2.0 %collective-permute-done.5.edge_core_ref = f32[1,64,256]{2,1,0:T(8,128)S(1)} collective-permute-done((f32[1,64,256]{2,1,0:T(8,128)S(1)}, f32[1,64,256]{2,1,0:T(8,128)S(1)}, u32[]{:S(2)}, u32[]{:S(2)}) %collective-permute-start.5) | collective-permute-done | bytes 65568 | tf_op jit(solution)/shard_map/ppermute | solution.py:620
  52.9 0.0 collective-permute-done.7.refs_1_
  52.9 0.0 collective-permute-done.8.refs_2_
  52.9 0.5 collective-permute-done.6.refs_0_
  53.4 1.5 %finish.1 = (f32[64,256]{1,0:T(8,128)}, f32[10,64,256]{2,1,0:T(8,128)}) custom-call(f32[64,128]{1,0:T(8,128)S(1)} %get-tuple-element.26.refs_2_.cosine_ref, f32[14,64,256]{2,1,0:T(8,128)S(1)} %get-tuple-element.44.mine_ref, f32[1,64,256]{2,1,0:T(8,128)S(1)} %get-tuple-element.45.edge_mine_ref, f32[1,64,256]{2,1,0:T(8,128)S(1)} %collective-permute-done.5.edge_core_ref, ...), custom_call_target="tpu_custom_call" | custom-call | flops 1 | bytes 1 | tf_op jit(solution)/shard_map/finish/pallas_call | solution.py:598
Async XLA Ops:
  0.6 7.2 %copy-start = (s32[48,4]{0,1:T(4,128)S(1)}, s32[48,4]{0,1:T(4,128)}, u32[]{:S(2)}) copy-start(s32[48,4]{0,1:T(4,128)} %param.5) | copy-start | bytes 2308
  0.6 7.2 %copy-start.1 = (f32[48]{0:T(128)S(1)}, f32[48]{0:T(128)}, u32[]{:S(2)}) copy-start(f32[48]{0:T(128)} %refs_0_.1) | copy-start | bytes 580
  2.8 23.8 %collective-permute-start = (f32[2,48,1024]{2,1,0:T(8,128)S(1)}, f32[2,48,1024]{2,1,0:T(8,128)S(1)}, u32[]{:S(2)}, u32[]{:S(2)}) collective-permute-start(f32[2,48,1024]{2,1,0:T(8,128)S(1)} %get-tuple-element.32.first_out), channel_id=1, source_target_pairs={{0,4},{8,12},{16,20},{24,28},{4,0},{12,8},{20,16},{28,24},{1,5},{9... | collective-permute-start | bytes 1179656 | tf_op jit(solution)/shard_map/ppermute | solution.py:633
  3.4 23.3 %collective-permute-start.1 = (f32[2,48,1024]{2,1,0:T(8,128)S(1)}, f32[2,48,1024]{2,1,0:T(8,128)S(1)}, u32[]{:S(2)}, u32[]{:S(2)}) collective-permute-start(f32[2,48,1024]{2,1,0:T(8,128)S(1)} %get-tuple-element.33.second_out), channel_id=1, source_target_pairs={{4,8},{12,16},{20,24},{8,4},{16,12},{24,20},{5,9},{13,17},{21,25},... | collective-permute-start | bytes 1179656 | tf_op jit(solution)/shard_map/ppermute | solution.py:633
  26.1 3.3 %collective-permute-start.2 = (f32[7,64,256]{2,1,0:T(8,128)S(1)}, f32[7,64,256]{2,1,0:T(8,128)S(1)}, u32[]{:S(2)}, u32[]{:S(2)}) collective-permute-start(f32[7,64,256]{2,1,0:T(8,128)S(1)} %get-tuple-element.36), channel_id=1, source_target_pairs={{0,1},{1,0},{2,3},{3,2},{4,5},{5,4},{6,7},{7,6},{8,9},{9,8},{10,11... | collective-permute-start | bytes 1376264 | tf_op jit(solution)/shard_map/ppermute | solution.py:620
  26.2 3.2 %collective-permute-start.3 = (f32[7,64,256]{2,1,0:T(8,128)S(1)}, f32[7,64,256]{2,1,0:T(8,128)S(1)}, u32[]{:S(2)}, u32[]{:S(2)}) collective-permute-start(f32[7,64,256]{2,1,0:T(8,128)S(1)} %get-tuple-element.37), channel_id=1, source_target_pairs={{0,1},{1,0},{2,3},{3,2},{4,5},{5,4},{6,7},{7,6},{8,9},{9,8},{10,11... | collective-permute-start | bytes 1376264 | tf_op jit(solution)/shard_map/ppermute | solution.py:620
  28.0 1.3 %collective-permute-start.4 = (f32[1,64,256]{2,1,0:T(8,128)S(1)}, f32[1,64,256]{2,1,0:T(8,128)S(1)}, u32[]{:S(2)}, u32[]{:S(2)}) collective-permute-start(f32[1,64,256]{2,1,0:T(8,128)S(1)} %get-tuple-element.40), channel_id=1, source_target_pairs={{0,1},{1,0},{2,3},{3,2},{4,5},{5,4},{6,7},{7,6},{8,9},{9,8},{10,11... | collective-permute-start | bytes 196616 | tf_op jit(solution)/shard_map/ppermute | solution.py:620
  29.5 23.9 %collective-permute-start.6 = (f32[960,256]{1,0:T(8,128)S(1)}, f32[960,256]{1,0:T(8,128)S(1)}, u32[]{:S(2)}, u32[]{:S(2)}) collective-permute-start(f32[960,256]{1,0:T(8,128)S(1)} %get-tuple-element.47), channel_id=1, source_target_pairs={{0,2},{1,3},{2,0},{3,1},{4,6},{5,7},{6,4},{7,5},{8,10},{9,11},{10,... | collective-permute-start | bytes 2949128 | tf_op jit(solution)/shard_map/ppermute | solution.py:620
  50.2 2.6 %collective-permute-start.7 = (f32[7,64,256]{2,1,0:T(8,128)S(1)}, f32[7,64,256]{2,1,0:T(8,128)S(1)}, u32[]{:S(2)}, u32[]{:S(2)}) collective-permute-start(f32[7,64,256]{2,1,0:T(8,128)S(1)} %get-tuple-element.48), channel_id=1, source_target_pairs={{0,1},{1,0},{2,3},{3,2},{4,5},{5,4},{6,7},{7,6},{8,9},{9,8},{10,11... | collective-permute-start | bytes 1376264 | tf_op jit(solution)/shard_map/ppermute | solution.py:620
  50.3 2.6 %collective-permute-start.8 = (f32[7,64,256]{2,1,0:T(8,128)S(1)}, f32[7,64,256]{2,1,0:T(8,128)S(1)}, u32[]{:S(2)}, u32[]{:S(2)}) collective-permute-start(f32[7,64,256]{2,1,0:T(8,128)S(1)} %get-tuple-element.49), channel_id=1, source_target_pairs={{0,1},{1,0},{2,3},{3,2},{4,5},{5,4},{6,7},{7,6},{8,9},{9,8},{10,11... | collective-permute-start | bytes 1376264 | tf_op jit(solution)/shard_map/ppermute | solution.py:620
  50.8 2.1 %collective-permute-start.5 = (f32[1,64,256]{2,1,0:T(8,128)S(1)}, f32[1,64,256]{2,1,0:T(8,128)S(1)}, u32[]{:S(2)}, u32[]{:S(2)}) collective-permute-start(f32[1,64,256]{2,1,0:T(8,128)S(1)} %get-tuple-element.46), channel_id=1, source_target_pairs={{0,1},{1,0},{2,3},{3,2},{4,5},{5,4},{6,7},{7,6},{8,9},{9,8},{10,11... | collective-permute-start | bytes 196616 | tf_op jit(solution)/shard_map/ppermute | solution.py:620
